TPU v7x, 32 devices: a whole 2x2x4 slice. The times are simulated.
32 devices in a mesh: dp: 16 (over z, y, x), fsdp: 2 (over core).
Axes of the slice: x: 2, y: 2, z: 4, core: 2. Of those that a mesh axis runs over, the one named last changes fastest.
Arguments:
- tokens_in: bfloat16 [32, 576, 768], P(('dp', 'fsdp')), may hold values from -6 to 6
- cotangent: bfloat16 [32, 576, 768], P(('dp', 'fsdp')), may hold values from -6 to 6
- segments: int32 [32, 576], P(('dp', 'fsdp')), may hold values from 0 to 3, as said below
- tile_sides: int32 [32, 576], P(('dp', 'fsdp')), may hold values from 1 to 15, as said below
- valid_slots: int32 [32, 576], P(('dp', 'fsdp')), may hold values from 0 to 1, as said below
- owners: int32 [32], replicated, may hold values from 0 to 31, as said below
- master_qkv: float32 [768, 2304], P(('dp', 'fsdp')), may hold values from -0.21875 to 0.21875
- master_out: float32 [768, 768], P(('dp', 'fsdp')), may hold values from -0.625 to 0.625
- master_up: float32 [768, 3072], P(('dp', 'fsdp')), may hold values from -0.21875 to 0.21875
- master_down: float32 [3072, 768], P(('dp', 'fsdp')), may hold values from -0.109375 to 0.109375
- master_vec: float32 [7680], P(('dp', 'fsdp'))
- first_qkv: float32 [768, 2304], P(('dp', 'fsdp')), may hold values from -56 to 56
- first_out: float32 [768, 768], P(('dp', 'fsdp')), may hold values from -40 to 40
- first_up: float32 [768, 3072], P(('dp', 'fsdp')), may hold values from -28 to 28
- first_down: float32 [3072, 768], P(('dp', 'fsdp')), may hold values from -64 to 64
- first_vec: float32 [7680], P(('dp', 'fsdp')), may hold values from -48 to 48
- second_qkv: float32 [768, 2304], P(('dp', 'fsdp')), may hold values from 7.3728 to 29.4912
- second_out: float32 [768, 768], P(('dp', 'fsdp')), may hold values from 3.6864 to 14.7456
- second_up: float32 [768, 3072], P(('dp', 'fsdp')), may hold values from 1.8432 to 7.3728
- second_down: float32 [3072, 768], P(('dp', 'fsdp')), may hold values from 11.9808 to 47.9232
- second_vec: float32 [7680], P(('dp', 'fsdp')), may hold values from 4.608 to 18.432
Outputs:
- block_out: bfloat16 [32, 576, 768], P(('dp', 'fsdp'))
- tokens_grad: float32 [32, 576, 768], P(('dp', 'fsdp'))
- first_qkv_new: float32 [768, 2304], P(('dp', 'fsdp'))
- second_qkv_new: float32 [768, 2304], P(('dp', 'fsdp'))
- master_qkv_new: float32 [768, 2304], P(('dp', 'fsdp'))
- first_out_new: float32 [768, 768], P(('dp', 'fsdp'))
- second_out_new: float32 [768, 768], P(('dp', 'fsdp'))
- master_out_new: float32 [768, 768], P(('dp', 'fsdp'))
- first_up_new: float32 [768, 3072], P(('dp', 'fsdp'))
- second_up_new: float32 [768, 3072], P(('dp', 'fsdp'))
- master_up_new: float32 [768, 3072], P(('dp', 'fsdp'))
- first_down_new: float32 [3072, 768], P(('dp', 'fsdp'))
- second_down_new: float32 [3072, 768], P(('dp', 'fsdp'))
- master_down_new: float32 [3072, 768], P(('dp', 'fsdp'))
- first_vec_new: float32 [7680], P(('dp', 'fsdp'))
- second_vec_new: float32 [7680], P(('dp', 'fsdp'))
- master_vec_new: float32 [7680], P(('dp', 'fsdp'))
Inputs may be any that keep to these rules, and one draw needn't show every extreme that they name: In each row, segments never fall from slot to slot and count tiles from 0; a row holds four small tiles, two large tiles then padding, or a large tile, two small tiles then padding; padding slots form the row's last segment. `tile_sides`: every slot of a tile carries that tile's side (12 or 15); padding slots carry 1. `valid_slots`: padding slots are 0 and stand at the end of a row. `owners`: A permutation of 0 .. 31.
All inputs are finite; a program needn't handle non-finite values.
Results may differ from a plain program's by a relative error of at most 0.011.
Values may be sent and summed in bfloat16 or wider, within the bound.
No kernel may reach another device: no remote copies, remote signals or barrier semaphores. Data moves between devices by JAX's collectives and lax.ppermute only.
A program may use at most 192 MiB of HBM per device.

v0:
```python
import functools

import jax
import jax.numpy as jnp
from jax import lax
from jax.experimental import pallas as pl
from jax.experimental.pallas import tpu as pltpu
from jax.sharding import PartitionSpec as P

D = 768
HEADS = 12
FF = 3072
STEP = 10
HALF = 384
WIN = 256
SMALL = 160
LARGE = 240
LOG2E = 1.4426950408889634
CUT_ONE = 1152
WIDTH_ONE = 1280
WIDTH_TWO = 1920
WIDTH_THREE = 384

EPSILON = 1e-05
BETA_ONE = 0.9
BETA_TWO = 0.999
ADAM_EPS = 1e-08
RATE_MATRIX = 0.05
DECAY_MATRIX = 0.05
RATE_VECTOR = 0.3

AXES = ("dp", "fsdp")
LOW = jnp.bfloat16
WIDE = jnp.float32
VMEM_BYTES = 12 * 2**20


def nn(left, right):
    return lax.dot_general(left, right, (((1,), (0,)), ((), ())), preferred_element_type=WIDE)


def nt(left, right):
    return lax.dot_general(left, right, (((1,), (1,)), ((), ())), preferred_element_type=WIDE)


def tn(left, right):
    return lax.dot_general(left, right, (((0,), (0,)), ((), ())), preferred_element_type=WIDE)


def shape(rows, cols, kind=LOW):
    return jax.ShapeDtypeStruct((rows, cols), kind)


def later(kernel, inputs, extra):
    return lambda *refs: kernel(*refs[:inputs], *refs[inputs + extra :])


def whole_call(kernel, outs, scratch, smem, name, flops, *args, anywhere=(), after=()):
    specs = []
    for i in range(len(args)):
        space = pltpu.SMEM if i < smem else pl.ANY if i in anywhere else pltpu.VMEM
        specs.append(pl.BlockSpec(memory_space=space))
    moved = sum(a.size * a.dtype.itemsize for a in args) + sum(o.size * o.dtype.itemsize for o in outs)
    return pl.pallas_call(
        later(kernel, len(args), len(after)),
        in_specs=specs + [pl.BlockSpec(memory_space=pl.ANY)] * len(after),
        out_specs=[pl.BlockSpec(memory_space=pltpu.VMEM)] * len(outs),
        out_shape=outs,
        scratch_shapes=scratch,
        compiler_params=pltpu.CompilerParams(vmem_limit_bytes=VMEM_BYTES),
        cost_estimate=pl.CostEstimate(flops=flops, bytes_accessed=moved, transcendentals=0),
        name=name,
    )(*args, *after)


def over_rows(count, step, body, init=None):
    return lax.fori_loop(0, count // step, lambda i, c: body(pl.ds(pl.multiple_of(i * step, step), step), c), init)


def normal(values):
    centre = values - jnp.mean(values, axis=-1, keepdims=True)
    rstd = lax.rsqrt(jnp.mean(centre * centre, axis=-1, keepdims=True) + EPSILON)
    return centre * rstd, rstd


def both(pair, side, lo, width):
    rows = slice(HALF * side, HALF * (side + 1))
    return jnp.concatenate([z[rows, lo : lo + width] for z in pair], axis=0)


def qkv_kernel(x_ref, order_ref, own, other, a_ref, qkv_ref, vec_ref, tmp, wide):
    moved = jnp.concatenate([z[:HALF, CUT_ONE:] for z in (own, other)], axis=0)
    wide[...] = nn(order_ref[...], moved)
    vec_ref[...] = jnp.zeros_like(vec_ref)
    for k in range(10):
        first = min(D * k // 10 // 8 * 8, D - 88)

        def tenths(rows):
            entry = lax.broadcasted_iota(jnp.int32, (rows, D), 1) + D * k
            tenth = (entry * 52429) >> 19
            return tenth, entry - 10 * tenth, lax.broadcasted_iota(jnp.int32, (rows, D), 0)

        _, column, row = tenths(128)
        picked = nn(wide[first : first + 88, :].astype(LOW), (row == column).astype(LOW))
        tenth, _, row = tenths(88)
        vec_ref[k : k + 1, :] = jnp.sum(jnp.where(row + first == tenth, picked, 0.0), axis=0, keepdims=True)
    gain, shift = vec_ref[0:1, :], vec_ref[1:2, :]

    def norm(rows, _):
        tmp[rows, :] = (normal(x_ref[rows, :].astype(WIDE))[0] * gain + shift).astype(LOW)

    over_rows(x_ref.shape[0], 144, norm)
    a_ref[...] = nn(tmp[...], order_ref[...]).astype(LOW)
    for col in range(0, 3 * D, 384):
        w = both((own, other), *divmod(col, CUT_ONE), 384)
        qkv_ref[:, col : col + 384] = nn(a_ref[...], w).astype(LOW)


def project(x, order, one, after=()):
    n = x.shape[0]
    return whole_call(
        qkv_kernel, [shape(n, D), shape(n, 3 * D), shape(16, D, WIDE)],
        [pltpu.VMEM((n, D), LOW), pltpu.VMEM((D, 128), WIDE)], 0, "project",
        2 * n * D * (4 * D), x, order, *one, after=after,
    )


def each_tile(spans, body):
    def step(t, carry):
        for kind, rows in ((1, SMALL), (2, LARGE)):

            @pl.when(spans[t, 4] == kind)
            def _():
                body(t, pl.multiple_of(spans[t, 2], 16), rows, pl.multiple_of(spans[t, 3], 16))

        return carry

    lax.fori_loop(0, 4, step, 0)


def padding_rows(spans, shape_):
    return lax.broadcasted_iota(jnp.int32, shape_, 0) >= spans[4, 0]


def own_half(values, e):
    lane = lax.broadcasted_iota(jnp.int32, values.shape, 1)
    return jnp.where((lane < 64) if e == 0 else (lane >= 64), values, jnp.zeros_like(values))


def attend_kernel(base, spans, slopes, qkv_ref, far_ref, o_ref, p_ref, acc):
    acc[...] = jnp.zeros_like(acc)

    def tile(t, at, count, key):
        rows, keys = pl.ds(at, count), pl.ds(key, WIN)
        row = lax.broadcasted_iota(jnp.int32, (count, 1), 0) + at
        inside = ((row >= spans[t, 0]) & (row < spans[t, 1])).astype(WIDE)
        far = far_ref[t, :count, :]
        for pair in range(3):
            col = (base + pair) * 128
            q, k, v = [qkv_ref[z, col + i * D : col + i * D + 128] for i, z in enumerate((rows, keys, keys))]
            out = None
            for e in range(2):
                s = nt(q, own_half(k, e)) * (0.125 * LOG2E) - slopes[2 * (base + pair) + e] * far
                p = jnp.exp2(s - jnp.max(s, axis=1, keepdims=True))
                p = (p * (inside / jnp.sum(p, axis=1, keepdims=True))).astype(LOW)
                p_ref[t, 2 * pair + e, :count, :] = p
                part = nn(p, own_half(v, e))
                out = part if out is None else out + part
            acc[rows, pair * 128 : pair * 128 + 128] += out

    each_tile(spans, tile)
    v = qkv_ref[:, base * 128 + 2 * D : base * 128 + 2 * D + HALF]
    o_ref[...] = jnp.where(padding_rows(spans, v.shape), v, acc[...].astype(LOW))


def attend(base, qkv, far, spans, slopes, after=()):
    n = qkv.shape[0]
    return whole_call(
        functools.partial(attend_kernel, base),
        [shape(n, HALF), jax.ShapeDtypeStruct((4, HEADS // 2, LARGE, WIN), LOW)],
        [pltpu.VMEM((n, HALF), WIDE)], 2, "attend", 9 * 10**9, spans, slopes, qkv, far, after=after,
    )


def attend_back_kernel(base, spans, qkv_ref, g_ref, p_ref, dq_ref, dk_ref, dv_ref, aq, ak, av):
    for acc in (aq, ak, av):
        acc[...] = jnp.zeros_like(acc)

    def tile(t, at, count, key):
        rows, keys = pl.ds(at, count), pl.ds(key, WIN)
        for pair in range(3):
            col = (base + pair) * 128
            q, k, v = [qkv_ref[z, col + i * D : col + i * D + 128] for i, z in enumerate((rows, keys, keys))]
            g = g_ref[rows, col : col + 128]
            sums = None
            for e in range(2):
                ge = own_half(g, e)
                p = p_ref[t, 2 * pair + e, :count, :]
                wide = p.astype(WIDE)
                d = wide * nt(ge * 0.125, v)
                d = (d - wide * jnp.sum(d, axis=1, keepdims=True)).astype(LOW)
                parts = (nn(d, own_half(k, e)), tn(d, own_half(q, e)), tn(p, ge))
                sums = parts if sums is None else tuple(a + b for a, b in zip(sums, parts))
            part = slice(pair * 128, pair * 128 + 128)
            aq[rows, part] += sums[0]
            ak[keys, part] += sums[1]
            av[keys, part] += sums[2]

    each_tile(spans, tile)
    dq_ref[...] = aq[...].astype(LOW)
    dk_ref[...] = ak[...].astype(LOW)
    g = g_ref[:, base * 128 : base * 128 + HALF]
    dv_ref[...] = jnp.where(padding_rows(spans, g.shape), g, av[...].astype(LOW))


def attend_back(base, qkv, grad, probs, spans, after=()):
    n = qkv.shape[0]
    return whole_call(
        functools.partial(attend_back_kernel, base), [shape(n, HALF)] * 3, [pltpu.VMEM((n, HALF), WIDE)] * 3, 1,
        "attend_back", 12 * 10**9, spans, qkv, grad, probs, after=after,
    )


def tables_kernel(seg_ref, side_ref, valid_ref, spans, far_ref):
    n = seg_ref.shape[1]
    seg, side, valid = [z[...].astype(WIDE) for z in (seg_ref, side_ref, valid_ref)]
    live = jnp.sum(valid).astype(jnp.int32)
    for z in range(5):
        spans[4, z] = live
    for t in range(4):
        low = jnp.sum((seg < t).astype(WIDE)).astype(jnp.int32)
        high = jnp.sum((seg <= t).astype(WIDE)).astype(jnp.int32)
        width = jnp.max(jnp.where(seg == t, side, 1.0))
        small = high - low <= SMALL - 16
        start = low // 16 * 16
        at = jnp.minimum(start, jnp.where(small, n - SMALL, n - LARGE))
        key = jnp.minimum(start, n - WIN)
        kind = jnp.where((high > low) & (low < live), jnp.where(small, 1, 2), 0)
        for z, value in enumerate((low, high, at, key, kind)):
            spans[t, z] = value

        def places(first, shape_, dim):
            slot = lax.broadcasted_iota(jnp.int32, shape_, dim) + first
            place = (slot - low).astype(WIDE)
            row = jnp.floor((place + 0.5) / width)
            return (slot >= low) & (slot < high), row, place - row * width

        inside, row, col = places(at, (LARGE, 1), 0)
        inside_key, row_key, col_key = places(key, (1, WIN), 1)
        down, along = row - row_key, col - col_key
        far_ref[t] = jnp.where(inside & inside_key, jnp.sqrt(down * down + along * along), 1e12)


def tables(seg, side, valid):
    vmem, smem = [pl.BlockSpec(memory_space=z) for z in (pltpu.VMEM, pltpu.SMEM)]
    return pl.pallas_call(
        tables_kernel,
        in_specs=[vmem] * 3,
        out_specs=[smem, vmem],
        out_shape=[jax.ShapeDtypeStruct((5, 5), jnp.int32), jax.ShapeDtypeStruct((4, LARGE, WIN), WIDE)],
        compiler_params=pltpu.CompilerParams(vmem_limit_bytes=VMEM_BYTES),
        name="tables",
    )(seg, side, valid)


def bell(u):
    share = 0.5 + 0.5 * lax.erf(u * 0.7071067811865476)
    return u * share, share + u * (jnp.exp2(u * u * -0.7213475204444817) * 0.3989422804014327)


def up_kernel(x_ref, o0_ref, o1_ref, vec_ref, order_ref, own, other, mixed_ref, h_ref, a_ref, gl_ref, gp_ref, tmp):
    mixed_ref[...] = (
        nn(o0_ref[...], order_ref[:HALF, :]) + nn(o1_ref[...], order_ref[HALF:, :])
    ).astype(LOW)
    for col in (0, 384):
        part = slice(col, col + 384)
        h_ref[:, part] = x_ref[:, part].astype(WIDE) + nn(mixed_ref[...], both((own, other), 0, col, 384)) + vec_ref[2:3, part]
    gain, shift = vec_ref[3:4, :], vec_ref[4:5, :]

    def norm(rows, _):
        tmp[rows, :] = (normal(h_ref[rows, :])[0] * gain + shift).astype(LOW)

    over_rows(x_ref.shape[0], 144, norm)
    a_ref[...] = nn(tmp[...], order_ref[...]).astype(LOW)
    for col in range(0, FF, 384):
        k = 5 + col // D
        u = nn(a_ref[...], both((own, other), *divmod(col + D, WIDTH_TWO), 384)) + vec_ref[k : k + 1, col % D : col % D + 384]
        value, slope = bell(u)
        gl_ref[:, col : col + 384] = value.astype(LOW)
        gp_ref[:, col : col + 384] = slope.astype(LOW)


def upward(x, o, vec, order, two, after=()):
    n = x.shape[0]
    return whole_call(
        up_kernel, [shape(n, D), shape(n, D, WIDE), shape(n, D), shape(n, FF), shape(n, FF)],
        [pltpu.VMEM((n, D), LOW)], 0, "upward", 2 * n * D * (7 * D) * 2, x, *o, vec, order, *two,
        after=after,
    )


def down_kernel(place, vec_ref, gl_ref, gp_ref, dy_ref, h_ref, own, other, out_ref, dur_ref, vg_ref, wd, sem):
    def copies(b, piece, row):
        dst = pl.ds(pl.multiple_of(b * 96, 96), 96)
        return [
            pltpu.make_async_copy(
                piece.at[pl.ds(pl.multiple_of(row * 96 + side * (FF // 2), 96), 96), :],
                wd.at[dst, pl.ds(side * WIDTH_THREE, WIDTH_THREE)],
                sem,
            )
            for side in (0, 1)
        ]

    def begin(b, carry):
        p = place[b]
        pl.when(p < 16)(lambda: [z.start() for z in copies(b, own, p)] and None)
        pl.when(p >= 16)(lambda: [z.start() for z in copies(b, other, p - 16)] and None)
        return carry

    def finish(b, carry):
        for z in copies(b, own, 0):
            z.wait()
        return carry

    lax.fori_loop(0, 32, begin, 0)
    lax.fori_loop(0, 32, finish, 0)
    for col in range(0, FF, 384):
        part = slice(col, col + 384)
        du = nt(dy_ref[...], wd[part, :]) * gp_ref[:, part].astype(WIDE)
        dur_ref[:, part] = du.astype(LOW)
        k = col // D
        vg_ref[k : k + 1, col % D : col % D + 384] = jnp.sum(du, axis=0, keepdims=True)
    for col in (0, 384):
        part = slice(col, col + 384)
        out_ref[:, part] = (h_ref[:, part] + nn(gl_ref[...], wd[:, part]) + vec_ref[9:10, part]).astype(LOW)


def downward(place, vec, gl, gp, dy, h, three, after=()):
    n = h.shape[0]
    return whole_call(
        down_kernel, [shape(n, D), shape(n, FF), shape(8, D, WIDE)],
        [pltpu.VMEM((FF, D), LOW), pltpu.SemaphoreType.DMA], 1, "downward",
        2 * n * D * (8 * D), place, vec, gl, gp, dy, h, *three, anywhere=(6, 7), after=after,
    )


def hidden_kernel(vec_ref, order_ref, dur_ref, dy_ref, h_ref, own, other, dh_ref, dhr_ref, dor_ref, vg_ref, tmp):
    split = WIDTH_TWO - D
    for i, w in enumerate((own, other)):
        tmp[:, HALF * i : HALF * (i + 1)] = (
            nt(dur_ref[:, :split], w[:HALF, D:]) + nt(dur_ref[:, split:], w[HALF:, :])
        ).astype(LOW)
    dh_ref[...] = nt(tmp[...], order_ref[...])
    gain = vec_ref[3:4, :]

    def step(rows, sums):
        e = dh_ref[rows, :]
        dy = dy_ref[rows, :].astype(WIDE)
        n, rstd = normal(h_ref[rows, :])
        w = e * gain
        dh = dy + rstd * (w - jnp.mean(w, axis=-1, keepdims=True) - n * jnp.mean(w * n, axis=-1, keepdims=True))
        dh_ref[rows, :] = dh
        dhr_ref[rows, :] = dh.astype(LOW)
        return tuple(s + jnp.sum(z.reshape(-1, 8, D), axis=0) for s, z in zip(sums, (dh, e * n, e, dy)))

    zero = jnp.zeros((8, D), WIDE)
    sums = over_rows(h_ref.shape[0], 144, step, (zero,) * 4)
    for k, s in enumerate(sums):
        vg_ref[k : k + 1, :] = jnp.sum(s, axis=0, keepdims=True)
    for i, w in enumerate((own, other)):
        tmp[:, HALF * i : HALF * (i + 1)] = nt(dhr_ref[...], w[:HALF, :D]).astype(LOW)
    dor_ref[...] = nt(tmp[...], order_ref[...]).astype(LOW)


def hidden_grad(vec, order, dur, dy, h, two, after=()):
    n = h.shape[0]
    return whole_call(
        hidden_kernel, [shape(n, D, WIDE), shape(n, D), shape(n, D), shape(8, D, WIDE)],
        [pltpu.VMEM((n, D), LOW)], 0, "hidden_grad",
        2 * n * D * (7 * D), vec, order, dur, dy, h, *two, after=after,
    )


def down_grad_kernel(place, gl_ref, dy_ref, own, other):
    for c in range(8):
        t = tn(gl_ref[:, 384 * c : 384 * (c + 1)], dy_ref[...]).astype(LOW)
        for i in range(4):
            p = place[4 * c + i]

            def put(piece, row):
                for side in (0, 1):
                    rows = pl.ds(pl.multiple_of(row * 96 + side * (FF // 2), 96), 96)
                    piece[rows, :] = t[96 * i : 96 * (i + 1), side * WIDTH_THREE : (side + 1) * WIDTH_THREE]

            pl.when(p < 16)(lambda: put(own, p))
            pl.when(p >= 16)(lambda: put(other, p - 16))


def down_grad(place, gl, dy, after=()):
    n = dy.shape[0]
    return whole_call(down_grad_kernel, [shape(FF, WIDTH_THREE)] * 2, [], 1, "down_grad", 2 * n * D * FF, place, gl, dy, after=after)


def two_grad_kernel(mixed_ref, a_ref, dhr_ref, dur_ref, own, other):
    for col in range(0, D + FF, 384):
        left, right = (mixed_ref, dhr_ref[:, col : col + 384]) if col < D else (a_ref, dur_ref[:, col - D : col - D + 384])
        t = tn(left[...], right).astype(LOW)
        side, lo = divmod(col, WIDTH_TWO)
        own[HALF * side : HALF * (side + 1), lo : lo + 384] = t[:HALF]
        other[HALF * side : HALF * (side + 1), lo : lo + 384] = t[HALF:]


def two_grad(mixed, a, dhr, dur, after=()):
    n = a.shape[0]
    return whole_call(two_grad_kernel, [shape(D, WIDTH_TWO)] * 2, [], 0, "two_grad", 2 * n * D * (D + FF), mixed, a, dhr, dur,
                      after=after)


def one_grad_kernel(a_ref, *refs):
    halves, (own, other) = refs[:6], refs[6:]
    for i, half in enumerate(halves):
        t = tn(a_ref[...], half[...]).astype(LOW)
        side, lo = divmod(384 * i, CUT_ONE)
        own[HALF * side : HALF * (side + 1), lo : lo + 384] = t[:HALF]
        other[HALF * side : HALF * (side + 1), lo : lo + 384] = t[HALF:]


def one_grad(a, d, after=()):
    n = a.shape[0]
    return whole_call(one_grad_kernel, [shape(D, CUT_ONE)] * 2, [], 0, "one_grad", 2 * n * D * 3 * D, a, *d, after=after)


def input_back_kernel(order_ref, q0, q1, k0, k1, v0, v1, own, other, e_ref, tmp):
    for i, w in enumerate((own, other)):
        total = 0.0
        for j, d in enumerate((q0, q1, k0, k1, v0, v1)):
            side, lo = divmod(384 * j, CUT_ONE)
            total = total + nt(d[...], w[HALF * side : HALF * (side + 1), lo : lo + 384])
        tmp[:, HALF * i : HALF * (i + 1)] = total.astype(LOW)
    e_ref[...] = nt(tmp[...], order_ref[...])


def input_back(order, d, one, after=()):
    n = d[0].shape[0]
    return whole_call(
        input_back_kernel, [shape(n, D, WIDE)], [pltpu.VMEM((n, D), LOW)], 0, "input_back",
        2 * n * D * 4 * D, order, *d, *one, after=after,
    )[0]


def input_kernel(x_ref, vec_ref, e_ref, dh_ref, dx_ref, vg_ref):
    gain = vec_ref[0:1, :]

    def step(rows, sums):
        e = e_ref[rows, :]
        n, rstd = normal(x_ref[rows, :].astype(WIDE))
        w = e * gain
        dx_ref[rows, :] = dh_ref[rows, :] + rstd * (
            w - jnp.mean(w, axis=-1, keepdims=True) - n * jnp.mean(w * n, axis=-1, keepdims=True)
        )
        return tuple(s + jnp.sum(z.reshape(-1, 8, D), axis=0) for s, z in zip(sums, (e * n, e)))

    zero = jnp.zeros((8, D), WIDE)
    sums = over_rows(x_ref.shape[0], 144, step, (zero,) * 2)
    for k, s in enumerate(sums):
        vg_ref[k : k + 1, :] = jnp.sum(s, axis=0, keepdims=True)


def input_grad(x, vec, e, dh, after=()):
    n = x.shape[0]
    return whole_call(
        input_kernel, [shape(n, D, WIDE), shape(8, D, WIDE)], [], 0, "input_grad",
        2 * n * D * 3 * D, x, vec, e, dh, after=after,
    )


def near_kernel(a, b, c, d, left_ref, right_ref):
    cut = left_ref.shape[1]
    for out, lo in ((left_ref, 0), (right_ref, cut)):
        out[...] = jnp.concatenate([z[:, lo : lo + cut].astype(WIDE) for z in (a, b, c, d)], axis=0).astype(LOW)


def near_pieces(pieces, after=()):
    rows, cols = pieces[0].shape
    return whole_call(near_kernel, [shape(4 * rows, cols // 2)] * 2, [], 0, "near", 1, *pieces, after=after)


def first_kernel(left, got_left, right, got_right, left_ref, right_ref):
    rows = left.shape[0]
    for out, mine, got in ((left_ref, left, got_left), (right_ref, right, got_right)):
        out[:rows, :] = mine[...]
        out[rows:, :] = got[...]


def first_pieces(left, right, got, after=()):
    rows, cols = left.shape
    return whole_call(
        first_kernel, [shape(2 * rows, cols)] * 2, [], 0, "first", 1, left, got[0], right, got[1], after=after
    )


def second_kernel(left, got, right, far, own_ref):
    rows = left.shape[0]
    half = rows // 2
    own_ref[:rows, :] = left[...]
    own_ref[rows : 2 * rows, :] = got[...]
    for i in (0, 1):
        own_ref[2 * rows + 2 * i * half : 2 * rows + (2 * i + 1) * half, :] = right[i * half : (i + 1) * half, :]
        own_ref[2 * rows + (2 * i + 1) * half : 2 * rows + (2 * i + 2) * half, :] = far[i * half : (i + 1) * half, :]


def second_pieces(left, right, got, after=()):
    rows, cols = left.shape
    return whole_call(
        second_kernel, [shape(4 * rows, cols)], [], 0, "second", 1, left, got[0], right, got[1], after=after
    )[0]


def core_sum_kernel(own, got, left_keep, right_keep, left_out, right_out):
    half = left_keep.shape[0]
    rows = half // 2

    def total(lo, count):
        return own[lo : lo + count, :].astype(WIDE) + got[lo : lo + count, :].astype(WIDE)

    left_keep[...] = total(0, half)
    left_out[...] = total(half, half).astype(LOW)
    for i in (0, 1):
        lo = 2 * half + 2 * i * rows
        right_keep[i * rows : (i + 1) * rows, :] = total(lo, rows)
        right_out[i * rows : (i + 1) * rows, :] = total(lo + rows, rows).astype(LOW)


def core_sum(own, got, after=()):
    rows, cols = own.shape[0] // 4, own.shape[1]
    return whole_call(
        core_sum_kernel, [shape(rows, cols, WIDE)] * 2 + [shape(rows, cols)] * 2, [], 0, "core_sum", 1, own, got,
        after=after,
    )


def half_sum_kernel(left, got_left, right, got_right, left_keep, right_keep, left_out, right_out):
    rows = left_keep.shape[0]
    for mine, got, keep, out in ((left, got_left, left_keep, left_out), (right, got_right, right_keep, right_out)):
        keep[...] = mine[:rows, :] + got[:rows, :].astype(WIDE)
        out[...] = (mine[rows:, :] + got[rows:, :].astype(WIDE)).astype(LOW)


def half_sum(left, right, got, after=()):
    rows, cols = left.shape[0] // 2, left.shape[1]
    return whole_call(
        half_sum_kernel, [shape(rows, cols, WIDE)] * 2 + [shape(rows, cols)] * 2, [], 0, "half_sum", 1,
        left, got[0], right, got[1], after=after,
    )


def last_sum_kernel(left, got_left, right, got_right, keep, *outs):
    unit, cut = keep.shape[0], left.shape[1]
    for lo, mine, got in ((0, left, got_left), (cut, right, got_right)):
        total = mine[...] + got[...].astype(WIDE)
        keep[:, lo : lo + cut] = total[:unit]
        for i, out in enumerate(outs):
            out[:, lo : lo + cut] = total[unit * (i + 1) : unit * (i + 2)].astype(LOW)


def last_sum(left, right, got, after=()):
    unit, cols = left.shape[0] // 4, 2 * left.shape[1]
    return whole_call(
        last_sum_kernel, [shape(unit, cols, WIDE)] + [shape(unit, cols)] * 3, [], 0, "last_sum", 1,
        left, got[0], right, got[1], after=after,
    )


def swap(value, bits):
    pairs = [(i, i ^ bits) for i in range(32)]
    return lax.ppermute(value, AXES, pairs)


def tie(values, *first):
    return lax.optimization_barrier((tuple(values), first))[0]


class Flow:
    def __init__(self, steps):
        self.steps = steps
        self.next = next(steps)[:2]

    def issue(self, start=()):
        values, bits = self.next
        values = tie(values, start)
        self.got = tuple(swap(value, bit) for value, bit in zip(values, bits))
        return self.got

    def land(self, end=()):
        values, *bits = self.steps.send(tie(self.got, end))
        if values is None:
            return bits[0]
        self.next = (values, bits[0])
        return bits[1]


def spread(block):
    got = yield (block,) * 3, (8, 16, 24)
    left, right = near_pieces((block,) + got)
    got = yield (left, right), (2, 4), (left, right)
    left, right = first_pieces(left, right, got)
    got = yield (left, right), (4, 2), (left, right)
    own = second_pieces(left, right, got)
    got = yield (own,), (1,), (own,)
    yield None, (own, got[0])


def collect(pieces):
    (got,) = yield (pieces[1],), (1,)
    left, right, *out = ready = core_sum(pieces[0], got)
    got = yield out, (4, 2), tuple(ready)
    left, right, *out = ready = half_sum(left, right, got)
    got = yield out, (2, 4), tuple(ready)
    total, *out = ready = last_sum(left, right, got)
    got = yield out, (8, 16, 24), tuple(ready)
    yield None, (sum((z.astype(WIDE) for z in got), total),)


def collect_vec(blocks):
    half = blocks.shape[0] // 2
    (got,) = yield (blocks[half:],), (1,)
    blocks = blocks[:half] + got
    rows = half // 4
    got = yield [blocks[rows * k : rows * (k + 1)] for k in (1, 2, 3)], (2, 4, 6), (blocks,)
    blocks = sum(got, blocks[:rows])
    got = yield [blocks[k : k + 1] for k in (1, 2, 3)], (8, 16, 24), (blocks,)
    yield None, (sum(got, blocks[:1]).reshape(-1),)


def stack(whole):
    half, cut = whole.shape[0] // 2, whole.shape[1] // 2
    return tuple(jnp.concatenate([z[:, :cut], z[:, cut:]], axis=0) for z in (whole[:half], whole[half:]))


def unstack(pieces):
    half = pieces[0].shape[0] // 2
    return jnp.concatenate([jnp.concatenate([z[:half], z[half:]], axis=1) for z in pieces], axis=0)


class Whole:
    def __init__(self, result):
        self.result = result

    def issue(self, start=()):
        return ()

    def land(self, end=()):
        return self.result


def spread_any(block):
    return stack(lax.all_gather(block, AXES, axis=0, tiled=True))


def collect_any(pieces):
    return (lax.psum_scatter(unstack(pieces), AXES, scatter_dimension=0, tiled=True).astype(WIDE),)


def rearrange(whole, order, shards):
    return jnp.take(whole.reshape(shards, -1, whole.shape[1]), order, axis=0, mode="clip").reshape(whole.shape)


def adamw(master, moment_one, moment_two, gradient, step_rate, decay_rate):
    first_new = BETA_ONE * moment_one + (1.0 - BETA_ONE) * gradient
    second_new = BETA_TWO * moment_two + (1.0 - BETA_TWO) * gradient * gradient
    first_hat = first_new / (1.0 - BETA_ONE**STEP)
    second_hat = second_new / (1.0 - BETA_TWO**STEP)
    master_new = master - step_rate * (
        first_hat / (jnp.sqrt(second_hat) + ADAM_EPS) + decay_rate * master
    )
    return (first_new, second_new, master_new)


def local(
    tokens_in, cotangent, segments, tile_sides, valid_slots, owners,
    master_qkv, master_out, master_up, master_down, master_vec,
    first_qkv, first_out, first_up, first_down, first_vec,
    second_qkv, second_out, second_up, second_down, second_vec,
):
    shards = lax.axis_size(AXES)
    near = shards == 32
    unit = D // shards
    per_row = master_vec.shape[0] // unit
    share = master_vec.shape[0]
    ids = jnp.arange(shards, dtype=jnp.int32)
    if near:
        away = owners ^ lax.axis_index(AXES).astype(jnp.int32)
        place = (away >> 3) + 4 * ((away >> 1) & 1) + 8 * ((away >> 2) & 1) + 16 * (away & 1)
        place_down = place
    else:
        place = owners
        place_down = jnp.arange(32, dtype=jnp.int32)
    inverse = jnp.sum(ids[:, None] * (place[:, None] == ids[None, :]), axis=0)
    target = (place[:, None] * unit + jnp.arange(unit, dtype=jnp.int32)[None, :]).reshape(-1)
    order = (target[:, None] == jnp.arange(D, dtype=jnp.int32)[None, :]).astype(LOW)

    def gather(block):
        return Flow(spread(block)) if near else Whole(spread_any(block))

    def scatter(pieces):
        return Flow(collect(pieces)) if near else Whole(collect_any(pieces))

    vec_block = jnp.pad(master_vec.reshape(unit, per_row), ((0, 0), (0, 128 - per_row)))
    block_one = jnp.concatenate(
        [master_qkv[:, :CUT_ONE], vec_block, master_qkv[:, CUT_ONE:], jnp.zeros_like(vec_block)], axis=1
    )
    spans, far = tables(segments, tile_sides, valid_slots)
    slopes = LOG2E * jnp.exp2(-8.0 * (jnp.arange(HEADS, dtype=jnp.int32).astype(WIDE) + 1.0) / HEADS)
    one = gather(block_one.astype(LOW))
    two = gather(jnp.concatenate([master_out, master_up], axis=1).astype(LOW))
    if near:
        three = gather(master_down.astype(LOW))
    else:
        whole = lax.all_gather(master_down.astype(LOW), AXES, axis=0, tiled=True)
        three = Whole(stack(rearrange(whole, owners, shards)))
    one.issue()
    done = one.land((far, spans, slopes, order))
    one.issue(done)
    done = one.land()
    sent = one.issue(done) + two.issue(done)
    done = one.land()
    done = done + two.land(sent + done)
    one.issue(done)
    sent = two.issue(done)
    one = one.land()

    x = tokens_in[0]
    dy = cotangent[0]
    act_one, qkv, vec = project(x, order, one)
    done = two.land((qkv,))
    sent = two.issue(done) + three.issue(done)
    mixed_0, probs_0 = attend(0, qkv, far, spans, slopes, done)
    done = two.land((mixed_0,))
    done = done + three.land((mixed_0,) + sent + done)
    sent = two.issue(done) + three.issue(done)
    mixed_1, probs_1 = attend(3, qkv, far, spans, slopes, done + (mixed_0,))
    done = three.land((mixed_1,) + sent)
    two = two.land((mixed_1,) + sent)
    three.issue(done + two[1:])
    mixed, hidden, act_two, gelu, gelu_slope = upward(x, (mixed_0, mixed_1), vec, order, two, done)
    grad_three = down_grad(place_down, gelu, dy)
    done = three.land(tuple(grad_three))
    three.issue(done)
    three = three.land()
    if not near:
        back = jnp.sum(ids[:, None] * (owners[:, None] == ids[None, :]), axis=0)
        grad_three = stack(rearrange(unstack(grad_three), back, shards))
    flow_three = scatter(grad_three)
    flow_three.issue((three[1],))
    block_out, dur, sums_up = downward(place_down, vec, gelu, gelu_slope, dy, hidden, three)
    done = flow_three.land((dur,))
    flow_three.issue(done)
    dh, dh_low, dmixed, sums = hidden_grad(vec, order, dur, dy, hidden, two, done)
    grad_two = two_grad(mixed, act_two, dh_low, dur)
    done = flow_three.land(tuple(grad_two)) + tuple(grad_two)
    flow_two = scatter(grad_two)
    sent = flow_three.issue(done) + flow_two.issue(done)
    d0 = attend_back(0, qkv, dmixed, probs_0, spans, done)
    done = flow_three.land(tuple(d0) + sent) + flow_two.land(tuple(d0) + sent)
    sent = flow_three.issue(done) + flow_two.issue(done)
    d1 = attend_back(3, qkv, dmixed, probs_1, spans, done + tuple(d0))
    d = [z for pair in zip(d0, d1) for z in pair]
    grad_one = one_grad(act_one, d)
    dact = input_back(order, d, one, tuple(grad_one))
    done = (dact,) + tuple(grad_one) + sent
    sum_three, = flow_three.land(done)
    done = flow_two.land(done)
    flow_one = scatter(grad_one)
    sent = flow_one.issue(done) + flow_two.issue(done)
    tokens_grad, sums_one = input_grad(x, vec, dact, dh, done)
    vector_grad = jnp.concatenate([sums_one[:2], sums[:3], sums_up[:4], sums[3:4]], axis=0)
    blocks = jnp.take(vector_grad.reshape(shards, share), inverse, axis=0, mode="clip")
    if near:
        flow_vec = Flow(collect_vec(blocks))
    else:
        flow_vec = Whole((lax.psum_scatter(blocks.reshape(-1), AXES, scatter_dimension=0, tiled=True),))
    done = flow_one.land((blocks,) + sent) + flow_two.land((blocks,) + sent)
    sent = flow_one.issue(done) + flow_two.issue(done) + flow_vec.issue(done)
    upd_down = adamw(master_down, first_down, second_down, sum_three, RATE_MATRIX, DECAY_MATRIX)
    sent = sent + upd_down
    done = flow_one.land(sent) + flow_vec.land(sent)
    sum_two, = flow_two.land(sent)
    sent = flow_one.issue(done) + flow_vec.issue(done)
    done = flow_one.land(sent) + flow_vec.land(sent)
    sent = flow_one.issue(done) + flow_vec.issue(done)
    upd_out = adamw(master_out, first_out, second_out, sum_two[:, :D], RATE_MATRIX, DECAY_MATRIX)
    upd_up = adamw(master_up, first_up, second_up, sum_two[:, D:], RATE_MATRIX, DECAY_MATRIX)
    sum_one, = flow_one.land(sent + upd_out + upd_up)
    sum_vec, = flow_vec.land(sent + upd_out + upd_up)
    upd_qkv = adamw(master_qkv, first_qkv, second_qkv, sum_one, RATE_MATRIX, DECAY_MATRIX)
    upd_vec = adamw(master_vec, first_vec, second_vec, sum_vec, RATE_VECTOR, 0.0)
    return (
        (block_out[None], tokens_grad[None]) + upd_qkv + upd_out + upd_up + upd_down + upd_vec
    )


def solution(mesh):
    rows = P(AXES, None)
    flat = P(AXES)
    deep = P(AXES, None, None)
    stored = (rows,) * 4 + (flat,)
    in_specs = (deep,) * 2 + (rows,) * 3 + (P(),) + stored * 3
    out_specs = (deep,) * 2 + (rows,) * 12 + (flat,) * 3
    return jax.shard_map(local, mesh=mesh, in_specs=in_specs, out_specs=out_specs, check_vma=False)
```

profile of v0, /device:TPU:0, one launch (start us, length us, event | category | flops | bytes accessed | tf_op | source)
XLA Modules:
  0.0 239.9 jit_solution(13207521083114992747)
XLA Ops:
  2.5 3.1 %collective-permute-start = (bf16[24,2560]{1,0:T(8,128)(2,1)S(1)}, bf16[24,2560]{1,0:T(8,128)(2,1)S(1)}, u32[]{:S(2)}, u32[]{:S(2)}) collective-permute-start(bf16[24,2560]{1,0:T(8,128)(2,1)S(1)} %fusion.8.refs_0_), channel_id=1, source_target_pairs={{0,8},{1,9},{2,10},{3,11},{4,12},{5,13},{6,14},{7,15},{8,0},{9,1},... | collective-permute-start | bytes 368648 | tf_op jit(solution)/shard_map/ppermute | solution.py:576
  5.6 2.6 %collective-permute-start.1 = (bf16[24,2560]{1,0:T(8,128)(2,1)S(1)}, bf16[24,2560]{1,0:T(8,128)(2,1)S(1)}, u32[]{:S(2)}, u32[]{:S(2)}) collective-permute-start(bf16[24,2560]{1,0:T(8,128)(2,1)S(1)} %fusion.8.refs_0_), channel_id=1, source_target_pairs={{0,16},{1,17},{2,18},{3,19},{4,20},{5,21},{6,22},{7,23},{8,24},{9,... | collective-permute-start | bytes 368648 | tf_op jit(solution)/shard_map/ppermute | solution.py:576
  11.4 1.4 tables.1
  12.8 5.2 %collective-permute-done.1.refs_2_ = bf16[24,2560]{1,0:T(8,128)(2,1)S(1)} collective-permute-done((bf16[24,2560]{1,0:T(8,128)(2,1)S(1)}, bf16[24,2560]{1,0:T(8,128)(2,1)S(1)}, u32[]{:S(2)}, u32[]{:S(2)}) %collective-permute-start.1) | collective-permute-done | bytes 122912 | tf_op jit(solution)/shard_map/ppermute | solution.py:576
  18.0 1.6 collective-permute-start.3
  19.5 1.5 collective-permute-start.4
  21.1 3.1 %collective-permute-done.3.refs_1_ = bf16[96,1280]{1,0:T(8,128)(2,1)S(1)} collective-permute-done((bf16[96,1280]{1,0:T(8,128)(2,1)S(1)}, bf16[96,1280]{1,0:T(8,128)(2,1)S(1)}, u32[]{:S(2)}, u32[]{:S(2)}) %collective-permute-start.3) | collective-permute-done | bytes 245792 | tf_op jit(solution)/shard_map/ppermute | solution.py:576
  24.2 2.4 collective-permute-done.4.refs_3_
  26.7 1.6 collective-permute-start.5
  29.9 2.1 collective-permute-start.8
  32.0 1.6 collective-permute-start.9
  33.6 2.7 %collective-permute-done.5.refs_1_ = bf16[192,1280]{1,0:T(8,128)(2,1)S(1)} collective-permute-done((bf16[192,1280]{1,0:T(8,128)(2,1)S(1)}, bf16[192,1280]{1,0:T(8,128)(2,1)S(1)}, u32[]{:S(2)}, u32[]{:S(2)}) %collective-permute-start.5) | collective-permute-done | bytes 491552 | tf_op jit(solution)/shard_map/ppermute | solution.py:576
  37.2 6.5 %collective-permute-done.8.refs_2_ = bf16[24,3840]{1,0:T(8,128)(2,1)S(1)} collective-permute-done((bf16[24,3840]{1,0:T(8,128)(2,1)S(1)}, bf16[24,3840]{1,0:T(8,128)(2,1)S(1)}, u32[]{:S(2)}, u32[]{:S(2)}) %collective-permute-start.8) | collective-permute-done | bytes 184352 | tf_op jit(solution)/shard_map/ppermute | solution.py:576
  43.8 1.6 collective-permute-start.11
  45.9 1.9 collective-permute-done.10.refs_3_.refs_8_
  47.8 6.2 %project.1 = (bf16[576,768]{1,0:T(8,128)(2,1)S(1)}, bf16[576,2304]{1,0:T(8,128)(2,1)S(1)}, f32[16,768]{1,0:T(8,128)S(1)}) custom-call(bf16[576,768]{1,0:T(8,128)(2,1)S(1)} %bitcast.8, bf16[768,768]{1,0:T(8,128)(2,1)S(1)} %fusion.refs_1_.refs_4_.refs_0_, bf16[768,1280]{1,0:T(8,128)(2,1)S(1)} %second.3.refs_2_.refs_7_, ...), custom_call_target="tpu_custom_call" | custom-call | flops 2717908992 | bytes 9584640 | tf_op jit(solution)/shard_map/project/pallas_call | solution.py:64
  54.8 1.2 collective-permute-done.12.refs_3_
  56.2 2.6 %collective-permute-start.15 = (bf16[96,768]{1,0:T(8,128)(2,1)S(1)}, bf16[96,768]{1,0:T(8,128)(2,1)S(1)}, u32[]{:S(2)}, u32[]{:S(2)}) collective-permute-start(bf16[96,768]{1,0:T(8,128)(2,1)S(1)} %convert_element_type.47.refs_0_), channel_id=1, source_target_pairs={{0,8},{1,9},{2,10},{3,11},{4,12},{5,13},{6,14},{7,15},{8,0},{9,1},... | collective-permute-start | bytes 442376 | tf_op jit(solution)/shard_map/ppermute | solution.py:576
  58.8 1.8 collective-permute-start.16
  60.5 1.4 collective-permute-start.17
  63.0 4.6 %attend.2 = (bf16[576,384]{1,0:T(8,128)(2,1)S(1)}, bf16[4,6,240,256]{3,2,1,0:T(8,128)(2,1)S(1)}) custom-call(s32[5,5]{1,0:T(8,128)S(1)} %get-tuple-element.212.refs_0_, f32[12]{0:T(128)S(1)} %exponential_multiply_fusion.refs_1_, bf16[576,2304]{1,0:T(8,128)(2,1)S(1)} %get-tuple-element.238.refs_2_.refs_1_, f32[4,240,256]{2,1,0:T(8,128)S(1)} %get-tuple-element.211.refs_3_, ...), custom_call_target="tpu_custom_call" | custom-call | flops 8999999488 | bytes 7028884 | tf_op jit(solution)/shard_map/attend/pallas_call | solution.py:64
  67.6 1.6 copy-done.15
  69.2 9.9 %collective-permute-done.13.refs_1_ = bf16[192,1920]{1,0:T(8,128)(2,1)S(1)} collective-permute-done((bf16[192,1920]{1,0:T(8,128)(2,1)S(1)}, bf16[192,1920]{1,0:T(8,128)(2,1)S(1)}, u32[]{:S(2)}, u32[]{:S(2)}) %collective-permute-start.13) | collective-permute-done | bytes 737312 | tf_op jit(solution)/shard_map/ppermute | solution.py:576
  80.4 1.5 collective-permute-start.20
  81.9 4.6 %attend.3 = (bf16[576,384]{1,0:T(8,128)(2,1)S(1)}, bf16[4,6,240,256]{3,2,1,0:T(8,128)(2,1)S(1)}) custom-call(s32[5,5]{1,0:T(8,128)S(1)} %get-tuple-element.212.refs_0_, f32[12]{0:T(128)S(1)} %exponential_multiply_fusion.refs_1_, bf16[576,2304]{1,0:T(8,128)(2,1)S(1)} %get-tuple-element.238.refs_2_.refs_1_, f32[4,240,256]{2,1,0:T(8,128)S(1)} %get-tuple-element.211.refs_3_, ...), custom_call_target="tpu_custom_call" | custom-call | flops 8999999488 | bytes 7028884 | tf_op jit(solution)/shard_map/attend/pallas_call | solution.py:64
  86.5 1.7 copy-done.13
  89.6 1.6 collective-permute-start.21
  91.1 1.4 collective-permute-start.22
  92.6 8.4 %upward.1 = (bf16[576,768]{1,0:T(8,128)(2,1)S(1)}, f32[576,768]{1,0:T(8,128)S(1)}, bf16[576,768]{1,0:T(8,128)(2,1)S(1)}, bf16[576,3072]{1,0:T(8,128)(2,1)S(1)}, bf16[576,3072]{1,0:T(8,128)(2,1)S(1)}) custom-call(bf16[576,768]{1,0:T(8,128)(2,1)S(1)} %bitcast.9, bf16[576,384]{1,0:T(8,128)(2,1)S(1)} %get-tuple-element.245.refs_7_.refs_1_, ...), custom_call_target="tpu_custom_call" | custom-call | flops 9512681472 | bytes 19513344 | tf_op jit(solution)/shard_map/upward/pallas_call | solution.py:64
  101.0 7.8 %down_grad.1 = (bf16[3072,384]{1,0:T(8,128)(2,1)S(1)}, bf16[3072,384]{1,0:T(8,128)(2,1)S(1)}) custom-call(s32[32]{0:T(128)S(1)} %get-tuple-element.415.refs_0_, bf16[576,3072]{1,0:T(8,128)(2,1)S(1)} %get-tuple-element.267.refs_1_.refs_2_, bf16[576,768]{1,0:T(8,128)(2,1)S(1)} %bitcast.5), custom_call_target="tpu_custom_call" | custom-call | flops 2717908992 | bytes 9142400 | tf_op jit(solution)/shard_map/down_grad/pallas_call | solution.py:64
  109.1 4.5 %collective-permute-done.23.refs_7_ = bf16[3072,384]{1,0:T(8,128)(2,1)S(1)} collective-permute-done((bf16[3072,384]{1,0:T(8,128)(2,1)S(1)}, bf16[3072,384]{1,0:T(8,128)(2,1)S(1)}, u32[]{:S(2)}, u32[]{:S(2)}) %collective-permute-start.23) | collective-permute-done | bytes 2359328 | tf_op jit(solution)/shard_map/ppermute | solution.py:576
  113.7 10.8 %downward.1 = (bf16[576,768]{1,0:T(8,128)(2,1)}, bf16[576,3072]{1,0:T(8,128)(2,1)S(1)}, f32[8,768]{1,0:T(8,128)S(1)}) custom-call(s32[32]{0:T(128)S(1)} %get-tuple-element.415.refs_0_, f32[16,768]{1,0:T(8,128)S(1)} %get-tuple-element.237.refs_3_.refs_1_.refs_0_, bf16[576,3072]{1,0:T(8,128)(2,1)S(1)} %get-tuple-element.267.refs_1_.refs_2_, ...), custom_call_target="tpu_custom_call" | custom-call | flops 5435817984 | bytes 18948224 | tf_op jit(solution)/shard_map/downward/pallas_call | solution.py:64
  126.3 8.7 %hidden_grad.1 = (f32[576,768]{1,0:T(8,128)S(1)}, bf16[576,768]{1,0:T(8,128)(2,1)S(1)}, bf16[576,768]{1,0:T(8,128)(2,1)S(1)}, f32[8,768]{1,0:T(8,128)S(1)}) custom-call(f32[16,768]{1,0:T(8,128)S(1)} %get-tuple-element.237.refs_3_.refs_1_.refs_0_, bf16[768,768]{1,0:T(8,128)(2,1)S(1)} %fusion.refs_1_.refs_4_.refs_0_, ...), custom_call_target="tpu_custom_call" | custom-call | flops 4756340736 | bytes 16883712 | tf_op jit(solution)/shard_map/hidden_grad/pallas_call | solution.py:64
  135.0 5.8 %two_grad.1 = (bf16[768,1920]{1,0:T(8,128)(2,1)S(1)}, bf16[768,1920]{1,0:T(8,128)(2,1)S(1)}) custom-call(bf16[576,768]{1,0:T(8,128)(2,1)S(1)} %get-tuple-element.289.refs_0_, bf16[576,768]{1,0:T(8,128)(2,1)S(1)} %get-tuple-element.290.refs_1_, bf16[576,768]{1,0:T(8,128)(2,1)S(1)} %get-tuple-element.291.refs_2_, ...), custom_call_target="tpu_custom_call" | custom-call | flops 3397386240 | bytes 12091392 | tf_op jit(solution)/shard_map/two_grad/pallas_call | solution.py:64
  141.3 1.4 collective-permute-start.27
  142.7 1.5 collective-permute-start.28
  144.2 6.3 %attend_back.2 = (bf16[576,384]{1,0:T(8,128)(2,1)S(1)}, bf16[576,384]{1,0:T(8,128)(2,1)S(1)}, bf16[576,384]{1,0:T(8,128)(2,1)S(1)}) custom-call(s32[5,5]{1,0:T(8,128)S(1)} %get-tuple-element.212.refs_0_, bf16[576,2304]{1,0:T(8,128)(2,1)S(1)} %get-tuple-element.238.refs_2_.refs_1_, bf16[576,768]{1,0:T(8,128)(2,1)S(1)} %get-tuple-element.285.refs_2_, ...), custom_call_target="tpu_custom_call" | custom-call | flops 12000000000 | bytes 7815268 | tf_op jit(solution)/shard_map/attend_back/pallas_call | solution.py:64
  153.1 2.4 %collective-permute-start.33 = (bf16[96,768]{1,0:T(8,128)(2,1)S(1)}, bf16[96,768]{1,0:T(8,128)(2,1)S(1)}, u32[]{:S(2)}, u32[]{:S(2)}) collective-permute-start(bf16[96,768]{1,0:T(8,128)(2,1)S(1)} %get-tuple-element.328.refs_6_), channel_id=1, source_target_pairs={{0,16},{1,17},{2,18},{3,19},{4,20},{5,21},{6,22},{7,23},{8,24},{9,... | collective-permute-start | bytes 442376 | tf_op jit(solution)/shard_map/ppermute | solution.py:576
  155.6 1.4 collective-permute-start.34
  156.9 1.5 collective-permute-start.30
  159.2 6.5 %attend_back.3 = (bf16[576,384]{1,0:T(8,128)(2,1)S(1)}, bf16[576,384]{1,0:T(8,128)(2,1)S(1)}, bf16[576,384]{1,0:T(8,128)(2,1)S(1)}) custom-call(s32[5,5]{1,0:T(8,128)S(1)} %get-tuple-element.212.refs_0_, bf16[576,2304]{1,0:T(8,128)(2,1)S(1)} %get-tuple-element.238.refs_2_.refs_1_, bf16[576,768]{1,0:T(8,128)(2,1)S(1)} %get-tuple-element.285.refs_2_, ...), custom_call_target="tpu_custom_call" | custom-call | flops 12000000000 | bytes 7815268 | tf_op jit(solution)/shard_map/attend_back/pallas_call | solution.py:64
  165.7 3.6 %one_grad.1 = (bf16[768,1152]{1,0:T(8,128)(2,1)S(1)}, bf16[768,1152]{1,0:T(8,128)(2,1)S(1)}) custom-call(bf16[576,768]{1,0:T(8,128)(2,1)S(1)} %get-tuple-element.321.refs_0_, bf16[576,384]{1,0:T(8,128)(2,1)S(1)} %get-tuple-element.300.refs_12_.refs_1_, bf16[576,384]{1,0:T(8,128)(2,1)S(1)} %get-tuple-element.318.refs_2_, ...), custom_call_target="tpu_custom_call" | custom-call | flops 2038431744 | bytes 7077888 | tf_op jit(solution)/shard_map/one_grad/pallas_call | solution.py:64
  169.3 4.4 %input_back.1.refs_2_ = f32[576,768]{1,0:T(8,128)S(1)} custom-call(bf16[768,768]{1,0:T(8,128)(2,1)S(1)} %fusion.refs_1_.refs_4_.refs_0_, bf16[576,384]{1,0:T(8,128)(2,1)S(1)} %get-tuple-element.300.refs_12_.refs_1_, bf16[576,384]{1,0:T(8,128)(2,1)S(1)} %get-tuple-element.318.refs_2_, bf16[576,384]{1,0:T(8,128)(2,1)S(1)} %get-tuple-element.304.refs_13_.refs_3_, ...), custom_call_target="tpu_custom_call" | custom-call | flops 2717908992 | bytes 9535488 | tf_op jit(solution)/shard_map/input_back/pallas_call | solution.py:64
  177.1 1.4 collective-permute-start.37
  178.5 2.9 %input_grad.1 = (f32[576,768]{1,0:T(8,128)}, f32[8,768]{1,0:T(8,128)S(1)}) custom-call(bf16[576,768]{1,0:T(8,128)(2,1)S(1)} %bitcast.10, f32[16,768]{1,0:T(8,128)S(1)} %get-tuple-element.237.refs_3_.refs_1_.refs_0_, f32[576,768]{1,0:T(8,128)S(1)} %input_back.1.refs_2_, f32[576,768]{1,0:T(8,128)S(1)} %get-tuple-element.324.refs_3_, ...), custom_call_target="tpu_custom_call" | custom-call | flops 2038431744 | bytes 6266880 | tf_op jit(solution)/shard_map/input_grad/pallas_call | solution.py:64
  182.1 1.5 reshape.62
  183.6 2.0 gather_fusion
  185.7 2.0 collective-permute-done.36.refs_1_
  188.1 1.9 core_sum.5
  190.0 1.2 last_sum.4
  191.2 1.5 collective-permute-start.38
  192.7 1.3 collective-permute-start.39
  194.1 3.0 %collective-permute-start.41 = (bf16[24,3840]{1,0:T(8,128)(2,1)S(1)}, bf16[24,3840]{1,0:T(8,128)(2,1)S(1)}, u32[]{:S(2)}, u32[]{:S(2)}) collective-permute-start(bf16[24,3840]{1,0:T(8,128)(2,1)S(1)} %get-tuple-element.357), channel_id=1, source_target_pairs={{0,16},{1,17},{2,18},{3,19},{4,20},{5,21},{6,22},{7,23},{8,24},{9,... | collective-permute-start | bytes 552968 | tf_op jit(solution)/shard_map/ppermute | solution.py:576
  197.1 1.4 collective-permute-start.42
  198.6 1.1 multiply_subtract_fusion.1
  199.7 5.0 %collective-permute-done.40 = bf16[24,3840]{1,0:T(8,128)(2,1)S(1)} collective-permute-done((bf16[24,3840]{1,0:T(8,128)(2,1)S(1)}, bf16[24,3840]{1,0:T(8,128)(2,1)S(1)}, u32[]{:S(2)}, u32[]{:S(2)}) %collective-permute-start.40) | collective-permute-done | bytes 184352 | tf_op jit(solution)/shard_map/ppermute | solution.py:576
  204.7 5.8 %collective-permute-done.41 = bf16[24,3840]{1,0:T(8,128)(2,1)S(1)} collective-permute-done((bf16[24,3840]{1,0:T(8,128)(2,1)S(1)}, bf16[24,3840]{1,0:T(8,128)(2,1)S(1)}, u32[]{:S(2)}, u32[]{:S(2)}) %collective-permute-start.41) | collective-permute-done | bytes 184352 | tf_op jit(solution)/shard_map/ppermute | solution.py:576
  212.2 2.2 collective-permute-start.48
  216.8 3.5 %collective-permute-done.44.refs_1_ = bf16[96,1152]{1,0:T(8,128)(2,1)S(1)} collective-permute-done((bf16[96,1152]{1,0:T(8,128)(2,1)S(1)}, bf16[96,1152]{1,0:T(8,128)(2,1)S(1)}, u32[]{:S(2)}, u32[]{:S(2)}) %collective-permute-start.44) | collective-permute-done | bytes 221216 | tf_op jit(solution)/shard_map/ppermute | solution.py:576
  221.2 4.0 %collective-permute-start.52 = (f32[1,240]{1,0:T(1,128)S(1)}, f32[1,240]{1,0:T(1,128)S(1)}, u32[]{:S(2)}, u32[]{:S(2)}) collective-permute-start(f32[1,240]{1,0:T(1,128)S(1)} %get-tuple-element.387), channel_id=1, source_target_pairs={{0,8},{1,9},{2,10},{3,11},{4,12},{5,13},{6,14},{7,15},{8,0},{9,1},... | collective-permute-start | bytes 2888 | tf_op jit(solution)/shard_map/ppermute | solution.py:576
  227.0 1.7 collective-permute-start.54
  229.7 1.6 collective-permute-start.50
  231.3 1.7 collective-permute-start.51
  234.8 3.2 %collective-permute-done.50 = bf16[24,2304]{1,0:T(8,128)(2,1)S(1)} collective-permute-done((bf16[24,2304]{1,0:T(8,128)(2,1)S(1)}, bf16[24,2304]{1,0:T(8,128)(2,1)S(1)}, u32[]{:S(2)}, u32[]{:S(2)}) %collective-permute-start.50) | collective-permute-done | bytes 110624 | tf_op jit(solution)/shard_map/ppermute | solution.py:576
  (199 shorter events, 34.6 us)
Async XLA Ops:
  2.5 10.2 %collective-permute-start = (bf16[24,2560]{1,0:T(8,128)(2,1)S(1)}, bf16[24,2560]{1,0:T(8,128)(2,1)S(1)}, u32[]{:S(2)}, u32[]{:S(2)}) collective-permute-start(bf16[24,2560]{1,0:T(8,128)(2,1)S(1)} %fusion.8.refs_0_), channel_id=1, source_target_pairs={{0,8},{1,9},{2,10},{3,11},{4,12},{5,13},{6,14},{7,15},{8,0},{9,1},... | collective-permute-start | bytes 368648 | tf_op jit(solution)/shard_map/ppermute | solution.py:576
  5.6 12.3 %collective-permute-start.1 = (bf16[24,2560]{1,0:T(8,128)(2,1)S(1)}, bf16[24,2560]{1,0:T(8,128)(2,1)S(1)}, u32[]{:S(2)}, u32[]{:S(2)}) collective-permute-start(bf16[24,2560]{1,0:T(8,128)(2,1)S(1)} %fusion.8.refs_0_), channel_id=1, source_target_pairs={{0,16},{1,17},{2,18},{3,19},{4,20},{5,21},{6,22},{7,23},{8,24},{9,... | collective-permute-start | bytes 368648 | tf_op jit(solution)/shard_map/ppermute | solution.py:576
  8.2 9.7 %collective-permute-start.2 = (bf16[24,2560]{1,0:T(8,128)(2,1)S(1)}, bf16[24,2560]{1,0:T(8,128)(2,1)S(1)}, u32[]{:S(2)}, u32[]{:S(2)}) collective-permute-start(bf16[24,2560]{1,0:T(8,128)(2,1)S(1)} %fusion.8.refs_0_), channel_id=1, source_target_pairs={{0,24},{1,25},{2,26},{3,27},{4,28},{5,29},{6,30},{7,31},{8,16},{9,... | collective-permute-start | bytes 368648 | tf_op jit(solution)/shard_map/ppermute | solution.py:576
  18.0 6.3 %collective-permute-start.3 = (bf16[96,1280]{1,0:T(8,128)(2,1)S(1)}, bf16[96,1280]{1,0:T(8,128)(2,1)S(1)}, u32[]{:S(2)}, u32[]{:S(2)}) collective-permute-start(bf16[96,1280]{1,0:T(8,128)(2,1)S(1)} %get-tuple-element.218.refs_0_), channel_id=1, source_target_pairs={{0,2},{1,3},{2,0},{3,1},{4,6},{5,7},{6,4},{7,5},{8,10},{9,11},{10,... | collective-permute-start | bytes 737288 | tf_op jit(solution)/shard_map/ppermute | solution.py:576
  19.5 7.1 %collective-permute-start.4 = (bf16[96,1280]{1,0:T(8,128)(2,1)S(1)}, bf16[96,1280]{1,0:T(8,128)(2,1)S(1)}, u32[]{:S(2)}, u32[]{:S(2)}) collective-permute-start(bf16[96,1280]{1,0:T(8,128)(2,1)S(1)} %get-tuple-element.219.refs_2_), channel_id=1, source_target_pairs={{0,4},{1,5},{2,6},{3,7},{4,0},{5,1},{6,2},{7,3},{8,12},{9,13},{10,... | collective-permute-start | bytes 737288 | tf_op jit(solution)/shard_map/ppermute | solution.py:576
  26.7 9.6 %collective-permute-start.5 = (bf16[192,1280]{1,0:T(8,128)(2,1)S(1)}, bf16[192,1280]{1,0:T(8,128)(2,1)S(1)}, u32[]{:S(2)}, u32[]{:S(2)}) collective-permute-start(bf16[192,1280]{1,0:T(8,128)(2,1)S(1)} %get-tuple-element.224.refs_0_), channel_id=1, source_target_pairs={{0,4},{1,5},{2,6},{3,7},{4,0},{5,1},{6,2},{7,3},{8,12},{9,13},{10,... | collective-permute-start | bytes 1474568 | tf_op jit(solution)/shard_map/ppermute | solution.py:576
  28.3 8.8 %collective-permute-start.6 = (bf16[192,1280]{1,0:T(8,128)(2,1)S(1)}, bf16[192,1280]{1,0:T(8,128)(2,1)S(1)}, u32[]{:S(2)}, u32[]{:S(2)}) collective-permute-start(bf16[192,1280]{1,0:T(8,128)(2,1)S(1)} %get-tuple-element.225.refs_2_), channel_id=1, source_target_pairs={{0,2},{1,3},{2,0},{3,1},{4,6},{5,7},{6,4},{7,5},{8,10},{9,11},{10,... | collective-permute-start | bytes 1474568 | tf_op jit(solution)/shard_map/ppermute | solution.py:576
  29.1 8.1 %collective-permute-start.7 = (bf16[24,3840]{1,0:T(8,128)(2,1)S(1)}, bf16[24,3840]{1,0:T(8,128)(2,1)S(1)}, u32[]{:S(2)}, u32[]{:S(2)}) collective-permute-start(bf16[24,3840]{1,0:T(8,128)(2,1)S(1)} %pad_maximum_fusion.refs_0_), channel_id=1, source_target_pairs={{0,8},{1,9},{2,10},{3,11},{4,12},{5,13},{6,14},{7,15},{8,0},{9,1},... | collective-permute-start | bytes 552968 | tf_op jit(solution)/shard_map/ppermute | solution.py:576
  29.9 13.8 %collective-permute-start.8 = (bf16[24,3840]{1,0:T(8,128)(2,1)S(1)}, bf16[24,3840]{1,0:T(8,128)(2,1)S(1)}, u32[]{:S(2)}, u32[]{:S(2)}) collective-permute-start(bf16[24,3840]{1,0:T(8,128)(2,1)S(1)} %pad_maximum_fusion.refs_0_), channel_id=1, source_target_pairs={{0,16},{1,17},{2,18},{3,19},{4,20},{5,21},{6,22},{7,23},{8,24},{9,... | collective-permute-start | bytes 552968 | tf_op jit(solution)/shard_map/ppermute | solution.py:576
  32.0 11.7 %collective-permute-start.9 = (bf16[24,3840]{1,0:T(8,128)(2,1)S(1)}, bf16[24,3840]{1,0:T(8,128)(2,1)S(1)}, u32[]{:S(2)}, u32[]{:S(2)}) collective-permute-start(bf16[24,3840]{1,0:T(8,128)(2,1)S(1)} %pad_maximum_fusion.refs_0_), channel_id=1, source_target_pairs={{0,24},{1,25},{2,26},{3,27},{4,28},{5,29},{6,30},{7,31},{8,16},{9,... | collective-permute-start | bytes 552968 | tf_op jit(solution)/shard_map/ppermute | solution.py:576
  43.8 4.0 %collective-permute-start.10 = (bf16[768,1280]{1,0:T(8,128)(2,1)S(1)}, bf16[768,1280]{1,0:T(8,128)(2,1)S(1)}, u32[]{:S(2)}, u32[]{:S(2)}) collective-permute-start(bf16[768,1280]{1,0:T(8,128)(2,1)S(1)} %second.3.refs_2_.refs_7_), channel_id=1, source_target_pairs={{0,1},{1,0},{2,3},{3,2},{4,5},{5,4},{6,7},{7,6},{8,9},{9,8},{10,11... | collective-permute-start | bytes 5898248 | tf_op jit(solution)/shard_map/ppermute | solution.py:576
  43.8 11.0 %collective-permute-start.11 = (bf16[96,1920]{1,0:T(8,128)(2,1)S(1)}, bf16[96,1920]{1,0:T(8,128)(2,1)S(1)}, u32[]{:S(2)}, u32[]{:S(2)}) collective-permute-start(bf16[96,1920]{1,0:T(8,128)(2,1)S(1)} %get-tuple-element.239.refs_0_), channel_id=1, source_target_pairs={{0,2},{1,3},{2,0},{3,1},{4,6},{5,7},{6,4},{7,5},{8,10},{9,11},{10,... | collective-permute-start | bytes 1105928 | tf_op jit(solution)/shard_map/ppermute | solution.py:576
  45.4 10.7 %collective-permute-start.12 = (bf16[96,1920]{1,0:T(8,128)(2,1)S(1)}, bf16[96,1920]{1,0:T(8,128)(2,1)S(1)}, u32[]{:S(2)}, u32[]{:S(2)}) collective-permute-start(bf16[96,1920]{1,0:T(8,128)(2,1)S(1)} %get-tuple-element.240.refs_2_), channel_id=1, source_target_pairs={{0,4},{1,5},{2,6},{3,7},{4,0},{5,1},{6,2},{7,3},{8,12},{9,13},{10,... | collective-permute-start | bytes 1105928 | tf_op jit(solution)/shard_map/ppermute | solution.py:576
  56.2 23.4 %collective-permute-start.15 = (bf16[96,768]{1,0:T(8,128)(2,1)S(1)}, bf16[96,768]{1,0:T(8,128)(2,1)S(1)}, u32[]{:S(2)}, u32[]{:S(2)}) collective-permute-start(bf16[96,768]{1,0:T(8,128)(2,1)S(1)} %convert_element_type.47.refs_0_), channel_id=1, source_target_pairs={{0,8},{1,9},{2,10},{3,11},{4,12},{5,13},{6,14},{7,15},{8,0},{9,1},... | collective-permute-start | bytes 442376 | tf_op jit(solution)/shard_map/ppermute | solution.py:576
  58.8 20.8 %collective-permute-start.16 = (bf16[96,768]{1,0:T(8,128)(2,1)S(1)}, bf16[96,768]{1,0:T(8,128)(2,1)S(1)}, u32[]{:S(2)}, u32[]{:S(2)}) collective-permute-start(bf16[96,768]{1,0:T(8,128)(2,1)S(1)} %convert_element_type.47.refs_0_), channel_id=1, source_target_pairs={{0,16},{1,17},{2,18},{3,19},{4,20},{5,21},{6,22},{7,23},{8,24},{9,... | collective-permute-start | bytes 442376 | tf_op jit(solution)/shard_map/ppermute | solution.py:576
  60.5 19.0 %collective-permute-start.17 = (bf16[96,768]{1,0:T(8,128)(2,1)S(1)}, bf16[96,768]{1,0:T(8,128)(2,1)S(1)}, u32[]{:S(2)}, u32[]{:S(2)}) collective-permute-start(bf16[96,768]{1,0:T(8,128)(2,1)S(1)} %convert_element_type.47.refs_0_), channel_id=1, source_target_pairs={{0,24},{1,25},{2,26},{3,27},{4,28},{5,29},{6,30},{7,31},{8,16},{9,... | collective-permute-start | bytes 442376 | tf_op jit(solution)/shard_map/ppermute | solution.py:576
  61.9 17.2 %collective-permute-start.13 = (bf16[192,1920]{1,0:T(8,128)(2,1)S(1)}, bf16[192,1920]{1,0:T(8,128)(2,1)S(1)}, u32[]{:S(2)}, u32[]{:S(2)}) collective-permute-start(bf16[192,1920]{1,0:T(8,128)(2,1)S(1)} %get-tuple-element.246.refs_4_.refs_0_), channel_id=1, source_target_pairs={{0,4},{1,5},{2,6},{3,7},{4,0},{5,1},{6,2},{7,3},{8,12},{9,13},{10,... | collective-permute-start | bytes 2211848 | tf_op jit(solution)/shard_map/ppermute | solution.py:576
  62.4 16.9 %collective-permute-start.14 = (bf16[192,1920]{1,0:T(8,128)(2,1)S(1)}, bf16[192,1920]{1,0:T(8,128)(2,1)S(1)}, u32[]{:S(2)}, u32[]{:S(2)}) collective-permute-start(bf16[192,1920]{1,0:T(8,128)(2,1)S(1)} %get-tuple-element.247.refs_5_.refs_2_), channel_id=1, source_target_pairs={{0,2},{1,3},{2,0},{3,1},{4,6},{5,7},{6,4},{7,5},{8,10},{9,11},{10,... | collective-permute-start | bytes 2211848 | tf_op jit(solution)/shard_map/ppermute | solution.py:576
  79.6 9.8 %collective-permute-start.18 = (bf16[768,1920]{1,0:T(8,128)(2,1)S(1)}, bf16[768,1920]{1,0:T(8,128)(2,1)S(1)}, u32[]{:S(2)}, u32[]{:S(2)}) collective-permute-start(bf16[768,1920]{1,0:T(8,128)(2,1)S(1)} %second.4.refs_4_.refs_5_), channel_id=1, source_target_pairs={{0,1},{1,0},{2,3},{3,2},{4,5},{5,4},{6,7},{7,6},{8,9},{9,8},{10,11... | collective-permute-start | bytes 8847368 | tf_op jit(solution)/shard_map/ppermute | solution.py:576
  79.7 9.4 %collective-permute-start.19 = (bf16[384,384]{1,0:T(8,128)(2,1)S(1)}, bf16[384,384]{1,0:T(8,128)(2,1)S(1)}, u32[]{:S(2)}, u32[]{:S(2)}) collective-permute-start(bf16[384,384]{1,0:T(8,128)(2,1)S(1)} %get-tuple-element.260.refs_5_.refs_0_), channel_id=1, source_target_pairs={{0,2},{1,3},{2,0},{3,1},{4,6},{5,7},{6,4},{7,5},{8,10},{9,11},{10,... | collective-permute-start | bytes 884744 | tf_op jit(solution)/shard_map/ppermute | solution.py:576
  80.4 9.1 %collective-permute-start.20 = (bf16[384,384]{1,0:T(8,128)(2,1)S(1)}, bf16[384,384]{1,0:T(8,128)(2,1)S(1)}, u32[]{:S(2)}, u32[]{:S(2)}) collective-permute-start(bf16[384,384]{1,0:T(8,128)(2,1)S(1)} %get-tuple-element.261.refs_6_.refs_2_), channel_id=1, source_target_pairs={{0,4},{1,5},{2,6},{3,7},{4,0},{5,1},{6,2},{7,3},{8,12},{9,13},{10,... | collective-permute-start | bytes 884744 | tf_op jit(solution)/shard_map/ppermute | solution.py:576
  89.6 19.2 %collective-permute-start.21 = (bf16[768,384]{1,0:T(8,128)(2,1)S(1)}, bf16[768,384]{1,0:T(8,128)(2,1)S(1)}, u32[]{:S(2)}, u32[]{:S(2)}) collective-permute-start(bf16[768,384]{1,0:T(8,128)(2,1)S(1)} %get-tuple-element.270.refs_7_.refs_0_), channel_id=1, source_target_pairs={{0,4},{1,5},{2,6},{3,7},{4,0},{5,1},{6,2},{7,3},{8,12},{9,13},{10,... | collective-permute-start | bytes 1769480 | tf_op jit(solution)/shard_map/ppermute | solution.py:576
  91.1 17.6 %collective-permute-start.22 = (bf16[768,384]{1,0:T(8,128)(2,1)S(1)}, bf16[768,384]{1,0:T(8,128)(2,1)S(1)}, u32[]{:S(2)}, u32[]{:S(2)}) collective-permute-start(bf16[768,384]{1,0:T(8,128)(2,1)S(1)} %get-tuple-element.271.refs_8_.refs_2_), channel_id=1, source_target_pairs={{0,2},{1,3},{2,0},{3,1},{4,6},{5,7},{6,4},{7,5},{8,10},{9,11},{10,... | collective-permute-start | bytes 1769480 | tf_op jit(solution)/shard_map/ppermute | solution.py:576
  109.0 4.6 %collective-permute-start.23 = (bf16[3072,384]{1,0:T(8,128)(2,1)S(1)}, bf16[3072,384]{1,0:T(8,128)(2,1)S(1)}, u32[]{:S(2)}, u32[]{:S(2)}) collective-permute-start(bf16[3072,384]{1,0:T(8,128)(2,1)S(1)} %second.5.refs_6_), channel_id=1, source_target_pairs={{0,1},{1,0},{2,3},{3,2},{4,5},{5,4},{6,7},{7,6},{8,9},{9,8},{10,11... | collective-permute-start | bytes 7077896 | tf_op jit(solution)/shard_map/ppermute | solution.py:576
  113.6 11.0 %collective-permute-start.24 = (bf16[3072,384]{1,0:T(8,128)(2,1)S(1)}, bf16[3072,384]{1,0:T(8,128)(2,1)S(1)}, u32[]{:S(2)}, u32[]{:S(2)}) collective-permute-start(bf16[3072,384]{1,0:T(8,128)(2,1)S(1)} %get-tuple-element.279), channel_id=1, source_target_pairs={{0,1},{1,0},{2,3},{3,2},{4,5},{5,4},{6,7},{7,6},{8,9},{9,8},{10,11... | collective-permute-start | bytes 7077896 | tf_op jit(solution)/shard_map/ppermute | solution.py:576
  125.1 15.8 %collective-permute-start.25 = (bf16[768,384]{1,0:T(8,128)(2,1)S(1)}, bf16[768,384]{1,0:T(8,128)(2,1)S(1)}, u32[]{:S(2)}, u32[]{:S(2)}) collective-permute-start(bf16[768,384]{1,0:T(8,128)(2,1)S(1)} %get-tuple-element.287.refs_9_), channel_id=1, source_target_pairs={{0,4},{1,5},{2,6},{3,7},{4,0},{5,1},{6,2},{7,3},{8,12},{9,13},{10,... | collective-permute-start | bytes 1769480 | tf_op jit(solution)/shard_map/ppermute | solution.py:576
  125.7 15.3 %collective-permute-start.26 = (bf16[768,384]{1,0:T(8,128)(2,1)S(1)}, bf16[768,384]{1,0:T(8,128)(2,1)S(1)}, u32[]{:S(2)}, u32[]{:S(2)}) collective-permute-start(bf16[768,384]{1,0:T(8,128)(2,1)S(1)} %get-tuple-element.288.refs_10_), channel_id=1, source_target_pairs={{0,2},{1,3},{2,0},{3,1},{4,6},{5,7},{6,4},{7,5},{8,10},{9,11},{10,... | collective-permute-start | bytes 1769480 | tf_op jit(solution)/shard_map/ppermute | solution.py:576
  141.2 10.5 %collective-permute-start.29 = (bf16[768,1920]{1,0:T(8,128)(2,1)S(1)}, bf16[768,1920]{1,0:T(8,128)(2,1)S(1)}, u32[]{:S(2)}, u32[]{:S(2)}) collective-permute-start(bf16[768,1920]{1,0:T(8,128)(2,1)S(1)} %get-tuple-element.306.refs_9_), channel_id=1, source_target_pairs={{0,1},{1,0},{2,3},{3,2},{4,5},{5,4},{6,7},{7,6},{8,9},{9,8},{10,11... | collective-permute-start | bytes 8847368 | tf_op jit(solution)/shard_map/ppermute | solution.py:576
  141.3 9.4 %collective-permute-start.27 = (bf16[384,384]{1,0:T(8,128)(2,1)S(1)}, bf16[384,384]{1,0:T(8,128)(2,1)S(1)}, u32[]{:S(2)}, u32[]{:S(2)}) collective-permute-start(bf16[384,384]{1,0:T(8,128)(2,1)S(1)} %get-tuple-element.302.refs_6_), channel_id=1, source_target_pairs={{0,2},{1,3},{2,0},{3,1},{4,6},{5,7},{6,4},{7,5},{8,10},{9,11},{10,... | collective-permute-start | bytes 884744 | tf_op jit(solution)/shard_map/ppermute | solution.py:576
  142.7 9.1 %collective-permute-start.28 = (bf16[384,384]{1,0:T(8,128)(2,1)S(1)}, bf16[384,384]{1,0:T(8,128)(2,1)S(1)}, u32[]{:S(2)}, u32[]{:S(2)}) collective-permute-start(bf16[384,384]{1,0:T(8,128)(2,1)S(1)} %get-tuple-element.303.refs_7_), channel_id=1, source_target_pairs={{0,4},{1,5},{2,6},{3,7},{4,0},{5,1},{6,2},{7,3},{8,12},{9,13},{10,... | collective-permute-start | bytes 884744 | tf_op jit(solution)/shard_map/ppermute | solution.py:576
  152.5 21.2 %collective-permute-start.32 = (bf16[96,768]{1,0:T(8,128)(2,1)S(1)}, bf16[96,768]{1,0:T(8,128)(2,1)S(1)}, u32[]{:S(2)}, u32[]{:S(2)}) collective-permute-start(bf16[96,768]{1,0:T(8,128)(2,1)S(1)} %get-tuple-element.327.refs_5_), channel_id=1, source_target_pairs={{0,8},{1,9},{2,10},{3,11},{4,12},{5,13},{6,14},{7,15},{8,0},{9,1},... | collective-permute-start | bytes 442376 | tf_op jit(solution)/shard_map/ppermute | solution.py:576
  153.1 20.6 %collective-permute-start.33 = (bf16[96,768]{1,0:T(8,128)(2,1)S(1)}, bf16[96,768]{1,0:T(8,128)(2,1)S(1)}, u32[]{:S(2)}, u32[]{:S(2)}) collective-permute-start(bf16[96,768]{1,0:T(8,128)(2,1)S(1)} %get-tuple-element.328.refs_6_), channel_id=1, source_target_pairs={{0,16},{1,17},{2,18},{3,19},{4,20},{5,21},{6,22},{7,23},{8,24},{9,... | collective-permute-start | bytes 442376 | tf_op jit(solution)/shard_map/ppermute | solution.py:576
  155.6 18.1 %collective-permute-start.34 = (bf16[96,768]{1,0:T(8,128)(2,1)S(1)}, bf16[96,768]{1,0:T(8,128)(2,1)S(1)}, u32[]{:S(2)}, u32[]{:S(2)}) collective-permute-start(bf16[96,768]{1,0:T(8,128)(2,1)S(1)} %get-tuple-element.329.refs_7_), channel_id=1, source_target_pairs={{0,24},{1,25},{2,26},{3,27},{4,28},{5,29},{6,30},{7,31},{8,16},{9,... | collective-permute-start | bytes 442376 | tf_op jit(solution)/shard_map/ppermute | solution.py:576
  156.9 17.8 %collective-permute-start.30 = (bf16[192,1920]{1,0:T(8,128)(2,1)S(1)}, bf16[192,1920]{1,0:T(8,128)(2,1)S(1)}, u32[]{:S(2)}, u32[]{:S(2)}) collective-permute-start(bf16[192,1920]{1,0:T(8,128)(2,1)S(1)} %get-tuple-element.325.refs_10_), channel_id=1, source_target_pairs={{0,4},{1,5},{2,6},{3,7},{4,0},{5,1},{6,2},{7,3},{8,12},{9,13},{10,... | collective-permute-start | bytes 2211848 | tf_op jit(solution)/shard_map/ppermute | solution.py:576
  158.5 16.6 %collective-permute-start.31 = (bf16[192,1920]{1,0:T(8,128)(2,1)S(1)}, bf16[192,1920]{1,0:T(8,128)(2,1)S(1)}, u32[]{:S(2)}, u32[]{:S(2)}) collective-permute-start(bf16[192,1920]{1,0:T(8,128)(2,1)S(1)} %get-tuple-element.326.refs_11_), channel_id=1, source_target_pairs={{0,2},{1,3},{2,0},{3,1},{4,6},{5,7},{6,4},{7,5},{8,10},{9,11},{10,... | collective-permute-start | bytes 2211848 | tf_op jit(solution)/shard_map/ppermute | solution.py:576
  176.2 11.9 %collective-permute-start.35 = (bf16[768,1152]{1,0:T(8,128)(2,1)S(1)}, bf16[768,1152]{1,0:T(8,128)(2,1)}, u32[]{:S(2)}, u32[]{:S(2)}) collective-permute-start(bf16[768,1152]{1,0:T(8,128)(2,1)S(1)} %get-tuple-element.337.refs_10_), channel_id=1, source_target_pairs={{0,1},{1,0},{2,3},{3,2},{4,5},{5,4},{6,7},{7,6},{8,9},{9,8},{10,11... | collective-permute-start | bytes 5308424 | tf_op jit(solution)/shard_map/ppermute | solution.py:576
  176.3 11.4 %collective-permute-start.36 = (bf16[96,1920]{1,0:T(8,128)(2,1)}, bf16[96,1920]{1,0:T(8,128)(2,1)}, u32[]{:S(2)}, u32[]{:S(2)}) collective-permute-start(bf16[96,1920]{1,0:T(8,128)(2,1)} %get-tuple-element.341.refs_6_), channel_id=1, source_target_pairs={{0,2},{1,3},{2,0},{3,1},{4,6},{5,7},{6,4},{7,5},{8,10},{9,11},{10,... | collective-permute-start | bytes 1105928 | tf_op jit(solution)/shard_map/ppermute | solution.py:576
  177.1 11.0 %collective-permute-start.37 = (bf16[96,1920]{1,0:T(8,128)(2,1)}, bf16[96,1920]{1,0:T(8,128)(2,1)}, u32[]{:S(2)}, u32[]{:S(2)}) collective-permute-start(bf16[96,1920]{1,0:T(8,128)(2,1)} %get-tuple-element.342.refs_7_), channel_id=1, source_target_pairs={{0,4},{1,5},{2,6},{3,7},{4,0},{5,1},{6,2},{7,3},{8,12},{9,13},{10,... | collective-permute-start | bytes 1105928 | tf_op jit(solution)/shard_map/ppermute | solution.py:576
  191.2 19.3 %collective-permute-start.38 = (bf16[192,1152]{1,0:T(8,128)(2,1)S(1)}, bf16[192,1152]{1,0:T(8,128)(2,1)S(1)}, u32[]{:S(2)}, u32[]{:S(2)}) collective-permute-start(bf16[192,1152]{1,0:T(8,128)(2,1)S(1)} %get-tuple-element.354), channel_id=1, source_target_pairs={{0,4},{1,5},{2,6},{3,7},{4,0},{5,1},{6,2},{7,3},{8,12},{9,13},{10,... | collective-permute-start | bytes 1327112 | tf_op jit(solution)/shard_map/ppermute | solution.py:576
  192.7 17.8 %collective-permute-start.39 = (bf16[192,1152]{1,0:T(8,128)(2,1)S(1)}, bf16[192,1152]{1,0:T(8,128)(2,1)S(1)}, u32[]{:S(2)}, u32[]{:S(2)}) collective-permute-start(bf16[192,1152]{1,0:T(8,128)(2,1)S(1)} %get-tuple-element.355), channel_id=1, source_target_pairs={{0,2},{1,3},{2,0},{3,1},{4,6},{5,7},{6,4},{7,5},{8,10},{9,11},{10,... | collective-permute-start | bytes 1327112 | tf_op jit(solution)/shard_map/ppermute | solution.py:576
  194.0 3.1 %collective-permute-start.43 = (f32[16,240]{1,0:T(8,128)S(1)}, f32[16,240]{1,0:T(8,128)S(1)}, u32[]{:S(2)}, u32[]{:S(2)}) collective-permute-start(f32[16,240]{1,0:T(8,128)S(1)} %slice.78), channel_id=1, source_target_pairs={{0,1},{1,0},{2,3},{3,2},{4,5},{5,4},{6,7},{7,6},{8,9},{9,8},{10,11... | collective-permute-start | bytes 46088 | tf_op jit(solution)/shard_map/ppermute | solution.py:576
  194.1 10.7 %collective-permute-start.40 = (bf16[24,3840]{1,0:T(8,128)(2,1)S(1)}, bf16[24,3840]{1,0:T(8,128)(2,1)S(1)}, u32[]{:S(2)}, u32[]{:S(2)}) collective-permute-start(bf16[24,3840]{1,0:T(8,128)(2,1)S(1)} %get-tuple-element.356), channel_id=1, source_target_pairs={{0,8},{1,9},{2,10},{3,11},{4,12},{5,13},{6,14},{7,15},{8,0},{9,1},... | collective-permute-start | bytes 552968 | tf_op jit(solution)/shard_map/ppermute | solution.py:576
  194.1 16.4 %collective-permute-start.41 = (bf16[24,3840]{1,0:T(8,128)(2,1)S(1)}, bf16[24,3840]{1,0:T(8,128)(2,1)S(1)}, u32[]{:S(2)}, u32[]{:S(2)}) collective-permute-start(bf16[24,3840]{1,0:T(8,128)(2,1)S(1)} %get-tuple-element.357), channel_id=1, source_target_pairs={{0,16},{1,17},{2,18},{3,19},{4,20},{5,21},{6,22},{7,23},{8,24},{9,... | collective-permute-start | bytes 552968 | tf_op jit(solution)/shard_map/ppermute | solution.py:576
  197.1 13.4 %collective-permute-start.42 = (bf16[24,3840]{1,0:T(8,128)(2,1)S(1)}, bf16[24,3840]{1,0:T(8,128)(2,1)S(1)}, u32[]{:S(2)}, u32[]{:S(2)}) collective-permute-start(bf16[24,3840]{1,0:T(8,128)(2,1)S(1)} %get-tuple-element.358), channel_id=1, source_target_pairs={{0,24},{1,25},{2,26},{3,27},{4,28},{5,29},{6,30},{7,31},{8,16},{9,... | collective-permute-start | bytes 552968 | tf_op jit(solution)/shard_map/ppermute | solution.py:576
  210.8 22.3 %copy-start.25 = (f32[24,768]{1,0:T(8,128)S(1)}, f32[24,768]{1,0:T(8,128)}, u32[]{:S(2)}) copy-start(f32[24,768]{1,0:T(8,128)} %param.28) | copy-start | bytes 221188
  210.8 22.3 %copy-start.37 = (f32[24,768]{1,0:T(8,128)S(1)}, f32[24,768]{1,0:T(8,128)}, u32[]{:S(2)}) copy-start(f32[24,768]{1,0:T(8,128)} %param.38) | copy-start | bytes 221188
  210.8 22.3 %copy-start.38 = (f32[24,768]{1,0:T(8,128)S(1)}, f32[24,768]{1,0:T(8,128)}, u32[]{:S(2)}) copy-start(f32[24,768]{1,0:T(8,128)} %param.33) | copy-start | bytes 221188
  210.8 27.3 %copy-start.39 = (f32[240]{0:T(256)S(1)}, f32[240]{0:T(256)}, u32[]{:S(2)}) copy-start(f32[240]{0:T(256)} %param.31) | copy-start | bytes 2884
  210.8 27.3 %copy-start.40 = (f32[240]{0:T(256)S(1)}, f32[240]{0:T(256)}, u32[]{:S(2)}) copy-start(f32[240]{0:T(256)} %param.41) | copy-start | bytes 2884
  210.8 27.3 %copy-start.41 = (f32[240]{0:T(256)S(1)}, f32[240]{0:T(256)}, u32[]{:S(2)}) copy-start(f32[240]{0:T(256)} %param.36) | copy-start | bytes 2884
  210.8 27.9 %copy-start.21 = (f32[24,2304]{1,0:T(8,128)S(1)}, f32[24,2304]{1,0:T(8,128)}, u32[]{:S(2)}) copy-start(f32[24,2304]{1,0:T(8,128)} %param.27) | copy-start | bytes 663556
  210.9 27.9 %copy-start.28 = (f32[24,2304]{1,0:T(8,128)S(1)}, f32[24,2304]{1,0:T(8,128)}, u32[]{:S(2)}) copy-start(f32[24,2304]{1,0:T(8,128)} %param.37) | copy-start | bytes 663556
  210.9 27.8 %copy-start.29 = (f32[24,2304]{1,0:T(8,128)S(1)}, f32[24,2304]{1,0:T(8,128)}, u32[]{:S(2)}) copy-start(f32[24,2304]{1,0:T(8,128)} %param.32) | copy-start | bytes 663556
  210.9 4.9 %collective-permute-start.46 = (f32[4,240]{1,0:T(4,128)S(1)}, f32[4,240]{1,0:T(4,128)S(1)}, u32[]{:S(2)}, u32[]{:S(2)}) collective-permute-start(f32[4,240]{1,0:T(4,128)S(1)} %get-tuple-element.372), channel_id=1, source_target_pairs={{0,2},{1,3},{2,0},{3,1},{4,6},{5,7},{6,4},{7,5},{8,10},{9,11},{10,... | collective-permute-start | bytes 11528 | tf_op jit(solution)/shard_map/ppermute | solution.py:576
  211.6 4.2 %collective-permute-start.47 = (f32[4,240]{1,0:T(4,128)S(1)}, f32[4,240]{1,0:T(4,128)S(1)}, u32[]{:S(2)}, u32[]{:S(2)}) collective-permute-start(f32[4,240]{1,0:T(4,128)S(1)} %get-tuple-element.373), channel_id=1, source_target_pairs={{0,4},{1,5},{2,6},{3,7},{4,0},{5,1},{6,2},{7,3},{8,12},{9,13},{10,... | collective-permute-start | bytes 11528 | tf_op jit(solution)/shard_map/ppermute | solution.py:576
  212.2 4.6 %collective-permute-start.48 = (f32[4,240]{1,0:T(4,128)S(1)}, f32[4,240]{1,0:T(4,128)S(1)}, u32[]{:S(2)}, u32[]{:S(2)}) collective-permute-start(f32[4,240]{1,0:T(4,128)S(1)} %get-tuple-element.374), channel_id=1, source_target_pairs={{0,6},{1,7},{2,4},{3,5},{4,2},{5,3},{6,0},{7,1},{8,14},{9,15},{10,... | collective-permute-start | bytes 11528 | tf_op jit(solution)/shard_map/ppermute | solution.py:576
  214.4 5.9 %collective-permute-start.44 = (bf16[96,1152]{1,0:T(8,128)(2,1)S(1)}, bf16[96,1152]{1,0:T(8,128)(2,1)S(1)}, u32[]{:S(2)}, u32[]{:S(2)}) collective-permute-start(bf16[96,1152]{1,0:T(8,128)(2,1)S(1)} %get-tuple-element.370), channel_id=1, source_target_pairs={{0,2},{1,3},{2,0},{3,1},{4,6},{5,7},{6,4},{7,5},{8,10},{9,11},{10,... | collective-permute-start | bytes 663560 | tf_op jit(solution)/shard_map/ppermute | solution.py:576
  215.1 5.9 %collective-permute-start.45 = (bf16[96,1152]{1,0:T(8,128)(2,1)S(1)}, bf16[96,1152]{1,0:T(8,128)(2,1)S(1)}, u32[]{:S(2)}, u32[]{:S(2)}) collective-permute-start(bf16[96,1152]{1,0:T(8,128)(2,1)S(1)} %get-tuple-element.371), channel_id=1, source_target_pairs={{0,4},{1,5},{2,6},{3,7},{4,0},{5,1},{6,2},{7,3},{8,12},{9,13},{10,... | collective-permute-start | bytes 663560 | tf_op jit(solution)/shard_map/ppermute | solution.py:576
  221.2 10.2 %collective-permute-start.52 = (f32[1,240]{1,0:T(1,128)S(1)}, f32[1,240]{1,0:T(1,128)S(1)}, u32[]{:S(2)}, u32[]{:S(2)}) collective-permute-start(f32[1,240]{1,0:T(1,128)S(1)} %get-tuple-element.387), channel_id=1, source_target_pairs={{0,8},{1,9},{2,10},{3,11},{4,12},{5,13},{6,14},{7,15},{8,0},{9,1},... | collective-permute-start | bytes 2888 | tf_op jit(solution)/shard_map/ppermute | solution.py:576
  226.3 7.5 %collective-permute-start.53 = (f32[1,240]{1,0:T(1,128)S(1)}, f32[1,240]{1,0:T(1,128)S(1)}, u32[]{:S(2)}, u32[]{:S(2)}) collective-permute-start(f32[1,240]{1,0:T(1,128)S(1)} %get-tuple-element.388), channel_id=1, source_target_pairs={{0,16},{1,17},{2,18},{3,19},{4,20},{5,21},{6,22},{7,23},{8,24},{9,... | collective-permute-start | bytes 2888 | tf_op jit(solution)/shard_map/ppermute | solution.py:576
  227.0 6.8 %collective-permute-start.54 = (f32[1,240]{1,0:T(1,128)S(1)}, f32[1,240]{1,0:T(1,128)S(1)}, u32[]{:S(2)}, u32[]{:S(2)}) collective-permute-start(f32[1,240]{1,0:T(1,128)S(1)} %get-tuple-element.389), channel_id=1, source_target_pairs={{0,24},{1,25},{2,26},{3,27},{4,28},{5,29},{6,30},{7,31},{8,16},{9,... | collective-permute-start | bytes 2888 | tf_op jit(solution)/shard_map/ppermute | solution.py:576
  228.7 6.2 %collective-permute-start.49 = (bf16[24,2304]{1,0:T(8,128)(2,1)S(1)}, bf16[24,2304]{1,0:T(8,128)(2,1)S(1)}, u32[]{:S(2)}, u32[]{:S(2)}) collective-permute-start(bf16[24,2304]{1,0:T(8,128)(2,1)S(1)} %get-tuple-element.384), channel_id=1, source_target_pairs={{0,8},{1,9},{2,10},{3,11},{4,12},{5,13},{6,14},{7,15},{8,0},{9,1},... | collective-permute-start | bytes 331784 | tf_op jit(solution)/shard_map/ppermute | solution.py:576
  229.7 8.3 %collective-permute-start.50 = (bf16[24,2304]{1,0:T(8,128)(2,1)S(1)}, bf16[24,2304]{1,0:T(8,128)(2,1)S(1)}, u32[]{:S(2)}, u32[]{:S(2)}) collective-permute-start(bf16[24,2304]{1,0:T(8,128)(2,1)S(1)} %get-tuple-element.385), channel_id=1, source_target_pairs={{0,16},{1,17},{2,18},{3,19},{4,20},{5,21},{6,22},{7,23},{8,24},{9,... | collective-permute-start | bytes 331784 | tf_op jit(solution)/shard_map/ppermute | solution.py:576
  231.3 6.7 %collective-permute-start.51 = (bf16[24,2304]{1,0:T(8,128)(2,1)S(1)}, bf16[24,2304]{1,0:T(8,128)(2,1)S(1)}, u32[]{:S(2)}, u32[]{:S(2)}) collective-permute-start(bf16[24,2304]{1,0:T(8,128)(2,1)S(1)} %get-tuple-element.386), channel_id=1, source_target_pairs={{0,24},{1,25},{2,26},{3,27},{4,28},{5,29},{6,30},{7,31},{8,16},{9,... | collective-permute-start | bytes 331784 | tf_op jit(solution)/shard_map/ppermute | solution.py:576
  (33 other events, 312.0 us)
where the time goes:
time: 244 us; the launch traced here: 240 us
  Pallas kernels  88.7 us (36%)
  waiting for transfers between devices  66.1 us (27%)
  starting transfers between devices  66 us (27%)
  local copies, waits for them, and re-layouts  9.21 us (4%)
  other arithmetic  8.06 us (3%)
    pallas_call x31, Pallas kernels, whole_call(): pl.pallas_call(later(kernel, len(args), len(after)), in_specs=specs + [pl...  87.3 us
    ppermute x55, waiting for transfers between devices, swap(): return lax.ppermute(value, AXES, pairs)  66.1 us
    ppermute x55, starting transfers between devices, swap(): return lax.ppermute(value, AXES, pairs)  66 us
    unnamed x84, local copies, waits for them, and re-layouts  5.51 us
  transfers between devices with their start and end apart: 55, of which 28 were waited for; matrix products, arithmetic and copies ran while one was open for 3% of the time, Pallas kernels for 34%

commit v1 on v0

--- a/solution.py
+++ b/solution.py
@@ -571,6 +571,41 @@
     )
 
 
+def cast_kernel(values, out):
+    out[...] = values[...].astype(LOW)
+
+
+def cast(values, after=()):
+    return whole_call(cast_kernel, [shape(*values.shape)], [], 0, "cast", 1, values, after=after)[0]
+
+
+def vec_core_kernel(blocks, got, *outs):
+    half = got.shape[0]
+    total = blocks[:half, :] + got[...]
+    rows = half // 4
+    for k, out in enumerate(outs):
+        out[...] = total[rows * k : rows * (k + 1), :]
+
+
+def vec_core(blocks, got, after=()):
+    rows, cols = got.shape
+    return whole_call(
+        vec_core_kernel, [shape(rows // 4, cols, WIDE)] * 4, [], 0, "vec_core", 1, blocks, got, after=after
+    )
+
+
+def vec_plane_kernel(mine, a, b, c, *outs):
+    total = mine[...] + a[...] + b[...] + c[...]
+    for k, out in enumerate(outs):
+        out[...] = total[k : k + 1, :]
+
+
+def vec_plane(mine, got, after=()):
+    return whole_call(
+        vec_plane_kernel, [shape(1, mine.shape[1], WIDE)] * 4, [], 0, "vec_plane", 1, mine, *got, after=after
+    )
+
+
 def swap(value, bits):
     pairs = [(i, i ^ bits) for i in range(32)]
     return lax.ppermute(value, AXES, pairs)
@@ -591,8 +626,8 @@
         self.got = tuple(swap(value, bit) for value, bit in zip(values, bits))
         return self.got
 
-    def land(self, end=()):
-        values, *bits = self.steps.send(tie(self.got, end))
+    def land(self, end=(), behind=()):
+        values, *bits = self.steps.send((tie(self.got, end), tuple(behind)))
         if values is None:
             return bits[0]
         self.next = (values, bits[0])
@@ -600,36 +635,34 @@
 
 
 def spread(block):
-    got = yield (block,) * 3, (8, 16, 24)
-    left, right = near_pieces((block,) + got)
-    got = yield (left, right), (2, 4), (left, right)
-    left, right = first_pieces(left, right, got)
-    got = yield (left, right), (4, 2), (left, right)
-    own = second_pieces(left, right, got)
-    got = yield (own,), (1,), (own,)
+    got, behind = yield (block,) * 3, (8, 16, 24)
+    left, right = near_pieces((block,) + got, behind)
+    got, behind = yield (left, right), (2, 4), (left, right)
+    left, right = first_pieces(left, right, got, behind)
+    got, behind = yield (left, right), (4, 2), (left, right)
+    own = second_pieces(left, right, got, behind)
+    got, _ = yield (own,), (1,), (own,)
     yield None, (own, got[0])
 
 
 def collect(pieces):
-    (got,) = yield (pieces[1],), (1,)
-    left, right, *out = ready = core_sum(pieces[0], got)
-    got = yield out, (4, 2), tuple(ready)
-    left, right, *out = ready = half_sum(left, right, got)
-    got = yield out, (2, 4), tuple(ready)
-    total, *out = ready = last_sum(left, right, got)
-    got = yield out, (8, 16, 24), tuple(ready)
+    (got,), behind = yield (pieces[1],), (1,)
+    left, right, *out = ready = core_sum(pieces[0], got, behind)
+    got, behind = yield out, (4, 2), tuple(ready)
+    left, right, *out = ready = half_sum(left, right, got, behind)
+    got, behind = yield out, (2, 4), tuple(ready)
+    total, *out = ready = last_sum(left, right, got, behind)
+    got, _ = yield out, (8, 16, 24), tuple(ready)
     yield None, (sum((z.astype(WIDE) for z in got), total),)
 
 
 def collect_vec(blocks):
-    half = blocks.shape[0] // 2
-    (got,) = yield (blocks[half:],), (1,)
-    blocks = blocks[:half] + got
-    rows = half // 4
-    got = yield [blocks[rows * k : rows * (k + 1)] for k in (1, 2, 3)], (2, 4, 6), (blocks,)
-    blocks = sum(got, blocks[:rows])
-    got = yield [blocks[k : k + 1] for k in (1, 2, 3)], (8, 16, 24), (blocks,)
-    yield None, (sum(got, blocks[:1]).reshape(-1),)
+    (got,), behind = yield (blocks[blocks.shape[0] // 2 :],), (1,)
+    mine, *out = ready = vec_core(blocks, got, behind)
+    got, behind = yield out, (2, 4, 6), tuple(ready)
+    mine, *out = ready = vec_plane(mine, got, behind)
+    got, _ = yield out, (8, 16, 24), tuple(ready)
+    yield None, (sum(got, mine).reshape(-1),)
 
 
 def stack(whole):
@@ -649,7 +682,7 @@
     def issue(self, start=()):
         return ()
 
-    def land(self, end=()):
+    def land(self, end=(), behind=()):
         return self.result
 
 
@@ -713,11 +746,6 @@
     slopes = LOG2E * jnp.exp2(-8.0 * (jnp.arange(HEADS, dtype=jnp.int32).astype(WIDE) + 1.0) / HEADS)
     one = gather(block_one.astype(LOW))
     two = gather(jnp.concatenate([master_out, master_up], axis=1).astype(LOW))
-    if near:
-        three = gather(master_down.astype(LOW))
-    else:
-        whole = lax.all_gather(master_down.astype(LOW), AXES, axis=0, tiled=True)
-        three = Whole(stack(rearrange(whole, owners, shards)))
     one.issue()
     done = one.land((far, spans, slopes, order))
     one.issue(done)
@@ -733,10 +761,16 @@
     dy = cotangent[0]
     act_one, qkv, vec = project(x, order, one)
     done = two.land((qkv,))
-    sent = two.issue(done) + three.issue(done)
+    if near:
+        three = gather(master_down.astype(LOW))
+    else:
+        whole = lax.all_gather(master_down.astype(LOW), AXES, axis=0, tiled=True)
+        three = Whole(stack(rearrange(whole, owners, shards)))
+    two.issue(done)
     mixed_0, probs_0 = attend(0, qkv, far, spans, slopes, done)
+    three.issue((mixed_0,))
     done = two.land((mixed_0,))
-    done = done + three.land((mixed_0,) + sent + done)
+    done = done + three.land(done)
     sent = two.issue(done) + three.issue(done)
     mixed_1, probs_1 = attend(3, qkv, far, spans, slopes, done + (mixed_0,))
     done = three.land((mixed_1,) + sent)
@@ -761,8 +795,9 @@
     flow_two = scatter(grad_two)
     sent = flow_three.issue(done) + flow_two.issue(done)
     d0 = attend_back(0, qkv, dmixed, probs_0, spans, done)
-    done = flow_three.land(tuple(d0) + sent) + flow_two.land(tuple(d0) + sent)
-    sent = flow_three.issue(done) + flow_two.issue(done)
+    done = flow_two.land(tuple(d0) + sent)
+    done = done + flow_three.land(tuple(d0) + sent, done)
+    sent = flow_two.issue(done) + flow_three.issue(done)
     d1 = attend_back(3, qkv, dmixed, probs_1, spans, done + tuple(d0))
     d = [z for pair in zip(d0, d1) for z in pair]
     grad_one = one_grad(act_one, d)
@@ -781,17 +816,20 @@
         flow_vec = Whole((lax.psum_scatter(blocks.reshape(-1), AXES, scatter_dimension=0, tiled=True),))
     done = flow_one.land((blocks,) + sent) + flow_two.land((blocks,) + sent)
     sent = flow_one.issue(done) + flow_two.issue(done) + flow_vec.issue(done)
+    done = flow_one.land(sent)
+    sum_two, = flow_two.land(sent)
+    first = flow_one.issue(done)[:1]
+    flow_vec.land(done)
+    flow_vec.issue(first)
     upd_down = adamw(master_down, first_down, second_down, sum_three, RATE_MATRIX, DECAY_MATRIX)
-    sent = sent + upd_down
-    done = flow_one.land(sent) + flow_vec.land(sent)
-    sum_two, = flow_two.land(sent)
-    sent = flow_one.issue(done) + flow_vec.issue(done)
-    done = flow_one.land(sent) + flow_vec.land(sent)
-    sent = flow_one.issue(done) + flow_vec.issue(done)
+    done = flow_one.land()
+    first = flow_one.issue(done)[:1]
+    flow_vec.land(done)
+    flow_vec.issue(first)
     upd_out = adamw(master_out, first_out, second_out, sum_two[:, :D], RATE_MATRIX, DECAY_MATRIX)
     upd_up = adamw(master_up, first_up, second_up, sum_two[:, D:], RATE_MATRIX, DECAY_MATRIX)
-    sum_one, = flow_one.land(sent + upd_out + upd_up)
-    sum_vec, = flow_vec.land(sent + upd_out + upd_up)
+    sum_one, = flow_one.land(upd_out + upd_up)
+    sum_vec, = flow_vec.land()
     upd_qkv = adamw(master_qkv, first_qkv, second_qkv, sum_one, RATE_MATRIX, DECAY_MATRIX)
     upd_vec = adamw(master_vec, first_vec, second_vec, sum_vec, RATE_VECTOR, 0.0)
     return (

time: 244 us -> 246 us (level)
  starting transfers between devices: 66 us -> 70.3 us
    ppermute x55, starting transfers between devices: 66 us -> 70.3 us  [swap(): return lax.ppermute(value, AXES, pairs)]
    pallas_call x31 -> x33, Pallas kernels: 87.3 us -> 87.4 us  [whole_call(): pl.pallas_call(later(kernel, len(args), len(after)), in_specs=specs + [pl...]
  transfers between devices with their start and end apart: 55 -> 55, of which waited for: 28 -> 27; matrix products, arithmetic and copies ran while one was open for 3% -> 4% of each run, Pallas kernels for 34% -> 34%
where the time goes in v1:
time: 246 us; the launch traced here: 242 us
  Pallas kernels  88.8 us (36%)
  starting transfers between devices  70.3 us (29%)
  waiting for transfers between devices  64.3 us (26%)
  local copies, waits for them, and re-layouts  9.18 us (4%)
  other arithmetic  8.05 us (3%)
    pallas_call x33, Pallas kernels, whole_call(): pl.pallas_call(later(kernel, len(args), len(after)), in_specs=specs + [pl...  87.4 us
    ppermute x55, starting transfers between devices, swap(): return lax.ppermute(value, AXES, pairs)  70.3 us
    ppermute x55, waiting for transfers between devices, swap(): return lax.ppermute(value, AXES, pairs)  64.3 us
    unnamed x84, local copies, waits for them, and re-layouts  5.49 us
  transfers between devices with their start and end apart: 55, of which 27 were waited for; matrix products, arithmetic and copies ran while one was open for 4% of the time, Pallas kernels for 34%

profile of v1, /device:TPU:0, one launch (start us, length us, event | category | flops | bytes accessed | tf_op | source)
XLA Modules:
  0.0 242.2 jit_solution(15988637286218352652)
XLA Ops:
  2.5 3.1 %collective-permute-start = (bf16[24,2560]{1,0:T(8,128)(2,1)S(1)}, bf16[24,2560]{1,0:T(8,128)(2,1)S(1)}, u32[]{:S(2)}, u32[]{:S(2)}) collective-permute-start(bf16[24,2560]{1,0:T(8,128)(2,1)S(1)} %fusion.8.refs_0_), channel_id=1, source_target_pairs={{0,8},{1,9},{2,10},{3,11},{4,12},{5,13},{6,14},{7,15},{8,0},{9,1},... | collective-permute-start | bytes 368648 | tf_op jit(solution)/shard_map/ppermute | solution.py:611
  5.6 2.6 %collective-permute-start.1 = (bf16[24,2560]{1,0:T(8,128)(2,1)S(1)}, bf16[24,2560]{1,0:T(8,128)(2,1)S(1)}, u32[]{:S(2)}, u32[]{:S(2)}) collective-permute-start(bf16[24,2560]{1,0:T(8,128)(2,1)S(1)} %fusion.8.refs_0_), channel_id=1, source_target_pairs={{0,16},{1,17},{2,18},{3,19},{4,20},{5,21},{6,22},{7,23},{8,24},{9,... | collective-permute-start | bytes 368648 | tf_op jit(solution)/shard_map/ppermute | solution.py:611
  11.4 1.4 tables.1
  12.8 5.2 %collective-permute-done.1.refs_2_ = bf16[24,2560]{1,0:T(8,128)(2,1)S(1)} collective-permute-done((bf16[24,2560]{1,0:T(8,128)(2,1)S(1)}, bf16[24,2560]{1,0:T(8,128)(2,1)S(1)}, u32[]{:S(2)}, u32[]{:S(2)}) %collective-permute-start.1) | collective-permute-done | bytes 122912 | tf_op jit(solution)/shard_map/ppermute | solution.py:611
  18.0 1.6 collective-permute-start.3
  19.5 1.5 collective-permute-start.4
  21.1 3.1 %collective-permute-done.3.refs_1_ = bf16[96,1280]{1,0:T(8,128)(2,1)S(1)} collective-permute-done((bf16[96,1280]{1,0:T(8,128)(2,1)S(1)}, bf16[96,1280]{1,0:T(8,128)(2,1)S(1)}, u32[]{:S(2)}, u32[]{:S(2)}) %collective-permute-start.3) | collective-permute-done | bytes 245792 | tf_op jit(solution)/shard_map/ppermute | solution.py:611
  24.2 2.4 collective-permute-done.4.refs_3_
  26.7 1.6 collective-permute-start.5
  29.9 2.1 collective-permute-start.8
  32.0 1.6 collective-permute-start.9
  33.6 2.7 %collective-permute-done.5.refs_1_ = bf16[192,1280]{1,0:T(8,128)(2,1)S(1)} collective-permute-done((bf16[192,1280]{1,0:T(8,128)(2,1)S(1)}, bf16[192,1280]{1,0:T(8,128)(2,1)S(1)}, u32[]{:S(2)}, u32[]{:S(2)}) %collective-permute-start.5) | collective-permute-done | bytes 491552 | tf_op jit(solution)/shard_map/ppermute | solution.py:611
  37.2 6.5 %collective-permute-done.8.refs_2_ = bf16[24,3840]{1,0:T(8,128)(2,1)S(1)} collective-permute-done((bf16[24,3840]{1,0:T(8,128)(2,1)S(1)}, bf16[24,3840]{1,0:T(8,128)(2,1)S(1)}, u32[]{:S(2)}, u32[]{:S(2)}) %collective-permute-start.8) | collective-permute-done | bytes 184352 | tf_op jit(solution)/shard_map/ppermute | solution.py:611
  43.8 1.6 collective-permute-start.11
  45.9 1.9 collective-permute-done.10.refs_3_.refs_8_
  47.8 6.2 %project.1 = (bf16[576,768]{1,0:T(8,128)(2,1)S(1)}, bf16[576,2304]{1,0:T(8,128)(2,1)S(1)}, f32[16,768]{1,0:T(8,128)S(1)}) custom-call(bf16[576,768]{1,0:T(8,128)(2,1)S(1)} %bitcast.8, bf16[768,768]{1,0:T(8,128)(2,1)S(1)} %fusion.refs_1_.refs_4_.refs_0_, bf16[768,1280]{1,0:T(8,128)(2,1)S(1)} %second.3.refs_2_.refs_7_, ...), custom_call_target="tpu_custom_call" | custom-call | flops 2717908992 | bytes 9584640 | tf_op jit(solution)/shard_map/project/pallas_call | solution.py:64
  57.3 4.6 %attend.2 = (bf16[576,384]{1,0:T(8,128)(2,1)S(1)}, bf16[4,6,240,256]{3,2,1,0:T(8,128)(2,1)S(1)}) custom-call(s32[5,5]{1,0:T(8,128)S(1)} %get-tuple-element.220.refs_0_, f32[12]{0:T(128)S(1)} %exponential_multiply_fusion.refs_1_, bf16[576,2304]{1,0:T(8,128)(2,1)S(1)} %get-tuple-element.246.refs_2_.refs_1_, f32[4,240,256]{2,1,0:T(8,128)S(1)} %get-tuple-element.219.refs_3_, ...), custom_call_target="tpu_custom_call" | custom-call | flops 8999999488 | bytes 7028884 | tf_op jit(solution)/shard_map/attend/pallas_call | solution.py:64
  61.9 1.6 copy-done.16
  63.5 1.4 collective-permute-start.15
  64.8 4.0 %collective-permute-start.16 = (bf16[96,768]{1,0:T(8,128)(2,1)S(1)}, bf16[96,768]{1,0:T(8,128)(2,1)S(1)}, u32[]{:S(2)}, u32[]{:S(2)}) collective-permute-start(bf16[96,768]{1,0:T(8,128)(2,1)S(1)} %convert_element_type.47.refs_0_), channel_id=1, source_target_pairs={{0,16},{1,17},{2,18},{3,19},{4,20},{5,21},{6,22},{7,23},{8,24},{9,... | collective-permute-start | bytes 442376 | tf_op jit(solution)/shard_map/ppermute | solution.py:611
  68.8 1.5 collective-permute-start.17
  70.3 3.6 %collective-permute-done.13.refs_1_ = bf16[192,1920]{1,0:T(8,128)(2,1)S(1)} collective-permute-done((bf16[192,1920]{1,0:T(8,128)(2,1)S(1)}, bf16[192,1920]{1,0:T(8,128)(2,1)S(1)}, u32[]{:S(2)}, u32[]{:S(2)}) %collective-permute-start.13) | collective-permute-done | bytes 737312 | tf_op jit(solution)/shard_map/ppermute | solution.py:611
  74.4 5.3 %collective-permute-done.16.refs_2_ = bf16[96,768]{1,0:T(8,128)(2,1)S(1)} collective-permute-done((bf16[96,768]{1,0:T(8,128)(2,1)S(1)}, bf16[96,768]{1,0:T(8,128)(2,1)S(1)}, u32[]{:S(2)}, u32[]{:S(2)}) %collective-permute-start.16) | collective-permute-done | bytes 147488 | tf_op jit(solution)/shard_map/ppermute | solution.py:611
  79.9 1.5 collective-permute-start.19
  81.4 1.5 collective-permute-start.20
  82.9 4.6 %attend.3 = (bf16[576,384]{1,0:T(8,128)(2,1)S(1)}, bf16[4,6,240,256]{3,2,1,0:T(8,128)(2,1)S(1)}) custom-call(s32[5,5]{1,0:T(8,128)S(1)} %get-tuple-element.220.refs_0_, f32[12]{0:T(128)S(1)} %exponential_multiply_fusion.refs_1_, bf16[576,2304]{1,0:T(8,128)(2,1)S(1)} %get-tuple-element.246.refs_2_.refs_1_, f32[4,240,256]{2,1,0:T(8,128)S(1)} %get-tuple-element.219.refs_3_, ...), custom_call_target="tpu_custom_call" | custom-call | flops 8999999488 | bytes 7028884 | tf_op jit(solution)/shard_map/attend/pallas_call | solution.py:64
  87.5 1.7 copy-done.14
  90.6 1.6 collective-permute-start.21
  92.4 8.4 %upward.1 = (bf16[576,768]{1,0:T(8,128)(2,1)S(1)}, f32[576,768]{1,0:T(8,128)S(1)}, bf16[576,768]{1,0:T(8,128)(2,1)S(1)}, bf16[576,3072]{1,0:T(8,128)(2,1)S(1)}, bf16[576,3072]{1,0:T(8,128)(2,1)S(1)}) custom-call(bf16[576,768]{1,0:T(8,128)(2,1)S(1)} %bitcast.9, bf16[576,384]{1,0:T(8,128)(2,1)S(1)} %get-tuple-element.253.refs_7_.refs_1_, ...), custom_call_target="tpu_custom_call" | custom-call | flops 9512681472 | bytes 19513344 | tf_op jit(solution)/shard_map/upward/pallas_call | solution.py:64
  100.9 7.8 %down_grad.1 = (bf16[3072,384]{1,0:T(8,128)(2,1)S(1)}, bf16[3072,384]{1,0:T(8,128)(2,1)S(1)}) custom-call(s32[32]{0:T(128)S(1)} %get-tuple-element.431.refs_0_, bf16[576,3072]{1,0:T(8,128)(2,1)S(1)} %get-tuple-element.275.refs_1_.refs_2_, bf16[576,768]{1,0:T(8,128)(2,1)S(1)} %bitcast.5), custom_call_target="tpu_custom_call" | custom-call | flops 2717908992 | bytes 9142400 | tf_op jit(solution)/shard_map/down_grad/pallas_call | solution.py:64
  109.0 4.5 %collective-permute-done.23.refs_7_ = bf16[3072,384]{1,0:T(8,128)(2,1)S(1)} collective-permute-done((bf16[3072,384]{1,0:T(8,128)(2,1)S(1)}, bf16[3072,384]{1,0:T(8,128)(2,1)S(1)}, u32[]{:S(2)}, u32[]{:S(2)}) %collective-permute-start.23) | collective-permute-done | bytes 2359328 | tf_op jit(solution)/shard_map/ppermute | solution.py:611
  113.6 10.8 %downward.1 = (bf16[576,768]{1,0:T(8,128)(2,1)}, bf16[576,3072]{1,0:T(8,128)(2,1)S(1)}, f32[8,768]{1,0:T(8,128)S(1)}) custom-call(s32[32]{0:T(128)S(1)} %get-tuple-element.431.refs_0_, f32[16,768]{1,0:T(8,128)S(1)} %get-tuple-element.245.refs_3_.refs_1_.refs_0_, bf16[576,3072]{1,0:T(8,128)(2,1)S(1)} %get-tuple-element.275.refs_1_.refs_2_, ...), custom_call_target="tpu_custom_call" | custom-call | flops 5435817984 | bytes 18948224 | tf_op jit(solution)/shard_map/downward/pallas_call | solution.py:64
  125.9 1.4 collective-permute-start.26
  127.3 8.7 %hidden_grad.1 = (f32[576,768]{1,0:T(8,128)S(1)}, bf16[576,768]{1,0:T(8,128)(2,1)S(1)}, bf16[576,768]{1,0:T(8,128)(2,1)S(1)}, f32[8,768]{1,0:T(8,128)S(1)}) custom-call(f32[16,768]{1,0:T(8,128)S(1)} %get-tuple-element.245.refs_3_.refs_1_.refs_0_, bf16[768,768]{1,0:T(8,128)(2,1)S(1)} %fusion.refs_1_.refs_4_.refs_0_, ...), custom_call_target="tpu_custom_call" | custom-call | flops 4756340736 | bytes 16883712 | tf_op jit(solution)/shard_map/hidden_grad/pallas_call | solution.py:64
  136.0 5.8 %two_grad.1 = (bf16[768,1920]{1,0:T(8,128)(2,1)S(1)}, bf16[768,1920]{1,0:T(8,128)(2,1)S(1)}) custom-call(bf16[576,768]{1,0:T(8,128)(2,1)S(1)} %get-tuple-element.297.refs_0_, bf16[576,768]{1,0:T(8,128)(2,1)S(1)} %get-tuple-element.298.refs_1_, bf16[576,768]{1,0:T(8,128)(2,1)S(1)} %get-tuple-element.299.refs_2_, ...), custom_call_target="tpu_custom_call" | custom-call | flops 3397386240 | bytes 12091392 | tf_op jit(solution)/shard_map/two_grad/pallas_call | solution.py:64
  143.0 1.5 collective-permute-start.29
  144.5 6.3 %attend_back.2 = (bf16[576,384]{1,0:T(8,128)(2,1)S(1)}, bf16[576,384]{1,0:T(8,128)(2,1)S(1)}, bf16[576,384]{1,0:T(8,128)(2,1)S(1)}) custom-call(s32[5,5]{1,0:T(8,128)S(1)} %get-tuple-element.220.refs_0_, bf16[576,2304]{1,0:T(8,128)(2,1)S(1)} %get-tuple-element.246.refs_2_.refs_1_, bf16[576,768]{1,0:T(8,128)(2,1)S(1)} %get-tuple-element.293.refs_2_, ...), custom_call_target="tpu_custom_call" | custom-call | flops 12000000000 | bytes 7815268 | tf_op jit(solution)/shard_map/attend_back/pallas_call | solution.py:64
  152.8 2.7 %collective-permute-start.32 = (bf16[96,768]{1,0:T(8,128)(2,1)S(1)}, bf16[96,768]{1,0:T(8,128)(2,1)S(1)}, u32[]{:S(2)}, u32[]{:S(2)}) collective-permute-start(bf16[96,768]{1,0:T(8,128)(2,1)S(1)} %get-tuple-element.335.refs_9_), channel_id=1, source_target_pairs={{0,8},{1,9},{2,10},{3,11},{4,12},{5,13},{6,14},{7,15},{8,0},{9,1},... | collective-permute-start | bytes 442376 | tf_op jit(solution)/shard_map/ppermute | solution.py:611
  156.6 1.4 collective-permute-start.34
  157.9 1.5 collective-permute-start.30
  160.8 6.5 %attend_back.3 = (bf16[576,384]{1,0:T(8,128)(2,1)S(1)}, bf16[576,384]{1,0:T(8,128)(2,1)S(1)}, bf16[576,384]{1,0:T(8,128)(2,1)S(1)}) custom-call(s32[5,5]{1,0:T(8,128)S(1)} %get-tuple-element.220.refs_0_, bf16[576,2304]{1,0:T(8,128)(2,1)S(1)} %get-tuple-element.246.refs_2_.refs_1_, bf16[576,768]{1,0:T(8,128)(2,1)S(1)} %get-tuple-element.293.refs_2_, ...), custom_call_target="tpu_custom_call" | custom-call | flops 12000000000 | bytes 7815268 | tf_op jit(solution)/shard_map/attend_back/pallas_call | solution.py:64
  167.3 3.6 %one_grad.1 = (bf16[768,1152]{1,0:T(8,128)(2,1)S(1)}, bf16[768,1152]{1,0:T(8,128)(2,1)S(1)}) custom-call(bf16[576,768]{1,0:T(8,128)(2,1)S(1)} %get-tuple-element.329.refs_0_, bf16[576,384]{1,0:T(8,128)(2,1)S(1)} %get-tuple-element.308.refs_12_.refs_1_, bf16[576,384]{1,0:T(8,128)(2,1)S(1)} %get-tuple-element.326.refs_2_, ...), custom_call_target="tpu_custom_call" | custom-call | flops 2038431744 | bytes 7077888 | tf_op jit(solution)/shard_map/one_grad/pallas_call | solution.py:64
  170.9 4.4 %input_back.1.refs_2_ = f32[576,768]{1,0:T(8,128)S(1)} custom-call(bf16[768,768]{1,0:T(8,128)(2,1)S(1)} %fusion.refs_1_.refs_4_.refs_0_, bf16[576,384]{1,0:T(8,128)(2,1)S(1)} %get-tuple-element.308.refs_12_.refs_1_, bf16[576,384]{1,0:T(8,128)(2,1)S(1)} %get-tuple-element.326.refs_2_, bf16[576,384]{1,0:T(8,128)(2,1)S(1)} %get-tuple-element.311.refs_13_.refs_3_, ...), custom_call_target="tpu_custom_call" | custom-call | flops 2717908992 | bytes 9535488 | tf_op jit(solution)/shard_map/input_back/pallas_call | solution.py:64
  177.6 1.4 collective-permute-start.36
  179.0 1.4 collective-permute-start.37
  180.4 2.9 %input_grad.1 = (f32[576,768]{1,0:T(8,128)}, f32[8,768]{1,0:T(8,128)S(1)}) custom-call(bf16[576,768]{1,0:T(8,128)(2,1)S(1)} %bitcast.10, f32[16,768]{1,0:T(8,128)S(1)} %get-tuple-element.245.refs_3_.refs_1_.refs_0_, f32[576,768]{1,0:T(8,128)S(1)} %input_back.1.refs_2_, f32[576,768]{1,0:T(8,128)S(1)} %get-tuple-element.332.refs_3_, ...), custom_call_target="tpu_custom_call" | custom-call | flops 2038431744 | bytes 6266880 | tf_op jit(solution)/shard_map/input_grad/pallas_call | solution.py:64
  184.0 1.5 reshape.62
  185.5 2.0 gather_fusion
  187.6 1.4 collective-permute-done.36.refs_1_
  190.0 1.9 core_sum.5
  193.1 1.5 collective-permute-start.38
  196.2 1.9 collective-permute-start.41
  198.1 1.7 collective-permute-start.42
  201.0 4.9 %collective-permute-done.40 = bf16[24,3840]{1,0:T(8,128)(2,1)S(1)} collective-permute-done((bf16[24,3840]{1,0:T(8,128)(2,1)S(1)}, bf16[24,3840]{1,0:T(8,128)(2,1)S(1)}, u32[]{:S(2)}, u32[]{:S(2)}) %collective-permute-start.40) | collective-permute-done | bytes 184352 | tf_op jit(solution)/shard_map/ppermute | solution.py:611
  205.8 6.7 %collective-permute-done.41 = bf16[24,3840]{1,0:T(8,128)(2,1)S(1)} collective-permute-done((bf16[24,3840]{1,0:T(8,128)(2,1)S(1)}, bf16[24,3840]{1,0:T(8,128)(2,1)S(1)}, u32[]{:S(2)}, u32[]{:S(2)}) %collective-permute-start.41) | collective-permute-done | bytes 184352 | tf_op jit(solution)/shard_map/ppermute | solution.py:611
  212.8 1.4 collective-permute-start.44
  214.8 4.0 %collective-permute-done.44.refs_1_ = bf16[96,1152]{1,0:T(8,128)(2,1)S(1)} collective-permute-done((bf16[96,1152]{1,0:T(8,128)(2,1)S(1)}, bf16[96,1152]{1,0:T(8,128)(2,1)S(1)}, u32[]{:S(2)}, u32[]{:S(2)}) %collective-permute-start.44) | collective-permute-done | bytes 221216 | tf_op jit(solution)/shard_map/ppermute | solution.py:611
  218.8 1.4 collective-permute-start.49
  221.8 1.6 collective-permute-start.51
  223.5 4.5 %collective-permute-start.46 = (bf16[24,2304]{1,0:T(8,128)(2,1)S(1)}, bf16[24,2304]{1,0:T(8,128)(2,1)S(1)}, u32[]{:S(2)}, u32[]{:S(2)}) collective-permute-start(bf16[24,2304]{1,0:T(8,128)(2,1)S(1)} %get-tuple-element.382), channel_id=1, source_target_pairs={{0,8},{1,9},{2,10},{3,11},{4,12},{5,13},{6,14},{7,15},{8,0},{9,1},... | collective-permute-start | bytes 331784 | tf_op jit(solution)/shard_map/ppermute | solution.py:611
  229.0 1.4 collective-permute-start.48
  231.2 1.8 collective-permute-start.52
  233.0 3.0 %collective-permute-start.53 = (f32[1,240]{1,0:T(1,128)S(1)}, f32[1,240]{1,0:T(1,128)S(1)}, u32[]{:S(2)}, u32[]{:S(2)}) collective-permute-start(f32[1,240]{1,0:T(1,128)S(1)} %get-tuple-element.410), channel_id=1, source_target_pairs={{0,16},{1,17},{2,18},{3,19},{4,20},{5,21},{6,22},{7,23},{8,24},{9,... | collective-permute-start | bytes 2888 | tf_op jit(solution)/shard_map/ppermute | solution.py:611
  238.3 3.0 %collective-permute-done.54 = f32[1,240]{1,0:T(1,128)S(1)} collective-permute-done((f32[1,240]{1,0:T(1,128)S(1)}, f32[1,240]{1,0:T(1,128)S(1)}, u32[]{:S(2)}, u32[]{:S(2)}) %collective-permute-start.54) | collective-permute-done | bytes 992 | tf_op jit(solution)/shard_map/ppermute | solution.py:611
  (197 shorter events, 36.3 us)
Async XLA Ops:
  0.7 20.4 %copy-start.20 = (f32[24,3072]{1,0:T(8,128)S(1)}, f32[24,3072]{1,0:T(8,128)}, u32[]{:S(2)}) copy-start(f32[24,3072]{1,0:T(8,128)} %param.29) | copy-start | bytes 884740
  0.7 20.4 %copy-start.25 = (f32[24,768]{1,0:T(8,128)S(1)}, f32[24,768]{1,0:T(8,128)}, u32[]{:S(2)}) copy-start(f32[24,768]{1,0:T(8,128)} %param.28) | copy-start | bytes 221188
  2.5 10.2 %collective-permute-start = (bf16[24,2560]{1,0:T(8,128)(2,1)S(1)}, bf16[24,2560]{1,0:T(8,128)(2,1)S(1)}, u32[]{:S(2)}, u32[]{:S(2)}) collective-permute-start(bf16[24,2560]{1,0:T(8,128)(2,1)S(1)} %fusion.8.refs_0_), channel_id=1, source_target_pairs={{0,8},{1,9},{2,10},{3,11},{4,12},{5,13},{6,14},{7,15},{8,0},{9,1},... | collective-permute-start | bytes 368648 | tf_op jit(solution)/shard_map/ppermute | solution.py:611
  5.6 12.3 %collective-permute-start.1 = (bf16[24,2560]{1,0:T(8,128)(2,1)S(1)}, bf16[24,2560]{1,0:T(8,128)(2,1)S(1)}, u32[]{:S(2)}, u32[]{:S(2)}) collective-permute-start(bf16[24,2560]{1,0:T(8,128)(2,1)S(1)} %fusion.8.refs_0_), channel_id=1, source_target_pairs={{0,16},{1,17},{2,18},{3,19},{4,20},{5,21},{6,22},{7,23},{8,24},{9,... | collective-permute-start | bytes 368648 | tf_op jit(solution)/shard_map/ppermute | solution.py:611
  8.2 9.7 %collective-permute-start.2 = (bf16[24,2560]{1,0:T(8,128)(2,1)S(1)}, bf16[24,2560]{1,0:T(8,128)(2,1)S(1)}, u32[]{:S(2)}, u32[]{:S(2)}) collective-permute-start(bf16[24,2560]{1,0:T(8,128)(2,1)S(1)} %fusion.8.refs_0_), channel_id=1, source_target_pairs={{0,24},{1,25},{2,26},{3,27},{4,28},{5,29},{6,30},{7,31},{8,16},{9,... | collective-permute-start | bytes 368648 | tf_op jit(solution)/shard_map/ppermute | solution.py:611
  18.0 6.3 %collective-permute-start.3 = (bf16[96,1280]{1,0:T(8,128)(2,1)S(1)}, bf16[96,1280]{1,0:T(8,128)(2,1)S(1)}, u32[]{:S(2)}, u32[]{:S(2)}) collective-permute-start(bf16[96,1280]{1,0:T(8,128)(2,1)S(1)} %get-tuple-element.226.refs_0_), channel_id=1, source_target_pairs={{0,2},{1,3},{2,0},{3,1},{4,6},{5,7},{6,4},{7,5},{8,10},{9,11},{10,... | collective-permute-start | bytes 737288 | tf_op jit(solution)/shard_map/ppermute | solution.py:611
  19.5 7.1 %collective-permute-start.4 = (bf16[96,1280]{1,0:T(8,128)(2,1)S(1)}, bf16[96,1280]{1,0:T(8,128)(2,1)S(1)}, u32[]{:S(2)}, u32[]{:S(2)}) collective-permute-start(bf16[96,1280]{1,0:T(8,128)(2,1)S(1)} %get-tuple-element.227.refs_2_), channel_id=1, source_target_pairs={{0,4},{1,5},{2,6},{3,7},{4,0},{5,1},{6,2},{7,3},{8,12},{9,13},{10,... | collective-permute-start | bytes 737288 | tf_op jit(solution)/shard_map/ppermute | solution.py:611
  26.7 9.6 %collective-permute-start.5 = (bf16[192,1280]{1,0:T(8,128)(2,1)S(1)}, bf16[192,1280]{1,0:T(8,128)(2,1)S(1)}, u32[]{:S(2)}, u32[]{:S(2)}) collective-permute-start(bf16[192,1280]{1,0:T(8,128)(2,1)S(1)} %get-tuple-element.232.refs_0_), channel_id=1, source_target_pairs={{0,4},{1,5},{2,6},{3,7},{4,0},{5,1},{6,2},{7,3},{8,12},{9,13},{10,... | collective-permute-start | bytes 1474568 | tf_op jit(solution)/shard_map/ppermute | solution.py:611
  28.3 8.8 %collective-permute-start.6 = (bf16[192,1280]{1,0:T(8,128)(2,1)S(1)}, bf16[192,1280]{1,0:T(8,128)(2,1)S(1)}, u32[]{:S(2)}, u32[]{:S(2)}) collective-permute-start(bf16[192,1280]{1,0:T(8,128)(2,1)S(1)} %get-tuple-element.233.refs_2_), channel_id=1, source_target_pairs={{0,2},{1,3},{2,0},{3,1},{4,6},{5,7},{6,4},{7,5},{8,10},{9,11},{10,... | collective-permute-start | bytes 1474568 | tf_op jit(solution)/shard_map/ppermute | solution.py:611
  29.1 8.1 %collective-permute-start.7 = (bf16[24,3840]{1,0:T(8,128)(2,1)S(1)}, bf16[24,3840]{1,0:T(8,128)(2,1)S(1)}, u32[]{:S(2)}, u32[]{:S(2)}) collective-permute-start(bf16[24,3840]{1,0:T(8,128)(2,1)S(1)} %pad_maximum_fusion.refs_0_), channel_id=1, source_target_pairs={{0,8},{1,9},{2,10},{3,11},{4,12},{5,13},{6,14},{7,15},{8,0},{9,1},... | collective-permute-start | bytes 552968 | tf_op jit(solution)/shard_map/ppermute | solution.py:611
  29.9 13.8 %collective-permute-start.8 = (bf16[24,3840]{1,0:T(8,128)(2,1)S(1)}, bf16[24,3840]{1,0:T(8,128)(2,1)S(1)}, u32[]{:S(2)}, u32[]{:S(2)}) collective-permute-start(bf16[24,3840]{1,0:T(8,128)(2,1)S(1)} %pad_maximum_fusion.refs_0_), channel_id=1, source_target_pairs={{0,16},{1,17},{2,18},{3,19},{4,20},{5,21},{6,22},{7,23},{8,24},{9,... | collective-permute-start | bytes 552968 | tf_op jit(solution)/shard_map/ppermute | solution.py:611
  32.0 11.7 %collective-permute-start.9 = (bf16[24,3840]{1,0:T(8,128)(2,1)S(1)}, bf16[24,3840]{1,0:T(8,128)(2,1)S(1)}, u32[]{:S(2)}, u32[]{:S(2)}) collective-permute-start(bf16[24,3840]{1,0:T(8,128)(2,1)S(1)} %pad_maximum_fusion.refs_0_), channel_id=1, source_target_pairs={{0,24},{1,25},{2,26},{3,27},{4,28},{5,29},{6,30},{7,31},{8,16},{9,... | collective-permute-start | bytes 552968 | tf_op jit(solution)/shard_map/ppermute | solution.py:611
  43.8 4.0 %collective-permute-start.10 = (bf16[768,1280]{1,0:T(8,128)(2,1)S(1)}, bf16[768,1280]{1,0:T(8,128)(2,1)S(1)}, u32[]{:S(2)}, u32[]{:S(2)}) collective-permute-start(bf16[768,1280]{1,0:T(8,128)(2,1)S(1)} %second.3.refs_2_.refs_7_), channel_id=1, source_target_pairs={{0,1},{1,0},{2,3},{3,2},{4,5},{5,4},{6,7},{7,6},{8,9},{9,8},{10,11... | collective-permute-start | bytes 5898248 | tf_op jit(solution)/shard_map/ppermute | solution.py:611
  43.8 11.0 %collective-permute-start.11 = (bf16[96,1920]{1,0:T(8,128)(2,1)S(1)}, bf16[96,1920]{1,0:T(8,128)(2,1)S(1)}, u32[]{:S(2)}, u32[]{:S(2)}) collective-permute-start(bf16[96,1920]{1,0:T(8,128)(2,1)S(1)} %get-tuple-element.247.refs_0_), channel_id=1, source_target_pairs={{0,2},{1,3},{2,0},{3,1},{4,6},{5,7},{6,4},{7,5},{8,10},{9,11},{10,... | collective-permute-start | bytes 1105928 | tf_op jit(solution)/shard_map/ppermute | solution.py:611
  45.4 10.7 %collective-permute-start.12 = (bf16[96,1920]{1,0:T(8,128)(2,1)S(1)}, bf16[96,1920]{1,0:T(8,128)(2,1)S(1)}, u32[]{:S(2)}, u32[]{:S(2)}) collective-permute-start(bf16[96,1920]{1,0:T(8,128)(2,1)S(1)} %get-tuple-element.248.refs_2_), channel_id=1, source_target_pairs={{0,4},{1,5},{2,6},{3,7},{4,0},{5,1},{6,2},{7,3},{8,12},{9,13},{10,... | collective-permute-start | bytes 1105928 | tf_op jit(solution)/shard_map/ppermute | solution.py:611
  56.2 17.8 %collective-permute-start.13 = (bf16[192,1920]{1,0:T(8,128)(2,1)S(1)}, bf16[192,1920]{1,0:T(8,128)(2,1)S(1)}, u32[]{:S(2)}, u32[]{:S(2)}) collective-permute-start(bf16[192,1920]{1,0:T(8,128)(2,1)S(1)} %get-tuple-element.254.refs_4_.refs_0_), channel_id=1, source_target_pairs={{0,4},{1,5},{2,6},{3,7},{4,0},{5,1},{6,2},{7,3},{8,12},{9,13},{10,... | collective-permute-start | bytes 2211848 | tf_op jit(solution)/shard_map/ppermute | solution.py:611
  56.7 17.4 %collective-permute-start.14 = (bf16[192,1920]{1,0:T(8,128)(2,1)S(1)}, bf16[192,1920]{1,0:T(8,128)(2,1)S(1)}, u32[]{:S(2)}, u32[]{:S(2)}) collective-permute-start(bf16[192,1920]{1,0:T(8,128)(2,1)S(1)} %get-tuple-element.255.refs_5_.refs_2_), channel_id=1, source_target_pairs={{0,2},{1,3},{2,0},{3,1},{4,6},{5,7},{6,4},{7,5},{8,10},{9,11},{10,... | collective-permute-start | bytes 2211848 | tf_op jit(solution)/shard_map/ppermute | solution.py:611
  63.5 10.9 %collective-permute-start.15 = (bf16[96,768]{1,0:T(8,128)(2,1)S(1)}, bf16[96,768]{1,0:T(8,128)(2,1)S(1)}, u32[]{:S(2)}, u32[]{:S(2)}) collective-permute-start(bf16[96,768]{1,0:T(8,128)(2,1)S(1)} %convert_element_type.47.refs_0_), channel_id=1, source_target_pairs={{0,8},{1,9},{2,10},{3,11},{4,12},{5,13},{6,14},{7,15},{8,0},{9,1},... | collective-permute-start | bytes 442376 | tf_op jit(solution)/shard_map/ppermute | solution.py:611
  64.8 14.9 %collective-permute-start.16 = (bf16[96,768]{1,0:T(8,128)(2,1)S(1)}, bf16[96,768]{1,0:T(8,128)(2,1)S(1)}, u32[]{:S(2)}, u32[]{:S(2)}) collective-permute-start(bf16[96,768]{1,0:T(8,128)(2,1)S(1)} %convert_element_type.47.refs_0_), channel_id=1, source_target_pairs={{0,16},{1,17},{2,18},{3,19},{4,20},{5,21},{6,22},{7,23},{8,24},{9,... | collective-permute-start | bytes 442376 | tf_op jit(solution)/shard_map/ppermute | solution.py:611
  68.8 10.9 %collective-permute-start.17 = (bf16[96,768]{1,0:T(8,128)(2,1)S(1)}, bf16[96,768]{1,0:T(8,128)(2,1)S(1)}, u32[]{:S(2)}, u32[]{:S(2)}) collective-permute-start(bf16[96,768]{1,0:T(8,128)(2,1)S(1)} %convert_element_type.47.refs_0_), channel_id=1, source_target_pairs={{0,24},{1,25},{2,26},{3,27},{4,28},{5,29},{6,30},{7,31},{8,16},{9,... | collective-permute-start | bytes 442376 | tf_op jit(solution)/shard_map/ppermute | solution.py:611
  79.8 10.6 %collective-permute-start.18 = (bf16[768,1920]{1,0:T(8,128)(2,1)S(1)}, bf16[768,1920]{1,0:T(8,128)(2,1)S(1)}, u32[]{:S(2)}, u32[]{:S(2)}) collective-permute-start(bf16[768,1920]{1,0:T(8,128)(2,1)S(1)} %second.4.refs_4_.refs_5_), channel_id=1, source_target_pairs={{0,1},{1,0},{2,3},{3,2},{4,5},{5,4},{6,7},{7,6},{8,9},{9,8},{10,11... | collective-permute-start | bytes 8847368 | tf_op jit(solution)/shard_map/ppermute | solution.py:611
  79.9 9.4 %collective-permute-start.19 = (bf16[384,384]{1,0:T(8,128)(2,1)S(1)}, bf16[384,384]{1,0:T(8,128)(2,1)S(1)}, u32[]{:S(2)}, u32[]{:S(2)}) collective-permute-start(bf16[384,384]{1,0:T(8,128)(2,1)S(1)} %get-tuple-element.268.refs_5_.refs_0_), channel_id=1, source_target_pairs={{0,2},{1,3},{2,0},{3,1},{4,6},{5,7},{6,4},{7,5},{8,10},{9,11},{10,... | collective-permute-start | bytes 884744 | tf_op jit(solution)/shard_map/ppermute | solution.py:611
  81.4 9.1 %collective-permute-start.20 = (bf16[384,384]{1,0:T(8,128)(2,1)S(1)}, bf16[384,384]{1,0:T(8,128)(2,1)S(1)}, u32[]{:S(2)}, u32[]{:S(2)}) collective-permute-start(bf16[384,384]{1,0:T(8,128)(2,1)S(1)} %get-tuple-element.269.refs_6_.refs_2_), channel_id=1, source_target_pairs={{0,4},{1,5},{2,6},{3,7},{4,0},{5,1},{6,2},{7,3},{8,12},{9,13},{10,... | collective-permute-start | bytes 884744 | tf_op jit(solution)/shard_map/ppermute | solution.py:611
  90.6 18.1 %collective-permute-start.21 = (bf16[768,384]{1,0:T(8,128)(2,1)S(1)}, bf16[768,384]{1,0:T(8,128)(2,1)S(1)}, u32[]{:S(2)}, u32[]{:S(2)}) collective-permute-start(bf16[768,384]{1,0:T(8,128)(2,1)S(1)} %get-tuple-element.278.refs_7_.refs_0_), channel_id=1, source_target_pairs={{0,4},{1,5},{2,6},{3,7},{4,0},{5,1},{6,2},{7,3},{8,12},{9,13},{10,... | collective-permute-start | bytes 1769480 | tf_op jit(solution)/shard_map/ppermute | solution.py:611
  92.2 16.5 %collective-permute-start.22 = (bf16[768,384]{1,0:T(8,128)(2,1)S(1)}, bf16[768,384]{1,0:T(8,128)(2,1)S(1)}, u32[]{:S(2)}, u32[]{:S(2)}) collective-permute-start(bf16[768,384]{1,0:T(8,128)(2,1)S(1)} %get-tuple-element.279.refs_8_.refs_2_), channel_id=1, source_target_pairs={{0,2},{1,3},{2,0},{3,1},{4,6},{5,7},{6,4},{7,5},{8,10},{9,11},{10,... | collective-permute-start | bytes 1769480 | tf_op jit(solution)/shard_map/ppermute | solution.py:611
  108.9 4.6 %collective-permute-start.23 = (bf16[3072,384]{1,0:T(8,128)(2,1)S(1)}, bf16[3072,384]{1,0:T(8,128)(2,1)S(1)}, u32[]{:S(2)}, u32[]{:S(2)}) collective-permute-start(bf16[3072,384]{1,0:T(8,128)(2,1)S(1)} %second.5.refs_6_), channel_id=1, source_target_pairs={{0,1},{1,0},{2,3},{3,2},{4,5},{5,4},{6,7},{7,6},{8,9},{9,8},{10,11... | collective-permute-start | bytes 7077896 | tf_op jit(solution)/shard_map/ppermute | solution.py:611
  113.5 11.0 %collective-permute-start.24 = (bf16[3072,384]{1,0:T(8,128)(2,1)S(1)}, bf16[3072,384]{1,0:T(8,128)(2,1)S(1)}, u32[]{:S(2)}, u32[]{:S(2)}) collective-permute-start(bf16[3072,384]{1,0:T(8,128)(2,1)S(1)} %get-tuple-element.287), channel_id=1, source_target_pairs={{0,1},{1,0},{2,3},{3,2},{4,5},{5,4},{6,7},{7,6},{8,9},{9,8},{10,11... | collective-permute-start | bytes 7077896 | tf_op jit(solution)/shard_map/ppermute | solution.py:611
  125.0 16.9 %collective-permute-start.25 = (bf16[768,384]{1,0:T(8,128)(2,1)S(1)}, bf16[768,384]{1,0:T(8,128)(2,1)S(1)}, u32[]{:S(2)}, u32[]{:S(2)}) collective-permute-start(bf16[768,384]{1,0:T(8,128)(2,1)S(1)} %get-tuple-element.295.refs_9_), channel_id=1, source_target_pairs={{0,4},{1,5},{2,6},{3,7},{4,0},{5,1},{6,2},{7,3},{8,12},{9,13},{10,... | collective-permute-start | bytes 1769480 | tf_op jit(solution)/shard_map/ppermute | solution.py:611
  125.9 16.0 %collective-permute-start.26 = (bf16[768,384]{1,0:T(8,128)(2,1)S(1)}, bf16[768,384]{1,0:T(8,128)(2,1)S(1)}, u32[]{:S(2)}, u32[]{:S(2)}) collective-permute-start(bf16[768,384]{1,0:T(8,128)(2,1)S(1)} %get-tuple-element.296.refs_10_), channel_id=1, source_target_pairs={{0,2},{1,3},{2,0},{3,1},{4,6},{5,7},{6,4},{7,5},{8,10},{9,11},{10,... | collective-permute-start | bytes 1769480 | tf_op jit(solution)/shard_map/ppermute | solution.py:611
  142.1 9.9 %collective-permute-start.27 = (bf16[768,1920]{1,0:T(8,128)(2,1)S(1)}, bf16[768,1920]{1,0:T(8,128)(2,1)S(1)}, u32[]{:S(2)}, u32[]{:S(2)}) collective-permute-start(bf16[768,1920]{1,0:T(8,128)(2,1)S(1)} %get-tuple-element.310.refs_9_), channel_id=1, source_target_pairs={{0,1},{1,0},{2,3},{3,2},{4,5},{5,4},{6,7},{7,6},{8,9},{9,8},{10,11... | collective-permute-start | bytes 8847368 | tf_op jit(solution)/shard_map/ppermute | solution.py:611
  142.2 9.4 %collective-permute-start.28 = (bf16[384,384]{1,0:T(8,128)(2,1)S(1)}, bf16[384,384]{1,0:T(8,128)(2,1)S(1)}, u32[]{:S(2)}, u32[]{:S(2)}) collective-permute-start(bf16[384,384]{1,0:T(8,128)(2,1)S(1)} %get-tuple-element.313.refs_6_), channel_id=1, source_target_pairs={{0,2},{1,3},{2,0},{3,1},{4,6},{5,7},{6,4},{7,5},{8,10},{9,11},{10,... | collective-permute-start | bytes 884744 | tf_op jit(solution)/shard_map/ppermute | solution.py:611
  143.0 9.1 %collective-permute-start.29 = (bf16[384,384]{1,0:T(8,128)(2,1)S(1)}, bf16[384,384]{1,0:T(8,128)(2,1)S(1)}, u32[]{:S(2)}, u32[]{:S(2)}) collective-permute-start(bf16[384,384]{1,0:T(8,128)(2,1)S(1)} %get-tuple-element.314.refs_7_), channel_id=1, source_target_pairs={{0,4},{1,5},{2,6},{3,7},{4,0},{5,1},{6,2},{7,3},{8,12},{9,13},{10,... | collective-permute-start | bytes 884744 | tf_op jit(solution)/shard_map/ppermute | solution.py:611
  152.8 22.5 %collective-permute-start.32 = (bf16[96,768]{1,0:T(8,128)(2,1)S(1)}, bf16[96,768]{1,0:T(8,128)(2,1)S(1)}, u32[]{:S(2)}, u32[]{:S(2)}) collective-permute-start(bf16[96,768]{1,0:T(8,128)(2,1)S(1)} %get-tuple-element.335.refs_9_), channel_id=1, source_target_pairs={{0,8},{1,9},{2,10},{3,11},{4,12},{5,13},{6,14},{7,15},{8,0},{9,1},... | collective-permute-start | bytes 442376 | tf_op jit(solution)/shard_map/ppermute | solution.py:611
  155.5 19.8 %collective-permute-start.33 = (bf16[96,768]{1,0:T(8,128)(2,1)S(1)}, bf16[96,768]{1,0:T(8,128)(2,1)S(1)}, u32[]{:S(2)}, u32[]{:S(2)}) collective-permute-start(bf16[96,768]{1,0:T(8,128)(2,1)S(1)} %get-tuple-element.336.refs_10_), channel_id=1, source_target_pairs={{0,16},{1,17},{2,18},{3,19},{4,20},{5,21},{6,22},{7,23},{8,24},{9,... | collective-permute-start | bytes 442376 | tf_op jit(solution)/shard_map/ppermute | solution.py:611
  156.6 18.8 %collective-permute-start.34 = (bf16[96,768]{1,0:T(8,128)(2,1)S(1)}, bf16[96,768]{1,0:T(8,128)(2,1)S(1)}, u32[]{:S(2)}, u32[]{:S(2)}) collective-permute-start(bf16[96,768]{1,0:T(8,128)(2,1)S(1)} %get-tuple-element.337.refs_11_), channel_id=1, source_target_pairs={{0,24},{1,25},{2,26},{3,27},{4,28},{5,29},{6,30},{7,31},{8,16},{9,... | collective-permute-start | bytes 442376 | tf_op jit(solution)/shard_map/ppermute | solution.py:611
  157.9 18.1 %collective-permute-start.30 = (bf16[192,1920]{1,0:T(8,128)(2,1)S(1)}, bf16[192,1920]{1,0:T(8,128)(2,1)S(1)}, u32[]{:S(2)}, u32[]{:S(2)}) collective-permute-start(bf16[192,1920]{1,0:T(8,128)(2,1)S(1)} %get-tuple-element.333.refs_6_), channel_id=1, source_target_pairs={{0,4},{1,5},{2,6},{3,7},{4,0},{5,1},{6,2},{7,3},{8,12},{9,13},{10,... | collective-permute-start | bytes 2211848 | tf_op jit(solution)/shard_map/ppermute | solution.py:611
  159.5 16.9 %collective-permute-start.31 = (bf16[192,1920]{1,0:T(8,128)(2,1)S(1)}, bf16[192,1920]{1,0:T(8,128)(2,1)S(1)}, u32[]{:S(2)}, u32[]{:S(2)}) collective-permute-start(bf16[192,1920]{1,0:T(8,128)(2,1)S(1)} %get-tuple-element.334.refs_7_), channel_id=1, source_target_pairs={{0,2},{1,3},{2,0},{3,1},{4,6},{5,7},{6,4},{7,5},{8,10},{9,11},{10,... | collective-permute-start | bytes 2211848 | tf_op jit(solution)/shard_map/ppermute | solution.py:611
  177.5 12.6 %collective-permute-start.35 = (bf16[768,1152]{1,0:T(8,128)(2,1)S(1)}, bf16[768,1152]{1,0:T(8,128)(2,1)}, u32[]{:S(2)}, u32[]{:S(2)}) collective-permute-start(bf16[768,1152]{1,0:T(8,128)(2,1)S(1)} %get-tuple-element.345.refs_10_), channel_id=1, source_target_pairs={{0,1},{1,0},{2,3},{3,2},{4,5},{5,4},{6,7},{7,6},{8,9},{9,8},{10,11... | collective-permute-start | bytes 5308424 | tf_op jit(solution)/shard_map/ppermute | solution.py:611
  177.6 11.4 %collective-permute-start.36 = (bf16[96,1920]{1,0:T(8,128)(2,1)}, bf16[96,1920]{1,0:T(8,128)(2,1)}, u32[]{:S(2)}, u32[]{:S(2)}) collective-permute-start(bf16[96,1920]{1,0:T(8,128)(2,1)} %get-tuple-element.349.refs_6_), channel_id=1, source_target_pairs={{0,2},{1,3},{2,0},{3,1},{4,6},{5,7},{6,4},{7,5},{8,10},{9,11},{10,... | collective-permute-start | bytes 1105928 | tf_op jit(solution)/shard_map/ppermute | solution.py:611
  179.0 11.0 %collective-permute-start.37 = (bf16[96,1920]{1,0:T(8,128)(2,1)}, bf16[96,1920]{1,0:T(8,128)(2,1)}, u32[]{:S(2)}, u32[]{:S(2)}) collective-permute-start(bf16[96,1920]{1,0:T(8,128)(2,1)} %get-tuple-element.350.refs_7_), channel_id=1, source_target_pairs={{0,4},{1,5},{2,6},{3,7},{4,0},{5,1},{6,2},{7,3},{8,12},{9,13},{10,... | collective-permute-start | bytes 1105928 | tf_op jit(solution)/shard_map/ppermute | solution.py:611
  193.1 19.4 %collective-permute-start.38 = (bf16[192,1152]{1,0:T(8,128)(2,1)S(1)}, bf16[192,1152]{1,0:T(8,128)(2,1)S(1)}, u32[]{:S(2)}, u32[]{:S(2)}) collective-permute-start(bf16[192,1152]{1,0:T(8,128)(2,1)S(1)} %get-tuple-element.362), channel_id=1, source_target_pairs={{0,4},{1,5},{2,6},{3,7},{4,0},{5,1},{6,2},{7,3},{8,12},{9,13},{10,... | collective-permute-start | bytes 1327112 | tf_op jit(solution)/shard_map/ppermute | solution.py:611
  194.6 17.9 %collective-permute-start.39 = (bf16[192,1152]{1,0:T(8,128)(2,1)S(1)}, bf16[192,1152]{1,0:T(8,128)(2,1)S(1)}, u32[]{:S(2)}, u32[]{:S(2)}) collective-permute-start(bf16[192,1152]{1,0:T(8,128)(2,1)S(1)} %get-tuple-element.363), channel_id=1, source_target_pairs={{0,2},{1,3},{2,0},{3,1},{4,6},{5,7},{6,4},{7,5},{8,10},{9,11},{10,... | collective-permute-start | bytes 1327112 | tf_op jit(solution)/shard_map/ppermute | solution.py:611
  195.3 2.7 %collective-permute-start.43 = (f32[16,240]{1,0:T(8,128)S(1)}, f32[16,240]{1,0:T(8,128)S(1)}, u32[]{:S(2)}, u32[]{:S(2)}) collective-permute-start(f32[16,240]{1,0:T(8,128)S(1)} %slice.42), channel_id=1, source_target_pairs={{0,1},{1,0},{2,3},{3,2},{4,5},{5,4},{6,7},{7,6},{8,9},{9,8},{10,11... | collective-permute-start | bytes 46088 | tf_op jit(solution)/shard_map/ppermute | solution.py:611
  195.3 10.5 %collective-permute-start.40 = (bf16[24,3840]{1,0:T(8,128)(2,1)S(1)}, bf16[24,3840]{1,0:T(8,128)(2,1)S(1)}, u32[]{:S(2)}, u32[]{:S(2)}) collective-permute-start(bf16[24,3840]{1,0:T(8,128)(2,1)S(1)} %get-tuple-element.364), channel_id=1, source_target_pairs={{0,8},{1,9},{2,10},{3,11},{4,12},{5,13},{6,14},{7,15},{8,0},{9,1},... | collective-permute-start | bytes 552968 | tf_op jit(solution)/shard_map/ppermute | solution.py:611
  196.2 16.3 %collective-permute-start.41 = (bf16[24,3840]{1,0:T(8,128)(2,1)S(1)}, bf16[24,3840]{1,0:T(8,128)(2,1)S(1)}, u32[]{:S(2)}, u32[]{:S(2)}) collective-permute-start(bf16[24,3840]{1,0:T(8,128)(2,1)S(1)} %get-tuple-element.365), channel_id=1, source_target_pairs={{0,16},{1,17},{2,18},{3,19},{4,20},{5,21},{6,22},{7,23},{8,24},{9,... | collective-permute-start | bytes 552968 | tf_op jit(solution)/shard_map/ppermute | solution.py:611
  198.1 14.4 %collective-permute-start.42 = (bf16[24,3840]{1,0:T(8,128)(2,1)S(1)}, bf16[24,3840]{1,0:T(8,128)(2,1)S(1)}, u32[]{:S(2)}, u32[]{:S(2)}) collective-permute-start(bf16[24,3840]{1,0:T(8,128)(2,1)S(1)} %get-tuple-element.366), channel_id=1, source_target_pairs={{0,24},{1,25},{2,26},{3,27},{4,28},{5,29},{6,30},{7,31},{8,16},{9,... | collective-permute-start | bytes 552968 | tf_op jit(solution)/shard_map/ppermute | solution.py:611
  201.0 19.2 %copy-start.28 = (f32[24,3072]{1,0:T(8,128)S(1)}, f32[24,3072]{1,0:T(8,128)}, u32[]{:S(2)}) copy-start(f32[24,3072]{1,0:T(8,128)} %param.34) | copy-start | bytes 884740
  212.8 24.4 %copy-start.22 = (f32[24,2304]{1,0:T(8,128)S(1)}, f32[24,2304]{1,0:T(8,128)}, u32[]{:S(2)}) copy-start(f32[24,2304]{1,0:T(8,128)} %param.27) | copy-start | bytes 663556
  212.8 24.4 %copy-start.29 = (f32[24,2304]{1,0:T(8,128)S(1)}, f32[24,2304]{1,0:T(8,128)}, u32[]{:S(2)}) copy-start(f32[24,2304]{1,0:T(8,128)} %param.37) | copy-start | bytes 663556
  212.8 24.4 %copy-start.30 = (f32[24,2304]{1,0:T(8,128)S(1)}, f32[24,2304]{1,0:T(8,128)}, u32[]{:S(2)}) copy-start(f32[24,2304]{1,0:T(8,128)} %param.32) | copy-start | bytes 663556
  212.8 6.0 %collective-permute-start.44 = (bf16[96,1152]{1,0:T(8,128)(2,1)S(1)}, bf16[96,1152]{1,0:T(8,128)(2,1)S(1)}, u32[]{:S(2)}, u32[]{:S(2)}) collective-permute-start(bf16[96,1152]{1,0:T(8,128)(2,1)S(1)} %get-tuple-element.374), channel_id=1, source_target_pairs={{0,2},{1,3},{2,0},{3,1},{4,6},{5,7},{6,4},{7,5},{8,10},{9,11},{10,... | collective-permute-start | bytes 663560 | tf_op jit(solution)/shard_map/ppermute | solution.py:611
  214.2 9.2 %collective-permute-start.45 = (bf16[96,1152]{1,0:T(8,128)(2,1)S(1)}, bf16[96,1152]{1,0:T(8,128)(2,1)S(1)}, u32[]{:S(2)}, u32[]{:S(2)}) collective-permute-start(bf16[96,1152]{1,0:T(8,128)(2,1)S(1)} %get-tuple-element.375), channel_id=1, source_target_pairs={{0,4},{1,5},{2,6},{3,7},{4,0},{5,1},{6,2},{7,3},{8,12},{9,13},{10,... | collective-permute-start | bytes 663560 | tf_op jit(solution)/shard_map/ppermute | solution.py:611
  218.8 10.2 %collective-permute-start.49 = (f32[4,240]{1,0:T(4,128)S(1)}, f32[4,240]{1,0:T(4,128)S(1)}, u32[]{:S(2)}, u32[]{:S(2)}) collective-permute-start(f32[4,240]{1,0:T(4,128)S(1)} %get-tuple-element.399), channel_id=1, source_target_pairs={{0,2},{1,3},{2,0},{3,1},{4,6},{5,7},{6,4},{7,5},{8,10},{9,11},{10,... | collective-permute-start | bytes 11528 | tf_op jit(solution)/shard_map/ppermute | solution.py:611
  221.2 20.1 %copy-start.39 = (f32[240]{0:T(256)S(1)}, f32[240]{0:T(256)}, u32[]{:S(2)}) copy-start(f32[240]{0:T(256)} %param.31) | copy-start | bytes 2884
  221.2 20.1 %copy-start.40 = (f32[240]{0:T(256)S(1)}, f32[240]{0:T(256)}, u32[]{:S(2)}) copy-start(f32[240]{0:T(256)} %param.41) | copy-start | bytes 2884
  221.2 20.1 %copy-start.41 = (f32[240]{0:T(256)S(1)}, f32[240]{0:T(256)}, u32[]{:S(2)}) copy-start(f32[240]{0:T(256)} %param.36) | copy-start | bytes 2884
  221.2 9.9 %collective-permute-start.50 = (f32[4,240]{1,0:T(4,128)S(1)}, f32[4,240]{1,0:T(4,128)S(1)}, u32[]{:S(2)}, u32[]{:S(2)}) collective-permute-start(f32[4,240]{1,0:T(4,128)S(1)} %get-tuple-element.400), channel_id=1, source_target_pairs={{0,4},{1,5},{2,6},{3,7},{4,0},{5,1},{6,2},{7,3},{8,12},{9,13},{10,... | collective-permute-start | bytes 11528 | tf_op jit(solution)/shard_map/ppermute | solution.py:611
  221.8 9.4 %collective-permute-start.51 = (f32[4,240]{1,0:T(4,128)S(1)}, f32[4,240]{1,0:T(4,128)S(1)}, u32[]{:S(2)}, u32[]{:S(2)}) collective-permute-start(f32[4,240]{1,0:T(4,128)S(1)} %get-tuple-element.401), channel_id=1, source_target_pairs={{0,6},{1,7},{2,4},{3,5},{4,2},{5,3},{6,0},{7,1},{8,14},{9,15},{10,... | collective-permute-start | bytes 11528 | tf_op jit(solution)/shard_map/ppermute | solution.py:611
  223.5 7.7 %collective-permute-start.46 = (bf16[24,2304]{1,0:T(8,128)(2,1)S(1)}, bf16[24,2304]{1,0:T(8,128)(2,1)S(1)}, u32[]{:S(2)}, u32[]{:S(2)}) collective-permute-start(bf16[24,2304]{1,0:T(8,128)(2,1)S(1)} %get-tuple-element.382), channel_id=1, source_target_pairs={{0,8},{1,9},{2,10},{3,11},{4,12},{5,13},{6,14},{7,15},{8,0},{9,1},... | collective-permute-start | bytes 331784 | tf_op jit(solution)/shard_map/ppermute | solution.py:611
  228.0 9.1 %collective-permute-start.47 = (bf16[24,2304]{1,0:T(8,128)(2,1)S(1)}, bf16[24,2304]{1,0:T(8,128)(2,1)S(1)}, u32[]{:S(2)}, u32[]{:S(2)}) collective-permute-start(bf16[24,2304]{1,0:T(8,128)(2,1)S(1)} %get-tuple-element.383), channel_id=1, source_target_pairs={{0,16},{1,17},{2,18},{3,19},{4,20},{5,21},{6,22},{7,23},{8,24},{9,... | collective-permute-start | bytes 331784 | tf_op jit(solution)/shard_map/ppermute | solution.py:611
  229.0 8.1 %collective-permute-start.48 = (bf16[24,2304]{1,0:T(8,128)(2,1)S(1)}, bf16[24,2304]{1,0:T(8,128)(2,1)S(1)}, u32[]{:S(2)}, u32[]{:S(2)}) collective-permute-start(bf16[24,2304]{1,0:T(8,128)(2,1)S(1)} %get-tuple-element.384), channel_id=1, source_target_pairs={{0,24},{1,25},{2,26},{3,27},{4,28},{5,29},{6,30},{7,31},{8,16},{9,... | collective-permute-start | bytes 331784 | tf_op jit(solution)/shard_map/ppermute | solution.py:611
  231.2 6.9 %collective-permute-start.52 = (f32[1,240]{1,0:T(1,128)S(1)}, f32[1,240]{1,0:T(1,128)S(1)}, u32[]{:S(2)}, u32[]{:S(2)}) collective-permute-start(f32[1,240]{1,0:T(1,128)S(1)} %get-tuple-element.409), channel_id=1, source_target_pairs={{0,8},{1,9},{2,10},{3,11},{4,12},{5,13},{6,14},{7,15},{8,0},{9,1},... | collective-permute-start | bytes 2888 | tf_op jit(solution)/shard_map/ppermute | solution.py:611
  233.0 5.4 %collective-permute-start.53 = (f32[1,240]{1,0:T(1,128)S(1)}, f32[1,240]{1,0:T(1,128)S(1)}, u32[]{:S(2)}, u32[]{:S(2)}) collective-permute-start(f32[1,240]{1,0:T(1,128)S(1)} %get-tuple-element.410), channel_id=1, source_target_pairs={{0,16},{1,17},{2,18},{3,19},{4,20},{5,21},{6,22},{7,23},{8,24},{9,... | collective-permute-start | bytes 2888 | tf_op jit(solution)/shard_map/ppermute | solution.py:611
  236.0 5.4 %collective-permute-start.54 = (f32[1,240]{1,0:T(1,128)S(1)}, f32[1,240]{1,0:T(1,128)S(1)}, u32[]{:S(2)}, u32[]{:S(2)}) collective-permute-start(f32[1,240]{1,0:T(1,128)S(1)} %get-tuple-element.411), channel_id=1, source_target_pairs={{0,24},{1,25},{2,26},{3,27},{4,28},{5,29},{6,30},{7,31},{8,16},{9,... | collective-permute-start | bytes 2888 | tf_op jit(solution)/shard_map/ppermute | solution.py:611
  (33 other events, 317.3 us)

commit v2 on v0

--- a/solution.py
+++ b/solution.py
@@ -299,7 +299,7 @@
     )
 
 
-def down_kernel(place, vec_ref, gl_ref, gp_ref, dy_ref, h_ref, own, other, out_ref, dur_ref, vg_ref, wd, sem):
+def fetch_down(place, own, other, wd, sem):
     def copies(b, piece, row):
         dst = pl.ds(pl.multiple_of(b * 96, 96), 96)
         return [
@@ -324,24 +324,39 @@
 
     lax.fori_loop(0, 32, begin, 0)
     lax.fori_loop(0, 32, finish, 0)
+
+
+def down_kernel(place, gp_ref, dy_ref, own, other, dur_ref, vg_ref, wd, sem):
+    fetch_down(place, own, other, wd, sem)
     for col in range(0, FF, 384):
         part = slice(col, col + 384)
         du = nt(dy_ref[...], wd[part, :]) * gp_ref[:, part].astype(WIDE)
         dur_ref[:, part] = du.astype(LOW)
         k = col // D
         vg_ref[k : k + 1, col % D : col % D + 384] = jnp.sum(du, axis=0, keepdims=True)
+
+
+def down_back(place, gp, dy, three, after=()):
+    n = dy.shape[0]
+    return whole_call(
+        down_kernel, [shape(n, FF), shape(8, D, WIDE)], [pltpu.VMEM((FF, D), LOW), pltpu.SemaphoreType.DMA], 1,
+        "down_back", 2 * n * D * (4 * D), place, gp, dy, *three, anywhere=(3, 4), after=after,
+    )
+
+
+def down_out_kernel(place, vec_ref, gl_ref, h_ref, own, other, out_ref, wd, sem):
+    fetch_down(place, own, other, wd, sem)
     for col in (0, 384):
         part = slice(col, col + 384)
         out_ref[:, part] = (h_ref[:, part] + nn(gl_ref[...], wd[:, part]) + vec_ref[9:10, part]).astype(LOW)
 
 
-def downward(place, vec, gl, gp, dy, h, three, after=()):
+def down_out(place, vec, gl, h, three, after=()):
     n = h.shape[0]
     return whole_call(
-        down_kernel, [shape(n, D), shape(n, FF), shape(8, D, WIDE)],
-        [pltpu.VMEM((FF, D), LOW), pltpu.SemaphoreType.DMA], 1, "downward",
-        2 * n * D * (8 * D), place, vec, gl, gp, dy, h, *three, anywhere=(6, 7), after=after,
-    )
+        down_out_kernel, [shape(n, D)], [pltpu.VMEM((FF, D), LOW), pltpu.SemaphoreType.DMA], 1,
+        "down_out", 2 * n * D * (4 * D), place, vec, gl, h, *three, anywhere=(4, 5), after=after,
+    )[0]
 
 
 def hidden_kernel(vec_ref, order_ref, dur_ref, dy_ref, h_ref, own, other, dh_ref, dhr_ref, dor_ref, vg_ref, tmp):
@@ -416,8 +431,24 @@
                       after=after)
 
 
-def one_grad_kernel(a_ref, *refs):
-    halves, (own, other) = refs[:6], refs[6:]
+def one_grad_kernel(a_ref, order_ref, first_ref, mid_ref, up_ref, *refs):
+    halves, (own, other, wide) = refs[:6], refs[6:]
+    wide[...] = jnp.zeros_like(wide)
+    rows = [first_ref[0:1, :], first_ref[1:2, :]] + [mid_ref[i : i + 1, :] for i in range(3)]
+    rows = rows + [up_ref[i : i + 1, :] for i in range(4)] + [mid_ref[3:4, :]]
+    for k, values in enumerate(rows):
+        first = min(D * k // 10 // 8 * 8, D - 88)
+        entry = lax.broadcasted_iota(jnp.int32, (88, D), 1) + D * k
+        row = lax.broadcasted_iota(jnp.int32, (88, D), 0) + first
+        spread_out = jnp.where(row == (entry * 52429) >> 19, values, 0.0).astype(LOW)
+        entry = lax.broadcasted_iota(jnp.int32, (D, 128), 0) + D * k
+        column = entry - 10 * ((entry * 52429) >> 19)
+        pick = (lax.broadcasted_iota(jnp.int32, (D, 128), 1) == column).astype(LOW)
+        wide[first : first + 88, :] += nn(spread_out, pick)
+    moved = tn(order_ref[...], wide[...].astype(LOW)).astype(LOW)
+    for i, out in enumerate((own, other)):
+        out[:HALF, CUT_ONE:] = moved[HALF * i : HALF * (i + 1), :]
+        out[HALF:, CUT_ONE:] = jnp.zeros((HALF, WIDTH_ONE - CUT_ONE), LOW)
     for i, half in enumerate(halves):
         t = tn(a_ref[...], half[...]).astype(LOW)
         side, lo = divmod(384 * i, CUT_ONE)
@@ -425,9 +456,12 @@
         other[HALF * side : HALF * (side + 1), lo : lo + 384] = t[HALF:]
 
 
-def one_grad(a, d, after=()):
+def one_grad(a, order, sums, d, after=()):
     n = a.shape[0]
-    return whole_call(one_grad_kernel, [shape(D, CUT_ONE)] * 2, [], 0, "one_grad", 2 * n * D * 3 * D, a, *d, after=after)
+    return whole_call(
+        one_grad_kernel, [shape(D, WIDTH_ONE)] * 2, [pltpu.VMEM((D, 128), WIDE)], 0, "one_grad",
+        2 * n * D * 3 * D, a, order, *sums, *d, after=after,
+    )
 
 
 def input_back_kernel(order_ref, q0, q1, k0, k1, v0, v1, own, other, e_ref, tmp):
@@ -619,17 +653,6 @@
     total, *out = ready = last_sum(left, right, got)
     got = yield out, (8, 16, 24), tuple(ready)
     yield None, (sum((z.astype(WIDE) for z in got), total),)
-
-
-def collect_vec(blocks):
-    half = blocks.shape[0] // 2
-    (got,) = yield (blocks[half:],), (1,)
-    blocks = blocks[:half] + got
-    rows = half // 4
-    got = yield [blocks[rows * k : rows * (k + 1)] for k in (1, 2, 3)], (2, 4, 6), (blocks,)
-    blocks = sum(got, blocks[:rows])
-    got = yield [blocks[k : k + 1] for k in (1, 2, 3)], (8, 16, 24), (blocks,)
-    yield None, (sum(got, blocks[:1]).reshape(-1),)
 
 
 def stack(whole):
@@ -686,7 +709,6 @@
     near = shards == 32
     unit = D // shards
     per_row = master_vec.shape[0] // unit
-    share = master_vec.shape[0]
     ids = jnp.arange(shards, dtype=jnp.int32)
     if near:
         away = owners ^ lax.axis_index(AXES).astype(jnp.int32)
@@ -695,7 +717,6 @@
     else:
         place = owners
         place_down = jnp.arange(32, dtype=jnp.int32)
-    inverse = jnp.sum(ids[:, None] * (place[:, None] == ids[None, :]), axis=0)
     target = (place[:, None] * unit + jnp.arange(unit, dtype=jnp.int32)[None, :]).reshape(-1)
     order = (target[:, None] == jnp.arange(D, dtype=jnp.int32)[None, :]).astype(LOW)
 
@@ -752,7 +773,7 @@
         grad_three = stack(rearrange(unstack(grad_three), back, shards))
     flow_three = scatter(grad_three)
     flow_three.issue((three[1],))
-    block_out, dur, sums_up = downward(place_down, vec, gelu, gelu_slope, dy, hidden, three)
+    dur, sums_up = down_back(place_down, gelu_slope, dy, three)
     done = flow_three.land((dur,))
     flow_three.issue(done)
     dh, dh_low, dmixed, sums = hidden_grad(vec, order, dur, dy, hidden, two, done)
@@ -765,33 +786,29 @@
     sent = flow_three.issue(done) + flow_two.issue(done)
     d1 = attend_back(3, qkv, dmixed, probs_1, spans, done + tuple(d0))
     d = [z for pair in zip(d0, d1) for z in pair]
-    grad_one = one_grad(act_one, d)
-    dact = input_back(order, d, one, tuple(grad_one))
-    done = (dact,) + tuple(grad_one) + sent
+    dact = input_back(order, d, one)
+    tokens_grad, sums_one = input_grad(x, vec, dact, dh)
+    grad_one = one_grad(act_one, order, (sums_one, sums, sums_up), d)
+    done = tuple(grad_one) + sent
     sum_three, = flow_three.land(done)
     done = flow_two.land(done)
     flow_one = scatter(grad_one)
     sent = flow_one.issue(done) + flow_two.issue(done)
-    tokens_grad, sums_one = input_grad(x, vec, dact, dh, done)
-    vector_grad = jnp.concatenate([sums_one[:2], sums[:3], sums_up[:4], sums[3:4]], axis=0)
-    blocks = jnp.take(vector_grad.reshape(shards, share), inverse, axis=0, mode="clip")
-    if near:
-        flow_vec = Flow(collect_vec(blocks))
-    else:
-        flow_vec = Whole((lax.psum_scatter(blocks.reshape(-1), AXES, scatter_dimension=0, tiled=True),))
-    done = flow_one.land((blocks,) + sent) + flow_two.land((blocks,) + sent)
-    sent = flow_one.issue(done) + flow_two.issue(done) + flow_vec.issue(done)
+    block_out = down_out(place_down, vec, gelu, hidden, three, done)
+    done = flow_one.land((block_out,) + sent) + flow_two.land((block_out,) + sent)
+    sent = flow_one.issue(done) + flow_two.issue(done)
     upd_down = adamw(master_down, first_down, second_down, sum_three, RATE_MATRIX, DECAY_MATRIX)
     sent = sent + upd_down
-    done = flow_one.land(sent) + flow_vec.land(sent)
+    done = flow_one.land(sent)
     sum_two, = flow_two.land(sent)
-    sent = flow_one.issue(done) + flow_vec.issue(done)
-    done = flow_one.land(sent) + flow_vec.land(sent)
-    sent = flow_one.issue(done) + flow_vec.issue(done)
+    flow_one.issue(done)
     upd_out = adamw(master_out, first_out, second_out, sum_two[:, :D], RATE_MATRIX, DECAY_MATRIX)
     upd_up = adamw(master_up, first_up, second_up, sum_two[:, D:], RATE_MATRIX, DECAY_MATRIX)
-    sum_one, = flow_one.land(sent + upd_out + upd_up)
-    sum_vec, = flow_vec.land(sent + upd_out + upd_up)
+    done = flow_one.land(upd_out)
+    flow_one.issue(done)
+    sum_one, = flow_one.land(upd_up)
+    sum_vec = sum_one[:, CUT_ONE : CUT_ONE + per_row].reshape(-1)
+    sum_one = jnp.concatenate([sum_one[:, :CUT_ONE], sum_one[:, WIDTH_ONE : WIDTH_ONE + CUT_ONE]], axis=1)
     upd_qkv = adamw(master_qkv, first_qkv, second_qkv, sum_one, RATE_MATRIX, DECAY_MATRIX)
     upd_vec = adamw(master_vec, first_vec, second_vec, sum_vec, RATE_VECTOR, 0.0)
     return (

time: 244 us -> 232 us (0.951)
  starting transfers between devices: 66 us -> 58.1 us
  local copies, waits for them, and re-layouts: 9.21 us -> 4.08 us
    ppermute x55 -> x48, starting transfers between devices: 66 us -> 58.1 us  [swap(): return lax.ppermute(value, AXES, pairs)]
    unnamed x84 -> x48, local copies, waits for them, and re-layouts: 5.51 us -> 3.76 us
    ppermute x55 -> x48, waiting for transfers between devices: 66.1 us -> 67.9 us  [swap(): return lax.ppermute(value, AXES, pairs)]
    pallas_call x31 -> x32, Pallas kernels: 87.3 us -> 88.5 us  [whole_call(): pl.pallas_call(later(kernel, len(args), len(after)), in_specs=specs + [pl...]
  transfers between devices with their start and end apart: 55 -> 48, of which waited for: 28 -> 23; matrix products, arithmetic and copies ran while one was open for 3% -> 2% of each run, Pallas kernels for 34% -> 38%
where the time goes in v2:
time: 232 us; the launch traced here: 229 us
  Pallas kernels  89.9 us (39%)
  waiting for transfers between devices  67.9 us (29%)
  starting transfers between devices  58.1 us (25%)
  other arithmetic  7.33 us (3%)
  local copies, waits for them, and re-layouts  4.08 us (2%)
    pallas_call x32, Pallas kernels, whole_call(): pl.pallas_call(later(kernel, len(args), len(after)), in_specs=specs + [pl...  88.5 us
    ppermute x48, waiting for transfers between devices, swap(): return lax.ppermute(value, AXES, pairs)  67.9 us
    ppermute x48, starting transfers between devices, swap(): return lax.ppermute(value, AXES, pairs)  58.1 us
  transfers between devices with their start and end apart: 48, of which 23 were waited for; matrix products, arithmetic and copies ran while one was open for 2% of the time, Pallas kernels for 38%

profile of v2, /device:TPU:0, one launch (start us, length us, event | category | flops | bytes accessed | tf_op | source)
XLA Modules:
  0.0 228.9 jit_solution(16521358142725127992)
XLA Ops:
  1.5 1.0 convert.20
  2.5 3.1 %collective-permute-start = (bf16[24,2560]{1,0:T(8,128)(2,1)S(1)}, bf16[24,2560]{1,0:T(8,128)(2,1)S(1)}, u32[]{:S(2)}, u32[]{:S(2)}) collective-permute-start(bf16[24,2560]{1,0:T(8,128)(2,1)S(1)} %fusion.8.refs_0_), channel_id=1, source_target_pairs={{0,8},{1,9},{2,10},{3,11},{4,12},{5,13},{6,14},{7,15},{8,0},{9,1},... | collective-permute-start | bytes 368648 | tf_op jit(solution)/shard_map/ppermute | solution.py:610
  5.6 2.6 %collective-permute-start.1 = (bf16[24,2560]{1,0:T(8,128)(2,1)S(1)}, bf16[24,2560]{1,0:T(8,128)(2,1)S(1)}, u32[]{:S(2)}, u32[]{:S(2)}) collective-permute-start(bf16[24,2560]{1,0:T(8,128)(2,1)S(1)} %fusion.8.refs_0_), channel_id=1, source_target_pairs={{0,16},{1,17},{2,18},{3,19},{4,20},{5,21},{6,22},{7,23},{8,24},{9,... | collective-permute-start | bytes 368648 | tf_op jit(solution)/shard_map/ppermute | solution.py:610
  11.4 1.4 tables.1
  12.8 5.2 %collective-permute-done.1.refs_2_ = bf16[24,2560]{1,0:T(8,128)(2,1)S(1)} collective-permute-done((bf16[24,2560]{1,0:T(8,128)(2,1)S(1)}, bf16[24,2560]{1,0:T(8,128)(2,1)S(1)}, u32[]{:S(2)}, u32[]{:S(2)}) %collective-permute-start.1) | collective-permute-done | bytes 122912 | tf_op jit(solution)/shard_map/ppermute | solution.py:610
  18.0 1.6 collective-permute-start.3
  19.5 1.5 collective-permute-start.4
  21.1 3.1 %collective-permute-done.3.refs_1_ = bf16[96,1280]{1,0:T(8,128)(2,1)S(1)} collective-permute-done((bf16[96,1280]{1,0:T(8,128)(2,1)S(1)}, bf16[96,1280]{1,0:T(8,128)(2,1)S(1)}, u32[]{:S(2)}, u32[]{:S(2)}) %collective-permute-start.3) | collective-permute-done | bytes 245792 | tf_op jit(solution)/shard_map/ppermute | solution.py:610
  24.3 2.4 %collective-permute-done.4.refs_3_ = bf16[96,1280]{1,0:T(8,128)(2,1)S(1)} collective-permute-done((bf16[96,1280]{1,0:T(8,128)(2,1)S(1)}, bf16[96,1280]{1,0:T(8,128)(2,1)S(1)}, u32[]{:S(2)}, u32[]{:S(2)}) %collective-permute-start.4) | collective-permute-done | bytes 245792 | tf_op jit(solution)/shard_map/ppermute | solution.py:610
  26.7 1.6 collective-permute-start.5
  29.9 2.1 collective-permute-start.8
  32.0 1.6 collective-permute-start.9
  33.6 2.7 %collective-permute-done.5.refs_1_ = bf16[192,1280]{1,0:T(8,128)(2,1)S(1)} collective-permute-done((bf16[192,1280]{1,0:T(8,128)(2,1)S(1)}, bf16[192,1280]{1,0:T(8,128)(2,1)S(1)}, u32[]{:S(2)}, u32[]{:S(2)}) %collective-permute-start.5) | collective-permute-done | bytes 491552 | tf_op jit(solution)/shard_map/ppermute | solution.py:610
  37.2 6.5 %collective-permute-done.8.refs_2_ = bf16[24,3840]{1,0:T(8,128)(2,1)S(1)} collective-permute-done((bf16[24,3840]{1,0:T(8,128)(2,1)S(1)}, bf16[24,3840]{1,0:T(8,128)(2,1)S(1)}, u32[]{:S(2)}, u32[]{:S(2)}) %collective-permute-start.8) | collective-permute-done | bytes 184352 | tf_op jit(solution)/shard_map/ppermute | solution.py:610
  43.8 1.6 collective-permute-start.11
  45.9 1.9 collective-permute-done.10.refs_3_.refs_8_
  47.8 6.2 %project.1 = (bf16[576,768]{1,0:T(8,128)(2,1)S(1)}, bf16[576,2304]{1,0:T(8,128)(2,1)S(1)}, f32[16,768]{1,0:T(8,128)S(1)}) custom-call(bf16[576,768]{1,0:T(8,128)(2,1)S(1)} %bitcast.7, bf16[768,768]{1,0:T(8,128)(2,1)S(1)} %fusion.refs_1_.refs_4_.refs_0_, bf16[768,1280]{1,0:T(8,128)(2,1)S(1)} %second.3.refs_2_.refs_7_, ...), custom_call_target="tpu_custom_call" | custom-call | flops 2717908992 | bytes 9584640 | tf_op jit(solution)/shard_map/project/pallas_call | solution.py:64
  54.8 1.2 collective-permute-done.12.refs_3_
  56.2 2.6 %collective-permute-start.15 = (bf16[96,768]{1,0:T(8,128)(2,1)S(1)}, bf16[96,768]{1,0:T(8,128)(2,1)S(1)}, u32[]{:S(2)}, u32[]{:S(2)}) collective-permute-start(bf16[96,768]{1,0:T(8,128)(2,1)S(1)} %convert_element_type.46.refs_0_), channel_id=1, source_target_pairs={{0,8},{1,9},{2,10},{3,11},{4,12},{5,13},{6,14},{7,15},{8,0},{9,1},... | collective-permute-start | bytes 442376 | tf_op jit(solution)/shard_map/ppermute | solution.py:610
  58.8 1.8 collective-permute-start.16
  60.5 1.4 collective-permute-start.17
  63.0 4.6 %attend.2 = (bf16[576,384]{1,0:T(8,128)(2,1)S(1)}, bf16[4,6,240,256]{3,2,1,0:T(8,128)(2,1)S(1)}) custom-call(s32[5,5]{1,0:T(8,128)S(1)} %get-tuple-element.197.refs_0_, f32[12]{0:T(128)S(1)} %exponential_multiply_fusion.refs_1_, bf16[576,2304]{1,0:T(8,128)(2,1)S(1)} %get-tuple-element.223.refs_2_.refs_1_, f32[4,240,256]{2,1,0:T(8,128)S(1)} %get-tuple-element.196.refs_3_, ...), custom_call_target="tpu_custom_call" | custom-call | flops 8999999488 | bytes 7028884 | tf_op jit(solution)/shard_map/attend/pallas_call | solution.py:64
  67.6 11.5 %collective-permute-done.13.refs_1_ = bf16[192,1920]{1,0:T(8,128)(2,1)S(1)} collective-permute-done((bf16[192,1920]{1,0:T(8,128)(2,1)S(1)}, bf16[192,1920]{1,0:T(8,128)(2,1)S(1)}, u32[]{:S(2)}, u32[]{:S(2)}) %collective-permute-start.13) | collective-permute-done | bytes 737312 | tf_op jit(solution)/shard_map/ppermute | solution.py:610
  80.4 1.5 collective-permute-start.20
  81.9 4.6 %attend.3 = (bf16[576,384]{1,0:T(8,128)(2,1)S(1)}, bf16[4,6,240,256]{3,2,1,0:T(8,128)(2,1)S(1)}) custom-call(s32[5,5]{1,0:T(8,128)S(1)} %get-tuple-element.197.refs_0_, f32[12]{0:T(128)S(1)} %exponential_multiply_fusion.refs_1_, bf16[576,2304]{1,0:T(8,128)(2,1)S(1)} %get-tuple-element.223.refs_2_.refs_1_, f32[4,240,256]{2,1,0:T(8,128)S(1)} %get-tuple-element.196.refs_3_, ...), custom_call_target="tpu_custom_call" | custom-call | flops 8999999488 | bytes 7028884 | tf_op jit(solution)/shard_map/attend/pallas_call | solution.py:64
  86.5 1.6 copy-done.5
  88.1 1.0 collective-permute-done.19.refs_1_
  89.6 1.6 collective-permute-start.21
  91.2 1.4 collective-permute-start.22
  92.6 8.5 %upward.1 = (bf16[576,768]{1,0:T(8,128)(2,1)S(1)}, f32[576,768]{1,0:T(8,128)S(1)}, bf16[576,768]{1,0:T(8,128)(2,1)S(1)}, bf16[576,3072]{1,0:T(8,128)(2,1)S(1)}, bf16[576,3072]{1,0:T(8,128)(2,1)S(1)}) custom-call(bf16[576,768]{1,0:T(8,128)(2,1)S(1)} %bitcast.8, bf16[576,384]{1,0:T(8,128)(2,1)S(1)} %get-tuple-element.230.refs_7_.refs_1_, ...), custom_call_target="tpu_custom_call" | custom-call | flops 9512681472 | bytes 19513344 | tf_op jit(solution)/shard_map/upward/pallas_call | solution.py:64
  101.1 7.9 %down_grad.1 = (bf16[3072,384]{1,0:T(8,128)(2,1)S(1)}, bf16[3072,384]{1,0:T(8,128)(2,1)S(1)}) custom-call(s32[32]{0:T(128)S(1)} %get-tuple-element.385.refs_0_, bf16[576,3072]{1,0:T(8,128)(2,1)S(1)} %get-tuple-element.252.refs_1_.refs_2_, bf16[576,768]{1,0:T(8,128)(2,1)S(1)} %bitcast.4), custom_call_target="tpu_custom_call" | custom-call | flops 2717908992 | bytes 9142400 | tf_op jit(solution)/shard_map/down_grad/pallas_call | solution.py:64
  109.3 4.5 %collective-permute-done.23.refs_4_.refs_5_ = bf16[3072,384]{1,0:T(8,128)(2,1)S(1)} collective-permute-done((bf16[3072,384]{1,0:T(8,128)(2,1)S(1)}, bf16[3072,384]{1,0:T(8,128)(2,1)S(1)}, u32[]{:S(2)}, u32[]{:S(2)}) %collective-permute-start.23) | collective-permute-done | bytes 2359328 | tf_op jit(solution)/shard_map/ppermute | solution.py:610
  114.0 6.2 %down_back.1 = (bf16[576,3072]{1,0:T(8,128)(2,1)S(1)}, f32[8,768]{1,0:T(8,128)S(1)}) custom-call(s32[32]{0:T(128)S(1)} %get-tuple-element.385.refs_0_, bf16[576,3072]{1,0:T(8,128)(2,1)S(1)} %get-tuple-element.263.refs_1_, bf16[576,768]{1,0:T(8,128)(2,1)S(1)} %bitcast.5, bf16[3072,384]{1,0:T(8,128)(2,1)S(1)} %second.5.refs_3_.refs_4_, ...), custom_call_target="tpu_custom_call" | custom-call | flops 2717908992 | bytes 12705920 | tf_op jit(solution)/shard_map/down_back/pallas_call | solution.py:64
  121.9 8.8 %hidden_grad.1 = (f32[576,768]{1,0:T(8,128)S(1)}, bf16[576,768]{1,0:T(8,128)(2,1)S(1)}, bf16[576,768]{1,0:T(8,128)(2,1)S(1)}, f32[8,768]{1,0:T(8,128)S(1)}) custom-call(f32[16,768]{1,0:T(8,128)S(1)} %get-tuple-element.222.refs_3_.refs_0_.refs_1_, bf16[768,768]{1,0:T(8,128)(2,1)S(1)} %fusion.refs_1_.refs_4_.refs_0_, ...), custom_call_target="tpu_custom_call" | custom-call | flops 4756340736 | bytes 16883712 | tf_op jit(solution)/shard_map/hidden_grad/pallas_call | solution.py:64
  130.8 5.8 %two_grad.1 = (bf16[768,1920]{1,0:T(8,128)(2,1)S(1)}, bf16[768,1920]{1,0:T(8,128)(2,1)S(1)}) custom-call(bf16[576,768]{1,0:T(8,128)(2,1)S(1)} %get-tuple-element.261.refs_0_, bf16[576,768]{1,0:T(8,128)(2,1)S(1)} %get-tuple-element.262.refs_1_, bf16[576,768]{1,0:T(8,128)(2,1)S(1)} %get-tuple-element.271.refs_2_, ...), custom_call_target="tpu_custom_call" | custom-call | flops 3397386240 | bytes 12091392 | tf_op jit(solution)/shard_map/two_grad/pallas_call | solution.py:64
  137.0 1.5 collective-permute-start.28
  138.5 1.5 collective-permute-start.29
  140.0 6.3 %attend_back.2 = (bf16[576,384]{1,0:T(8,128)(2,1)S(1)}, bf16[576,384]{1,0:T(8,128)(2,1)S(1)}, bf16[576,384]{1,0:T(8,128)(2,1)S(1)}) custom-call(s32[5,5]{1,0:T(8,128)S(1)} %get-tuple-element.197.refs_0_, bf16[576,2304]{1,0:T(8,128)(2,1)S(1)} %get-tuple-element.223.refs_2_.refs_1_, bf16[576,768]{1,0:T(8,128)(2,1)S(1)} %get-tuple-element.283.refs_2_, ...), custom_call_target="tpu_custom_call" | custom-call | flops 12000000000 | bytes 7815268 | tf_op jit(solution)/shard_map/attend_back/pallas_call | solution.py:64
  146.5 1.1 collective-permute-done.29.refs_3_
  148.4 1.6 collective-permute-start.30
  150.6 6.6 %attend_back.3 = (bf16[576,384]{1,0:T(8,128)(2,1)S(1)}, bf16[576,384]{1,0:T(8,128)(2,1)S(1)}, bf16[576,384]{1,0:T(8,128)(2,1)S(1)}) custom-call(s32[5,5]{1,0:T(8,128)S(1)} %get-tuple-element.197.refs_0_, bf16[576,2304]{1,0:T(8,128)(2,1)S(1)} %get-tuple-element.223.refs_2_.refs_1_, bf16[576,768]{1,0:T(8,128)(2,1)S(1)} %get-tuple-element.283.refs_2_, ...), custom_call_target="tpu_custom_call" | custom-call | flops 12000000000 | bytes 7815268 | tf_op jit(solution)/shard_map/attend_back/pallas_call | solution.py:64
  157.3 4.6 %collective-permute-start.33 = (bf16[96,768]{1,0:T(8,128)(2,1)S(1)}, bf16[96,768]{1,0:T(8,128)(2,1)S(1)}, u32[]{:S(2)}, u32[]{:S(2)}) collective-permute-start(bf16[96,768]{1,0:T(8,128)(2,1)S(1)} %get-tuple-element.315.refs_6_), channel_id=1, source_target_pairs={{0,16},{1,17},{2,18},{3,19},{4,20},{5,21},{6,22},{7,23},{8,24},{9,... | collective-permute-start | bytes 442376 | tf_op jit(solution)/shard_map/ppermute | solution.py:610
  161.9 4.5 %input_back.1.refs_2_ = f32[576,768]{1,0:T(8,128)S(1)} custom-call(bf16[768,768]{1,0:T(8,128)(2,1)S(1)} %fusion.refs_1_.refs_4_.refs_0_, bf16[576,384]{1,0:T(8,128)(2,1)S(1)} %get-tuple-element.285.refs_12_.refs_1_.refs_5_, bf16[576,384]{1,0:T(8,128)(2,1)S(1)} %get-tuple-element.305.refs_2_.refs_6_, ...), custom_call_target="tpu_custom_call" | custom-call | flops 2717908992 | bytes 9535488 | tf_op jit(solution)/shard_map/input_back/pallas_call | solution.py:64
  166.4 3.0 %input_grad.1 = (f32[576,768]{1,0:T(8,128)}, f32[8,768]{1,0:T(8,128)S(1)}) custom-call(bf16[576,768]{1,0:T(8,128)(2,1)S(1)} %bitcast.9, f32[16,768]{1,0:T(8,128)S(1)} %get-tuple-element.222.refs_3_.refs_0_.refs_1_, f32[576,768]{1,0:T(8,128)S(1)} %input_back.1.refs_2_, f32[576,768]{1,0:T(8,128)S(1)} %get-tuple-element.308.refs_3_), custom_call_target="tpu_custom_call" | custom-call | flops 2038431744 | bytes 6266880 | tf_op jit(solution)/shard_map/input_grad/pallas_call | solution.py:64
  169.4 5.0 %one_grad.1 = (bf16[768,1280]{1,0:T(8,128)(2,1)S(1)}, bf16[768,1280]{1,0:T(8,128)(2,1)S(1)}) custom-call(bf16[576,768]{1,0:T(8,128)(2,1)S(1)} %get-tuple-element.303.refs_0_, bf16[768,768]{1,0:T(8,128)(2,1)S(1)} %fusion.refs_1_.refs_4_.refs_0_, f32[8,768]{1,0:T(8,128)S(1)} %get-tuple-element.309.refs_2_, f32[8,768]{1,0:T(8,128)S(1)} %get-tuple-element.310.refs_3_, ...), custom_call_target="tpu_custom_call" | custom-call | flops 2038431744 | bytes 8724480 | tf_op jit(solution)/shard_map/one_grad/pallas_call | solution.py:64
  174.8 1.2 collective-permute-start.36
  176.0 1.2 collective-permute-start.37
  177.2 6.8 %down_out.1 = bf16[576,768]{1,0:T(8,128)(2,1)} custom-call(s32[32]{0:T(128)S(1)} %get-tuple-element.385.refs_0_, f32[16,768]{1,0:T(8,128)S(1)} %get-tuple-element.222.refs_3_.refs_0_.refs_1_, bf16[576,3072]{1,0:T(8,128)(2,1)S(1)} %get-tuple-element.252.refs_1_.refs_2_, f32[576,768]{1,0:T(8,128)S(1)} %get-tuple-element.253.refs_4_.refs_3_, ...), custom_call_target="tpu_custom_call" | custom-call | flops 2717908992 | bytes 10961024 | tf_op jit(solution)/shard_map/down_out/pallas_call | solution.py:64
  184.0 1.7 collective-permute-done.36.refs_1_
  187.3 1.3 collective-permute-start.38
  188.5 1.5 collective-permute-start.39
  190.1 3.1 %collective-permute-start.41 = (bf16[24,3840]{1,0:T(8,128)(2,1)S(1)}, bf16[24,3840]{1,0:T(8,128)(2,1)S(1)}, u32[]{:S(2)}, u32[]{:S(2)}) collective-permute-start(bf16[24,3840]{1,0:T(8,128)(2,1)S(1)} %get-tuple-element.341), channel_id=1, source_target_pairs={{0,16},{1,17},{2,18},{3,19},{4,20},{5,21},{6,22},{7,23},{8,24},{9,... | collective-permute-start | bytes 552968 | tf_op jit(solution)/shard_map/ppermute | solution.py:610
  193.2 1.3 collective-permute-start.42
  194.5 1.1 multiply_subtract_fusion.1
  195.6 2.7 %collective-permute-done.40 = bf16[24,3840]{1,0:T(8,128)(2,1)S(1)} collective-permute-done((bf16[24,3840]{1,0:T(8,128)(2,1)S(1)}, bf16[24,3840]{1,0:T(8,128)(2,1)S(1)}, u32[]{:S(2)}, u32[]{:S(2)}) %collective-permute-start.40) | collective-permute-done | bytes 184352 | tf_op jit(solution)/shard_map/ppermute | solution.py:610
  198.3 8.4 %collective-permute-done.41 = bf16[24,3840]{1,0:T(8,128)(2,1)S(1)} collective-permute-done((bf16[24,3840]{1,0:T(8,128)(2,1)S(1)}, bf16[24,3840]{1,0:T(8,128)(2,1)S(1)}, u32[]{:S(2)}, u32[]{:S(2)}) %collective-permute-start.41) | collective-permute-done | bytes 184352 | tf_op jit(solution)/shard_map/ppermute | solution.py:610
  206.9 1.6 collective-permute-start.43
  209.8 3.3 %collective-permute-done.43.refs_1_ = bf16[96,1280]{1,0:T(8,128)(2,1)S(1)} collective-permute-done((bf16[96,1280]{1,0:T(8,128)(2,1)S(1)}, bf16[96,1280]{1,0:T(8,128)(2,1)S(1)}, u32[]{:S(2)}, u32[]{:S(2)}) %collective-permute-start.43) | collective-permute-done | bytes 245792 | tf_op jit(solution)/shard_map/ppermute | solution.py:610
  213.2 1.5 collective-permute-done.44.refs_3_
  214.8 2.6 %collective-permute-start.45 = (bf16[24,2560]{1,0:T(8,128)(2,1)S(1)}, bf16[24,2560]{1,0:T(8,128)(2,1)S(1)}, u32[]{:S(2)}, u32[]{:S(2)}) collective-permute-start(bf16[24,2560]{1,0:T(8,128)(2,1)S(1)} %get-tuple-element.363), channel_id=1, source_target_pairs={{0,8},{1,9},{2,10},{3,11},{4,12},{5,13},{6,14},{7,15},{8,0},{9,1},... | collective-permute-start | bytes 368648 | tf_op jit(solution)/shard_map/ppermute | solution.py:610
  217.4 1.0 collective-permute-start.46
  218.4 1.5 collective-permute-start.47
  219.8 1.1 multiply_subtract_fusion
  220.9 5.9 %collective-permute-done.46 = bf16[24,2560]{1,0:T(8,128)(2,1)S(1)} collective-permute-done((bf16[24,2560]{1,0:T(8,128)(2,1)S(1)}, bf16[24,2560]{1,0:T(8,128)(2,1)S(1)}, u32[]{:S(2)}, u32[]{:S(2)}) %collective-permute-start.46) | collective-permute-done | bytes 122912 | tf_op jit(solution)/shard_map/ppermute | solution.py:610
  (139 shorter events, 20.4 us)
Async XLA Ops:
  0.7 20.4 %copy-start.14 = (f32[24,768]{1,0:T(8,128)S(1)}, f32[24,768]{1,0:T(8,128)}, u32[]{:S(2)}) copy-start(f32[24,768]{1,0:T(8,128)} %param.28) | copy-start | bytes 221188
  0.7 20.4 %copy-start.10 = (f32[24,3072]{1,0:T(8,128)S(1)}, f32[24,3072]{1,0:T(8,128)}, u32[]{:S(2)}) copy-start(f32[24,3072]{1,0:T(8,128)} %param.29) | copy-start | bytes 884740
  2.5 10.2 %collective-permute-start = (bf16[24,2560]{1,0:T(8,128)(2,1)S(1)}, bf16[24,2560]{1,0:T(8,128)(2,1)S(1)}, u32[]{:S(2)}, u32[]{:S(2)}) collective-permute-start(bf16[24,2560]{1,0:T(8,128)(2,1)S(1)} %fusion.8.refs_0_), channel_id=1, source_target_pairs={{0,8},{1,9},{2,10},{3,11},{4,12},{5,13},{6,14},{7,15},{8,0},{9,1},... | collective-permute-start | bytes 368648 | tf_op jit(solution)/shard_map/ppermute | solution.py:610
  5.6 12.3 %collective-permute-start.1 = (bf16[24,2560]{1,0:T(8,128)(2,1)S(1)}, bf16[24,2560]{1,0:T(8,128)(2,1)S(1)}, u32[]{:S(2)}, u32[]{:S(2)}) collective-permute-start(bf16[24,2560]{1,0:T(8,128)(2,1)S(1)} %fusion.8.refs_0_), channel_id=1, source_target_pairs={{0,16},{1,17},{2,18},{3,19},{4,20},{5,21},{6,22},{7,23},{8,24},{9,... | collective-permute-start | bytes 368648 | tf_op jit(solution)/shard_map/ppermute | solution.py:610
  8.2 9.7 %collective-permute-start.2 = (bf16[24,2560]{1,0:T(8,128)(2,1)S(1)}, bf16[24,2560]{1,0:T(8,128)(2,1)S(1)}, u32[]{:S(2)}, u32[]{:S(2)}) collective-permute-start(bf16[24,2560]{1,0:T(8,128)(2,1)S(1)} %fusion.8.refs_0_), channel_id=1, source_target_pairs={{0,24},{1,25},{2,26},{3,27},{4,28},{5,29},{6,30},{7,31},{8,16},{9,... | collective-permute-start | bytes 368648 | tf_op jit(solution)/shard_map/ppermute | solution.py:610
  18.0 6.3 %collective-permute-start.3 = (bf16[96,1280]{1,0:T(8,128)(2,1)S(1)}, bf16[96,1280]{1,0:T(8,128)(2,1)S(1)}, u32[]{:S(2)}, u32[]{:S(2)}) collective-permute-start(bf16[96,1280]{1,0:T(8,128)(2,1)S(1)} %get-tuple-element.203.refs_0_), channel_id=1, source_target_pairs={{0,2},{1,3},{2,0},{3,1},{4,6},{5,7},{6,4},{7,5},{8,10},{9,11},{10,... | collective-permute-start | bytes 737288 | tf_op jit(solution)/shard_map/ppermute | solution.py:610
  19.5 7.1 %collective-permute-start.4 = (bf16[96,1280]{1,0:T(8,128)(2,1)S(1)}, bf16[96,1280]{1,0:T(8,128)(2,1)S(1)}, u32[]{:S(2)}, u32[]{:S(2)}) collective-permute-start(bf16[96,1280]{1,0:T(8,128)(2,1)S(1)} %get-tuple-element.204.refs_2_), channel_id=1, source_target_pairs={{0,4},{1,5},{2,6},{3,7},{4,0},{5,1},{6,2},{7,3},{8,12},{9,13},{10,... | collective-permute-start | bytes 737288 | tf_op jit(solution)/shard_map/ppermute | solution.py:610
  26.7 9.6 %collective-permute-start.5 = (bf16[192,1280]{1,0:T(8,128)(2,1)S(1)}, bf16[192,1280]{1,0:T(8,128)(2,1)S(1)}, u32[]{:S(2)}, u32[]{:S(2)}) collective-permute-start(bf16[192,1280]{1,0:T(8,128)(2,1)S(1)} %get-tuple-element.209.refs_0_), channel_id=1, source_target_pairs={{0,4},{1,5},{2,6},{3,7},{4,0},{5,1},{6,2},{7,3},{8,12},{9,13},{10,... | collective-permute-start | bytes 1474568 | tf_op jit(solution)/shard_map/ppermute | solution.py:610
  28.3 8.8 %collective-permute-start.6 = (bf16[192,1280]{1,0:T(8,128)(2,1)S(1)}, bf16[192,1280]{1,0:T(8,128)(2,1)S(1)}, u32[]{:S(2)}, u32[]{:S(2)}) collective-permute-start(bf16[192,1280]{1,0:T(8,128)(2,1)S(1)} %get-tuple-element.210.refs_2_), channel_id=1, source_target_pairs={{0,2},{1,3},{2,0},{3,1},{4,6},{5,7},{6,4},{7,5},{8,10},{9,11},{10,... | collective-permute-start | bytes 1474568 | tf_op jit(solution)/shard_map/ppermute | solution.py:610
  29.1 16.8 %copy-start.9 = (f32[96,768]{1,0:T(8,128)S(1)}, f32[96,768]{1,0:T(8,128)}, u32[]{:S(2)}) copy-start(f32[96,768]{1,0:T(8,128)} %param.30) | copy-start | bytes 884740
  29.1 18.7 %copy-start.4 = (bf16[1,576,768]{2,1,0:T(8,128)(2,1)S(1)}, bf16[1,576,768]{2,1,0:T(8,128)(2,1)}, u32[]{:S(2)}) copy-start(bf16[1,576,768]{2,1,0:T(8,128)(2,1)} %param.21) | copy-start | bytes 2654212
  29.1 8.1 %collective-permute-start.7 = (bf16[24,3840]{1,0:T(8,128)(2,1)S(1)}, bf16[24,3840]{1,0:T(8,128)(2,1)S(1)}, u32[]{:S(2)}, u32[]{:S(2)}) collective-permute-start(bf16[24,3840]{1,0:T(8,128)(2,1)S(1)} %pad_maximum_fusion.1.refs_0_), channel_id=1, source_target_pairs={{0,8},{1,9},{2,10},{3,11},{4,12},{5,13},{6,14},{7,15},{8,0},{9,1},... | collective-permute-start | bytes 552968 | tf_op jit(solution)/shard_map/ppermute | solution.py:610
  29.9 13.8 %collective-permute-start.8 = (bf16[24,3840]{1,0:T(8,128)(2,1)S(1)}, bf16[24,3840]{1,0:T(8,128)(2,1)S(1)}, u32[]{:S(2)}, u32[]{:S(2)}) collective-permute-start(bf16[24,3840]{1,0:T(8,128)(2,1)S(1)} %pad_maximum_fusion.1.refs_0_), channel_id=1, source_target_pairs={{0,16},{1,17},{2,18},{3,19},{4,20},{5,21},{6,22},{7,23},{8,24},{9,... | collective-permute-start | bytes 552968 | tf_op jit(solution)/shard_map/ppermute | solution.py:610
  32.0 11.7 %collective-permute-start.9 = (bf16[24,3840]{1,0:T(8,128)(2,1)S(1)}, bf16[24,3840]{1,0:T(8,128)(2,1)S(1)}, u32[]{:S(2)}, u32[]{:S(2)}) collective-permute-start(bf16[24,3840]{1,0:T(8,128)(2,1)S(1)} %pad_maximum_fusion.1.refs_0_), channel_id=1, source_target_pairs={{0,24},{1,25},{2,26},{3,27},{4,28},{5,29},{6,30},{7,31},{8,16},{9,... | collective-permute-start | bytes 552968 | tf_op jit(solution)/shard_map/ppermute | solution.py:610
  43.8 4.0 %collective-permute-start.10 = (bf16[768,1280]{1,0:T(8,128)(2,1)S(1)}, bf16[768,1280]{1,0:T(8,128)(2,1)S(1)}, u32[]{:S(2)}, u32[]{:S(2)}) collective-permute-start(bf16[768,1280]{1,0:T(8,128)(2,1)S(1)} %second.3.refs_2_.refs_7_), channel_id=1, source_target_pairs={{0,1},{1,0},{2,3},{3,2},{4,5},{5,4},{6,7},{7,6},{8,9},{9,8},{10,11... | collective-permute-start | bytes 5898248 | tf_op jit(solution)/shard_map/ppermute | solution.py:610
  43.8 11.0 %collective-permute-start.11 = (bf16[96,1920]{1,0:T(8,128)(2,1)S(1)}, bf16[96,1920]{1,0:T(8,128)(2,1)S(1)}, u32[]{:S(2)}, u32[]{:S(2)}) collective-permute-start(bf16[96,1920]{1,0:T(8,128)(2,1)S(1)} %get-tuple-element.224.refs_0_), channel_id=1, source_target_pairs={{0,2},{1,3},{2,0},{3,1},{4,6},{5,7},{6,4},{7,5},{8,10},{9,11},{10,... | collective-permute-start | bytes 1105928 | tf_op jit(solution)/shard_map/ppermute | solution.py:610
  45.4 10.7 %collective-permute-start.12 = (bf16[96,1920]{1,0:T(8,128)(2,1)S(1)}, bf16[96,1920]{1,0:T(8,128)(2,1)S(1)}, u32[]{:S(2)}, u32[]{:S(2)}) collective-permute-start(bf16[96,1920]{1,0:T(8,128)(2,1)S(1)} %get-tuple-element.225.refs_2_), channel_id=1, source_target_pairs={{0,4},{1,5},{2,6},{3,7},{4,0},{5,1},{6,2},{7,3},{8,12},{9,13},{10,... | collective-permute-start | bytes 1105928 | tf_op jit(solution)/shard_map/ppermute | solution.py:610
  56.2 23.4 %collective-permute-start.15 = (bf16[96,768]{1,0:T(8,128)(2,1)S(1)}, bf16[96,768]{1,0:T(8,128)(2,1)S(1)}, u32[]{:S(2)}, u32[]{:S(2)}) collective-permute-start(bf16[96,768]{1,0:T(8,128)(2,1)S(1)} %convert_element_type.46.refs_0_), channel_id=1, source_target_pairs={{0,8},{1,9},{2,10},{3,11},{4,12},{5,13},{6,14},{7,15},{8,0},{9,1},... | collective-permute-start | bytes 442376 | tf_op jit(solution)/shard_map/ppermute | solution.py:610
  58.8 20.8 %collective-permute-start.16 = (bf16[96,768]{1,0:T(8,128)(2,1)S(1)}, bf16[96,768]{1,0:T(8,128)(2,1)S(1)}, u32[]{:S(2)}, u32[]{:S(2)}) collective-permute-start(bf16[96,768]{1,0:T(8,128)(2,1)S(1)} %convert_element_type.46.refs_0_), channel_id=1, source_target_pairs={{0,16},{1,17},{2,18},{3,19},{4,20},{5,21},{6,22},{7,23},{8,24},{9,... | collective-permute-start | bytes 442376 | tf_op jit(solution)/shard_map/ppermute | solution.py:610
  60.5 19.0 %collective-permute-start.17 = (bf16[96,768]{1,0:T(8,128)(2,1)S(1)}, bf16[96,768]{1,0:T(8,128)(2,1)S(1)}, u32[]{:S(2)}, u32[]{:S(2)}) collective-permute-start(bf16[96,768]{1,0:T(8,128)(2,1)S(1)} %convert_element_type.46.refs_0_), channel_id=1, source_target_pairs={{0,24},{1,25},{2,26},{3,27},{4,28},{5,29},{6,30},{7,31},{8,16},{9,... | collective-permute-start | bytes 442376 | tf_op jit(solution)/shard_map/ppermute | solution.py:610
  61.9 17.2 %collective-permute-start.13 = (bf16[192,1920]{1,0:T(8,128)(2,1)S(1)}, bf16[192,1920]{1,0:T(8,128)(2,1)S(1)}, u32[]{:S(2)}, u32[]{:S(2)}) collective-permute-start(bf16[192,1920]{1,0:T(8,128)(2,1)S(1)} %get-tuple-element.231.refs_4_.refs_0_), channel_id=1, source_target_pairs={{0,4},{1,5},{2,6},{3,7},{4,0},{5,1},{6,2},{7,3},{8,12},{9,13},{10,... | collective-permute-start | bytes 2211848 | tf_op jit(solution)/shard_map/ppermute | solution.py:610
  62.4 16.9 %collective-permute-start.14 = (bf16[192,1920]{1,0:T(8,128)(2,1)S(1)}, bf16[192,1920]{1,0:T(8,128)(2,1)S(1)}, u32[]{:S(2)}, u32[]{:S(2)}) collective-permute-start(bf16[192,1920]{1,0:T(8,128)(2,1)S(1)} %get-tuple-element.232.refs_5_.refs_2_), channel_id=1, source_target_pairs={{0,2},{1,3},{2,0},{3,1},{4,6},{5,7},{6,4},{7,5},{8,10},{9,11},{10,... | collective-permute-start | bytes 2211848 | tf_op jit(solution)/shard_map/ppermute | solution.py:610
  67.6 11.9 %copy-start.7 = (bf16[4,6,240,256]{3,2,1,0:T(8,128)(2,1)}, bf16[4,6,240,256]{3,2,1,0:T(8,128)(2,1)S(1)}, u32[]{:S(2)}) copy-start(bf16[4,6,240,256]{3,2,1,0:T(8,128)(2,1)S(1)} %get-tuple-element.284.refs_3_) | copy-start | bytes 8847364
  79.6 9.8 %collective-permute-start.18 = (bf16[768,1920]{1,0:T(8,128)(2,1)S(1)}, bf16[768,1920]{1,0:T(8,128)(2,1)S(1)}, u32[]{:S(2)}, u32[]{:S(2)}) collective-permute-start(bf16[768,1920]{1,0:T(8,128)(2,1)S(1)} %second.4.refs_4_.refs_5_), channel_id=1, source_target_pairs={{0,1},{1,0},{2,3},{3,2},{4,5},{5,4},{6,7},{7,6},{8,9},{9,8},{10,11... | collective-permute-start | bytes 8847368 | tf_op jit(solution)/shard_map/ppermute | solution.py:610
  79.7 9.4 %collective-permute-start.19 = (bf16[384,384]{1,0:T(8,128)(2,1)S(1)}, bf16[384,384]{1,0:T(8,128)(2,1)S(1)}, u32[]{:S(2)}, u32[]{:S(2)}) collective-permute-start(bf16[384,384]{1,0:T(8,128)(2,1)S(1)} %get-tuple-element.245.refs_5_.refs_0_), channel_id=1, source_target_pairs={{0,2},{1,3},{2,0},{3,1},{4,6},{5,7},{6,4},{7,5},{8,10},{9,11},{10,... | collective-permute-start | bytes 884744 | tf_op jit(solution)/shard_map/ppermute | solution.py:610
  80.4 9.1 %collective-permute-start.20 = (bf16[384,384]{1,0:T(8,128)(2,1)S(1)}, bf16[384,384]{1,0:T(8,128)(2,1)S(1)}, u32[]{:S(2)}, u32[]{:S(2)}) collective-permute-start(bf16[384,384]{1,0:T(8,128)(2,1)S(1)} %get-tuple-element.246.refs_6_.refs_2_), channel_id=1, source_target_pairs={{0,4},{1,5},{2,6},{3,7},{4,0},{5,1},{6,2},{7,3},{8,12},{9,13},{10,... | collective-permute-start | bytes 884744 | tf_op jit(solution)/shard_map/ppermute | solution.py:610
  89.6 19.4 %collective-permute-start.21 = (bf16[768,384]{1,0:T(8,128)(2,1)S(1)}, bf16[768,384]{1,0:T(8,128)(2,1)S(1)}, u32[]{:S(2)}, u32[]{:S(2)}) collective-permute-start(bf16[768,384]{1,0:T(8,128)(2,1)S(1)} %get-tuple-element.254.refs_7_.refs_0_), channel_id=1, source_target_pairs={{0,4},{1,5},{2,6},{3,7},{4,0},{5,1},{6,2},{7,3},{8,12},{9,13},{10,... | collective-permute-start | bytes 1769480 | tf_op jit(solution)/shard_map/ppermute | solution.py:610
  91.2 17.8 %collective-permute-start.22 = (bf16[768,384]{1,0:T(8,128)(2,1)S(1)}, bf16[768,384]{1,0:T(8,128)(2,1)S(1)}, u32[]{:S(2)}, u32[]{:S(2)}) collective-permute-start(bf16[768,384]{1,0:T(8,128)(2,1)S(1)} %get-tuple-element.255.refs_8_.refs_2_), channel_id=1, source_target_pairs={{0,2},{1,3},{2,0},{3,1},{4,6},{5,7},{6,4},{7,5},{8,10},{9,11},{10,... | collective-permute-start | bytes 1769480 | tf_op jit(solution)/shard_map/ppermute | solution.py:610
  109.2 4.6 %collective-permute-start.23 = (bf16[3072,384]{1,0:T(8,128)(2,1)S(1)}, bf16[3072,384]{1,0:T(8,128)(2,1)S(1)}, u32[]{:S(2)}, u32[]{:S(2)}) collective-permute-start(bf16[3072,384]{1,0:T(8,128)(2,1)S(1)} %second.5.refs_3_.refs_4_), channel_id=1, source_target_pairs={{0,1},{1,0},{2,3},{3,2},{4,5},{5,4},{6,7},{7,6},{8,9},{9,8},{10,11... | collective-permute-start | bytes 7077896 | tf_op jit(solution)/shard_map/ppermute | solution.py:610
  113.8 6.4 %collective-permute-start.24 = (bf16[3072,384]{1,0:T(8,128)(2,1)S(1)}, bf16[3072,384]{1,0:T(8,128)(2,1)S(1)}, u32[]{:S(2)}, u32[]{:S(2)}) collective-permute-start(bf16[3072,384]{1,0:T(8,128)(2,1)S(1)} %get-tuple-element.265), channel_id=1, source_target_pairs={{0,1},{1,0},{2,3},{3,2},{4,5},{5,4},{6,7},{7,6},{8,9},{9,8},{10,11... | collective-permute-start | bytes 7077896 | tf_op jit(solution)/shard_map/ppermute | solution.py:610
  120.7 15.9 %collective-permute-start.25 = (bf16[768,384]{1,0:T(8,128)(2,1)S(1)}, bf16[768,384]{1,0:T(8,128)(2,1)S(1)}, u32[]{:S(2)}, u32[]{:S(2)}) collective-permute-start(bf16[768,384]{1,0:T(8,128)(2,1)S(1)} %get-tuple-element.274.refs_9_), channel_id=1, source_target_pairs={{0,4},{1,5},{2,6},{3,7},{4,0},{5,1},{6,2},{7,3},{8,12},{9,13},{10,... | collective-permute-start | bytes 1769480 | tf_op jit(solution)/shard_map/ppermute | solution.py:610
  121.3 15.3 %collective-permute-start.26 = (bf16[768,384]{1,0:T(8,128)(2,1)S(1)}, bf16[768,384]{1,0:T(8,128)(2,1)S(1)}, u32[]{:S(2)}, u32[]{:S(2)}) collective-permute-start(bf16[768,384]{1,0:T(8,128)(2,1)S(1)} %get-tuple-element.275.refs_10_), channel_id=1, source_target_pairs={{0,2},{1,3},{2,0},{3,1},{4,6},{5,7},{6,4},{7,5},{8,10},{9,11},{10,... | collective-permute-start | bytes 1769480 | tf_op jit(solution)/shard_map/ppermute | solution.py:610
  137.0 10.6 %collective-permute-start.27 = (bf16[768,1920]{1,0:T(8,128)(2,1)S(1)}, bf16[768,1920]{1,0:T(8,128)(2,1)S(1)}, u32[]{:S(2)}, u32[]{:S(2)}) collective-permute-start(bf16[768,1920]{1,0:T(8,128)(2,1)S(1)} %get-tuple-element.282.refs_9_), channel_id=1, source_target_pairs={{0,1},{1,0},{2,3},{3,2},{4,5},{5,4},{6,7},{7,6},{8,9},{9,8},{10,11... | collective-permute-start | bytes 8847368 | tf_op jit(solution)/shard_map/ppermute | solution.py:610
  137.0 9.4 %collective-permute-start.28 = (bf16[384,384]{1,0:T(8,128)(2,1)S(1)}, bf16[384,384]{1,0:T(8,128)(2,1)S(1)}, u32[]{:S(2)}, u32[]{:S(2)}) collective-permute-start(bf16[384,384]{1,0:T(8,128)(2,1)S(1)} %get-tuple-element.288.refs_6_), channel_id=1, source_target_pairs={{0,2},{1,3},{2,0},{3,1},{4,6},{5,7},{6,4},{7,5},{8,10},{9,11},{10,... | collective-permute-start | bytes 884744 | tf_op jit(solution)/shard_map/ppermute | solution.py:610
  138.5 9.1 %collective-permute-start.29 = (bf16[384,384]{1,0:T(8,128)(2,1)S(1)}, bf16[384,384]{1,0:T(8,128)(2,1)S(1)}, u32[]{:S(2)}, u32[]{:S(2)}) collective-permute-start(bf16[384,384]{1,0:T(8,128)(2,1)S(1)} %get-tuple-element.289.refs_7_), channel_id=1, source_target_pairs={{0,4},{1,5},{2,6},{3,7},{4,0},{5,1},{6,2},{7,3},{8,12},{9,13},{10,... | collective-permute-start | bytes 884744 | tf_op jit(solution)/shard_map/ppermute | solution.py:610
  148.4 26.0 %collective-permute-start.30 = (bf16[192,1920]{1,0:T(8,128)(2,1)S(1)}, bf16[192,1920]{1,0:T(8,128)(2,1)S(1)}, u32[]{:S(2)}, u32[]{:S(2)}) collective-permute-start(bf16[192,1920]{1,0:T(8,128)(2,1)S(1)} %get-tuple-element.301.refs_10_), channel_id=1, source_target_pairs={{0,4},{1,5},{2,6},{3,7},{4,0},{5,1},{6,2},{7,3},{8,12},{9,13},{10,... | collective-permute-start | bytes 2211848 | tf_op jit(solution)/shard_map/ppermute | solution.py:610
  150.0 24.4 %collective-permute-start.31 = (bf16[192,1920]{1,0:T(8,128)(2,1)S(1)}, bf16[192,1920]{1,0:T(8,128)(2,1)S(1)}, u32[]{:S(2)}, u32[]{:S(2)}) collective-permute-start(bf16[192,1920]{1,0:T(8,128)(2,1)S(1)} %get-tuple-element.302.refs_11_), channel_id=1, source_target_pairs={{0,2},{1,3},{2,0},{3,1},{4,6},{5,7},{6,4},{7,5},{8,10},{9,11},{10,... | collective-permute-start | bytes 2211848 | tf_op jit(solution)/shard_map/ppermute | solution.py:610
  157.2 17.2 %collective-permute-start.32 = (bf16[96,768]{1,0:T(8,128)(2,1)S(1)}, bf16[96,768]{1,0:T(8,128)(2,1)S(1)}, u32[]{:S(2)}, u32[]{:S(2)}) collective-permute-start(bf16[96,768]{1,0:T(8,128)(2,1)S(1)} %get-tuple-element.314.refs_5_), channel_id=1, source_target_pairs={{0,8},{1,9},{2,10},{3,11},{4,12},{5,13},{6,14},{7,15},{8,0},{9,1},... | collective-permute-start | bytes 442376 | tf_op jit(solution)/shard_map/ppermute | solution.py:610
  157.3 17.1 %collective-permute-start.33 = (bf16[96,768]{1,0:T(8,128)(2,1)S(1)}, bf16[96,768]{1,0:T(8,128)(2,1)S(1)}, u32[]{:S(2)}, u32[]{:S(2)}) collective-permute-start(bf16[96,768]{1,0:T(8,128)(2,1)S(1)} %get-tuple-element.315.refs_6_), channel_id=1, source_target_pairs={{0,16},{1,17},{2,18},{3,19},{4,20},{5,21},{6,22},{7,23},{8,24},{9,... | collective-permute-start | bytes 442376 | tf_op jit(solution)/shard_map/ppermute | solution.py:610
  161.9 12.5 %collective-permute-start.34 = (bf16[96,768]{1,0:T(8,128)(2,1)S(1)}, bf16[96,768]{1,0:T(8,128)(2,1)S(1)}, u32[]{:S(2)}, u32[]{:S(2)}) collective-permute-start(bf16[96,768]{1,0:T(8,128)(2,1)S(1)} %get-tuple-element.316.refs_7_), channel_id=1, source_target_pairs={{0,24},{1,25},{2,26},{3,27},{4,28},{5,29},{6,30},{7,31},{8,16},{9,... | collective-permute-start | bytes 442376 | tf_op jit(solution)/shard_map/ppermute | solution.py:610
  174.7 12.0 %collective-permute-start.35 = (bf16[768,1280]{1,0:T(8,128)(2,1)S(1)}, bf16[768,1280]{1,0:T(8,128)(2,1)S(1)}, u32[]{:S(2)}, u32[]{:S(2)}) collective-permute-start(bf16[768,1280]{1,0:T(8,128)(2,1)S(1)} %get-tuple-element.324), channel_id=1, source_target_pairs={{0,1},{1,0},{2,3},{3,2},{4,5},{5,4},{6,7},{7,6},{8,9},{9,8},{10,11... | collective-permute-start | bytes 5898248 | tf_op jit(solution)/shard_map/ppermute | solution.py:610
  174.8 11.0 %collective-permute-start.36 = (bf16[96,1920]{1,0:T(8,128)(2,1)S(1)}, bf16[96,1920]{1,0:T(8,128)(2,1)S(1)}, u32[]{:S(2)}, u32[]{:S(2)}) collective-permute-start(bf16[96,1920]{1,0:T(8,128)(2,1)S(1)} %get-tuple-element.325.refs_8_), channel_id=1, source_target_pairs={{0,2},{1,3},{2,0},{3,1},{4,6},{5,7},{6,4},{7,5},{8,10},{9,11},{10,... | collective-permute-start | bytes 1105928 | tf_op jit(solution)/shard_map/ppermute | solution.py:610
  176.0 10.7 %collective-permute-start.37 = (bf16[96,1920]{1,0:T(8,128)(2,1)S(1)}, bf16[96,1920]{1,0:T(8,128)(2,1)S(1)}, u32[]{:S(2)}, u32[]{:S(2)}) collective-permute-start(bf16[96,1920]{1,0:T(8,128)(2,1)S(1)} %get-tuple-element.326.refs_9_), channel_id=1, source_target_pairs={{0,4},{1,5},{2,6},{3,7},{4,0},{5,1},{6,2},{7,3},{8,12},{9,13},{10,... | collective-permute-start | bytes 1105928 | tf_op jit(solution)/shard_map/ppermute | solution.py:610
  184.0 10.4 %copy-start.12 = (f32[96,768]{1,0:T(8,128)S(1)}, f32[96,768]{1,0:T(8,128)}, u32[]{:S(2)}) copy-start(f32[96,768]{1,0:T(8,128)} %param.40) | copy-start | bytes 884740
  187.3 19.4 %collective-permute-start.38 = (bf16[192,1280]{1,0:T(8,128)(2,1)S(1)}, bf16[192,1280]{1,0:T(8,128)(2,1)S(1)}, u32[]{:S(2)}, u32[]{:S(2)}) collective-permute-start(bf16[192,1280]{1,0:T(8,128)(2,1)S(1)} %get-tuple-element.338), channel_id=1, source_target_pairs={{0,4},{1,5},{2,6},{3,7},{4,0},{5,1},{6,2},{7,3},{8,12},{9,13},{10,... | collective-permute-start | bytes 1474568 | tf_op jit(solution)/shard_map/ppermute | solution.py:610
  188.5 18.1 %collective-permute-start.39 = (bf16[192,1280]{1,0:T(8,128)(2,1)S(1)}, bf16[192,1280]{1,0:T(8,128)(2,1)S(1)}, u32[]{:S(2)}, u32[]{:S(2)}) collective-permute-start(bf16[192,1280]{1,0:T(8,128)(2,1)S(1)} %get-tuple-element.339), channel_id=1, source_target_pairs={{0,2},{1,3},{2,0},{3,1},{4,6},{5,7},{6,4},{7,5},{8,10},{9,11},{10,... | collective-permute-start | bytes 1474568 | tf_op jit(solution)/shard_map/ppermute | solution.py:610
  190.1 8.2 %collective-permute-start.40 = (bf16[24,3840]{1,0:T(8,128)(2,1)S(1)}, bf16[24,3840]{1,0:T(8,128)(2,1)S(1)}, u32[]{:S(2)}, u32[]{:S(2)}) collective-permute-start(bf16[24,3840]{1,0:T(8,128)(2,1)S(1)} %get-tuple-element.340), channel_id=1, source_target_pairs={{0,8},{1,9},{2,10},{3,11},{4,12},{5,13},{6,14},{7,15},{8,0},{9,1},... | collective-permute-start | bytes 552968 | tf_op jit(solution)/shard_map/ppermute | solution.py:610
  190.1 16.6 %collective-permute-start.41 = (bf16[24,3840]{1,0:T(8,128)(2,1)S(1)}, bf16[24,3840]{1,0:T(8,128)(2,1)S(1)}, u32[]{:S(2)}, u32[]{:S(2)}) collective-permute-start(bf16[24,3840]{1,0:T(8,128)(2,1)S(1)} %get-tuple-element.341), channel_id=1, source_target_pairs={{0,16},{1,17},{2,18},{3,19},{4,20},{5,21},{6,22},{7,23},{8,24},{9,... | collective-permute-start | bytes 552968 | tf_op jit(solution)/shard_map/ppermute | solution.py:610
  193.2 13.5 %collective-permute-start.42 = (bf16[24,3840]{1,0:T(8,128)(2,1)S(1)}, bf16[24,3840]{1,0:T(8,128)(2,1)S(1)}, u32[]{:S(2)}, u32[]{:S(2)}) collective-permute-start(bf16[24,3840]{1,0:T(8,128)(2,1)S(1)} %get-tuple-element.342), channel_id=1, source_target_pairs={{0,24},{1,25},{2,26},{3,27},{4,28},{5,29},{6,30},{7,31},{8,16},{9,... | collective-permute-start | bytes 552968 | tf_op jit(solution)/shard_map/ppermute | solution.py:610
  195.6 13.5 %copy-start.19 = (f32[24,768]{1,0:T(8,128)S(1)}, f32[24,768]{1,0:T(8,128)}, u32[]{:S(2)}) copy-start(f32[24,768]{1,0:T(8,128)} %param.38) | copy-start | bytes 221188
  195.6 13.5 %copy-start.20 = (f32[24,768]{1,0:T(8,128)S(1)}, f32[24,768]{1,0:T(8,128)}, u32[]{:S(2)}) copy-start(f32[24,768]{1,0:T(8,128)} %param.33) | copy-start | bytes 221188
  206.9 13.0 %copy-start.15 = (f32[24,3072]{1,0:T(8,128)S(1)}, f32[24,3072]{1,0:T(8,128)}, u32[]{:S(2)}) copy-start(f32[24,3072]{1,0:T(8,128)} %param.39) | copy-start | bytes 884740
  206.9 13.0 %copy-start.16 = (f32[24,3072]{1,0:T(8,128)S(1)}, f32[24,3072]{1,0:T(8,128)}, u32[]{:S(2)}) copy-start(f32[24,3072]{1,0:T(8,128)} %param.34) | copy-start | bytes 884740
  206.9 6.3 %collective-permute-start.43 = (bf16[96,1280]{1,0:T(8,128)(2,1)S(1)}, bf16[96,1280]{1,0:T(8,128)(2,1)S(1)}, u32[]{:S(2)}, u32[]{:S(2)}) collective-permute-start(bf16[96,1280]{1,0:T(8,128)(2,1)S(1)} %get-tuple-element.352), channel_id=1, source_target_pairs={{0,2},{1,3},{2,0},{3,1},{4,6},{5,7},{6,4},{7,5},{8,10},{9,11},{10,... | collective-permute-start | bytes 737288 | tf_op jit(solution)/shard_map/ppermute | solution.py:610
  208.5 6.2 %collective-permute-start.44 = (bf16[96,1280]{1,0:T(8,128)(2,1)S(1)}, bf16[96,1280]{1,0:T(8,128)(2,1)S(1)}, u32[]{:S(2)}, u32[]{:S(2)}) collective-permute-start(bf16[96,1280]{1,0:T(8,128)(2,1)S(1)} %get-tuple-element.353), channel_id=1, source_target_pairs={{0,4},{1,5},{2,6},{3,7},{4,0},{5,1},{6,2},{7,3},{8,12},{9,13},{10,... | collective-permute-start | bytes 737288 | tf_op jit(solution)/shard_map/ppermute | solution.py:610
  214.6 12.4 %copy-start.21 = (f32[240]{0:T(256)S(1)}, f32[240]{0:T(256)}, u32[]{:S(2)}) copy-start(f32[240]{0:T(256)} %param.31) | copy-start | bytes 2884
  214.7 12.4 %copy-start.22 = (f32[240]{0:T(256)S(1)}, f32[240]{0:T(256)}, u32[]{:S(2)}) copy-start(f32[240]{0:T(256)} %param.41) | copy-start | bytes 2884
  214.7 12.4 %copy-start.23 = (f32[240]{0:T(256)S(1)}, f32[240]{0:T(256)}, u32[]{:S(2)}) copy-start(f32[240]{0:T(256)} %param.36) | copy-start | bytes 2884
  214.7 13.0 %copy-start.11 = (f32[24,2304]{1,0:T(8,128)S(1)}, f32[24,2304]{1,0:T(8,128)}, u32[]{:S(2)}) copy-start(f32[24,2304]{1,0:T(8,128)} %param.27) | copy-start | bytes 663556
  214.7 13.0 %copy-start.17 = (f32[24,2304]{1,0:T(8,128)S(1)}, f32[24,2304]{1,0:T(8,128)}, u32[]{:S(2)}) copy-start(f32[24,2304]{1,0:T(8,128)} %param.37) | copy-start | bytes 663556
  214.7 13.0 %copy-start.18 = (f32[24,2304]{1,0:T(8,128)S(1)}, f32[24,2304]{1,0:T(8,128)}, u32[]{:S(2)}) copy-start(f32[24,2304]{1,0:T(8,128)} %param.32) | copy-start | bytes 663556
  214.8 6.1 %collective-permute-start.45 = (bf16[24,2560]{1,0:T(8,128)(2,1)S(1)}, bf16[24,2560]{1,0:T(8,128)(2,1)S(1)}, u32[]{:S(2)}, u32[]{:S(2)}) collective-permute-start(bf16[24,2560]{1,0:T(8,128)(2,1)S(1)} %get-tuple-element.363), channel_id=1, source_target_pairs={{0,8},{1,9},{2,10},{3,11},{4,12},{5,13},{6,14},{7,15},{8,0},{9,1},... | collective-permute-start | bytes 368648 | tf_op jit(solution)/shard_map/ppermute | solution.py:610
  217.4 9.4 %collective-permute-start.46 = (bf16[24,2560]{1,0:T(8,128)(2,1)S(1)}, bf16[24,2560]{1,0:T(8,128)(2,1)S(1)}, u32[]{:S(2)}, u32[]{:S(2)}) collective-permute-start(bf16[24,2560]{1,0:T(8,128)(2,1)S(1)} %get-tuple-element.364), channel_id=1, source_target_pairs={{0,16},{1,17},{2,18},{3,19},{4,20},{5,21},{6,22},{7,23},{8,24},{9,... | collective-permute-start | bytes 368648 | tf_op jit(solution)/shard_map/ppermute | solution.py:610
  218.4 8.5 %collective-permute-start.47 = (bf16[24,2560]{1,0:T(8,128)(2,1)S(1)}, bf16[24,2560]{1,0:T(8,128)(2,1)S(1)}, u32[]{:S(2)}, u32[]{:S(2)}) collective-permute-start(bf16[24,2560]{1,0:T(8,128)(2,1)S(1)} %get-tuple-element.365), channel_id=1, source_target_pairs={{0,24},{1,25},{2,26},{3,27},{4,28},{5,29},{6,30},{7,31},{8,16},{9,... | collective-permute-start | bytes 368648 | tf_op jit(solution)/shard_map/ppermute | solution.py:610
  (8 other events, 29.1 us)
